TPU v7x, 32 devices: a whole 2x2x4 slice. The times are simulated.
32 devices in a mesh: dp: 8 (over z, core), seq: 4 (over y, x).
Axes of the slice: x: 2, y: 2, z: 4, core: 2. Of those that a mesh axis runs over, the one named last changes fastest.
Arguments:
- first_layer_input: bfloat16 [8, 2048, 1024], P('dp', 'seq'), may hold values from -6 to 6
- cotangent: bfloat16 [8, 2048, 1024], P('dp', 'seq'), may hold values from -6 to 6
- lengths: int32 [8, 16], P('dp'), may hold values from 1 to 1537, 2048 in all within a row
- w_qkv: bfloat16 [2, 1024, 3072], P(None, 'dp'), may hold values from -0.1875 to 0.1875
- bias_qkv: bfloat16 [2, 3072], replicated, may hold values from -3 to 3
- w_out: bfloat16 [2, 1024, 1024], P(None, 'dp'), may hold values from -0.75 to 0.75
- bias_out: bfloat16 [2, 1024], replicated, may hold values from -3 to 3
- w_in: bfloat16 [2, 1024, 4096], P(None, 'dp'), may hold values from -0.1875 to 0.1875
- bias_in: bfloat16 [2, 4096], replicated, may hold values from -3 to 3
- w_back: bfloat16 [2, 4096, 1024], P(None, 'dp'), may hold values from -0.09375 to 0.09375
- bias_back: bfloat16 [2, 1024], replicated, may hold values from -3 to 3
- norm_gain: bfloat16 [2, 2, 1024], replicated, may hold values from 0.5 to 1.5
- norm_shift: bfloat16 [2, 2, 1024], replicated, may hold values from -2 to 2
- prefix_keys: bfloat16 [2, 64, 1024], replicated, may hold values from -6 to 6
- prefix_values: bfloat16 [2, 64, 1024], replicated, may hold values from -6 to 6
Outputs:
- hidden_out: bfloat16 [8, 2048, 1024], P('dp', 'seq')
- input_grad: bfloat16 [8, 2048, 1024], P('dp', 'seq')
- prefix_key_grad: float32 [2, 64, 1024], replicated
- prefix_value_grad: float32 [2, 64, 1024], replicated
Inputs may be any that keep to these rules, and one draw needn't show every extreme that they name: The lengths of a row sum to 2048; in every row one pair has exactly 1537 tokens.
All inputs are finite; a program needn't handle non-finite values.
Results may differ from a plain program's by a relative error of at most 0.03.
Values may be sent and summed in bfloat16 or wider, within the bound.
No kernel may reach another device: no remote copies, remote signals or barrier semaphores. Data moves between devices by JAX's collectives and lax.ppermute only.
A program may use at most 576 MiB of HBM per device.

v0:
```python
import jax
import jax.numpy as jnp
from jax import lax
from jax.sharding import PartitionSpec as P

HEADS = 16
HEAD = 64


SCALE = 0.125
EPS = 1e-05


def layer_norm(values, gain_row, shift_row):
    center = jnp.mean(values, -1, keepdims=True)
    centered = values - center
    spread = jnp.mean(centered * centered, -1, keepdims=True)
    return centered * lax.rsqrt(spread + EPS) * gain_row + shift_row


def smooth(values):
    return jax.nn.gelu(values, approximate=False)


def back_dot(left, right):
    return lax.dot_general(
        left, right, (((1,), (1,)), ((), ())), preferred_element_type=jnp.float32
    )


def token_segment_codes(pair_lengths, offset_rows, row_count):
    ends_at = jnp.cumsum(pair_lengths, dtype=jnp.int32)
    places = offset_rows + jnp.arange(row_count, dtype=jnp.int32)
    return jnp.sum((places[:, None] >= ends_at[None, :]).astype(jnp.int32), 1, dtype=jnp.int32)


def allowed(query_codes, key_codes):
    return query_codes[:, None] == key_codes[None, :]


def heads_of(values):
    return values.reshape(values.shape[0], HEADS, HEAD)


def attend_forward(queries, keys, values, segment_codes, prefix_heads, prefix_value_heads):
    query_heads = heads_of(queries)
    prefix_scores = (
        jnp.einsum("qhe,khe->hqk", query_heads, prefix_heads, preferred_element_type=jnp.float32)
        * SCALE
    )
    running_top = jnp.max(prefix_scores, -1)
    prefix_weights = jnp.exp(prefix_scores - running_top[..., None])
    running_sum = jnp.sum(prefix_weights, -1)
    running_acc = jnp.einsum(
        "hqk,khe->hqe",
        prefix_weights.astype(jnp.bfloat16),
        prefix_value_heads,
        preferred_element_type=jnp.float32,
    )
    key_piece = lax.all_gather(keys, "seq", axis=0, tiled=True)
    value_piece = lax.all_gather(values, "seq", axis=0, tiled=True)
    code_piece = lax.all_gather(segment_codes, "seq", axis=0, tiled=True)
    scores = (
        jnp.einsum(
            "qhe,khe->hqk", query_heads, heads_of(key_piece), preferred_element_type=jnp.float32
        )
        * SCALE
    )
    scores = jnp.where(allowed(segment_codes, code_piece)[None], scores, -jnp.inf)
    new_top = jnp.maximum(running_top, jnp.max(scores, -1))
    factor = jnp.exp(running_top - new_top)
    weights = jnp.exp(scores - new_top[..., None])
    new_sum = running_sum * factor + jnp.sum(weights, -1)
    new_acc = running_acc * factor[..., None] + jnp.einsum(
        "hqk,khe->hqe",
        weights.astype(jnp.bfloat16),
        heads_of(value_piece),
        preferred_element_type=jnp.float32,
    )
    context = new_acc / new_sum[..., None]
    context = jnp.transpose(context, (1, 0, 2)).reshape(queries.shape[0], HEADS * HEAD)
    log_total = jnp.transpose(new_top + jnp.log(new_sum))
    return (context, log_total)


def attend_backward(
    queries,
    keys,
    values,
    segment_codes,
    prefix_heads,
    prefix_value_heads,
    log_total,
    delta_rows,
    grad_context,
):
    query_heads = heads_of(queries)
    grad_heads = heads_of(grad_context)
    log_heads = jnp.transpose(log_total)[..., None]
    delta_heads = jnp.transpose(delta_rows)[..., None]
    prefix_scores = (
        jnp.einsum("qhe,khe->hqk", query_heads, prefix_heads, preferred_element_type=jnp.float32)
        * SCALE
    )
    prefix_prob = jnp.exp(prefix_scores - log_heads)
    prefix_dprob = jnp.einsum(
        "qhe,khe->hqk", grad_heads, prefix_value_heads, preferred_element_type=jnp.float32
    )
    prefix_dscore = (prefix_prob * (prefix_dprob - delta_heads)).astype(jnp.bfloat16)
    grad_query = (
        jnp.einsum("hqk,khe->qhe", prefix_dscore, prefix_heads, preferred_element_type=jnp.float32)
        * SCALE
    )
    grad_prefix_key = (
        jnp.einsum("hqk,qhe->khe", prefix_dscore, query_heads, preferred_element_type=jnp.float32)
        * SCALE
    )
    grad_prefix_value = jnp.einsum(
        "hqk,qhe->khe",
        prefix_prob.astype(jnp.bfloat16),
        grad_heads,
        preferred_element_type=jnp.float32,
    )
    key_piece = lax.all_gather(keys, "seq", axis=0, tiled=True)
    value_piece = lax.all_gather(values, "seq", axis=0, tiled=True)
    code_piece = lax.all_gather(segment_codes, "seq", axis=0, tiled=True)
    query_key_heads = heads_of(key_piece)
    scores = (
        jnp.einsum("qhe,khe->hqk", query_heads, query_key_heads, preferred_element_type=jnp.float32)
        * SCALE
    )
    scores = jnp.where(allowed(segment_codes, code_piece)[None], scores, -jnp.inf)
    prob = jnp.exp(scores - log_heads)
    dprob = jnp.einsum(
        "qhe,khe->hqk", grad_heads, heads_of(value_piece), preferred_element_type=jnp.float32
    )
    dscore = (prob * (dprob - delta_heads)).astype(jnp.bfloat16)
    grad_query = (
        grad_query
        + jnp.einsum("hqk,khe->qhe", dscore, query_key_heads, preferred_element_type=jnp.float32)
        * SCALE
    )
    key_heads = heads_of(keys)
    value_heads = heads_of(values)
    query_piece = lax.all_gather(queries, "seq", axis=0, tiled=True)
    grad_piece = lax.all_gather(grad_context, "seq", axis=0, tiled=True)
    log_piece = lax.all_gather(log_total.astype(jnp.bfloat16), "seq", axis=0, tiled=True).astype(
        jnp.float32
    )
    delta_piece = lax.all_gather(delta_rows.astype(jnp.bfloat16), "seq", axis=0, tiled=True).astype(
        jnp.float32
    )
    code_piece = lax.all_gather(segment_codes, "seq", axis=0, tiled=True)
    piece_heads = heads_of(query_piece)
    piece_grads = heads_of(grad_piece)
    scores = (
        jnp.einsum("qhe,khe->hqk", piece_heads, key_heads, preferred_element_type=jnp.float32)
        * SCALE
    )
    scores = jnp.where(allowed(code_piece, segment_codes)[None], scores, -jnp.inf)
    prob = jnp.exp(scores - jnp.transpose(log_piece)[..., None])
    dprob = jnp.einsum("qhe,khe->hqk", piece_grads, value_heads, preferred_element_type=jnp.float32)
    dscore = (prob * (dprob - jnp.transpose(delta_piece)[..., None])).astype(jnp.bfloat16)
    grad_key_part = (
        jnp.einsum("hqk,qhe->khe", dscore, piece_heads, preferred_element_type=jnp.float32) * SCALE
    )
    grad_value_part = jnp.einsum(
        "hqk,qhe->khe", prob.astype(jnp.bfloat16), piece_grads, preferred_element_type=jnp.float32
    )
    return (grad_query, grad_key_part, grad_value_part, grad_prefix_key, grad_prefix_value)


def local(
    first_layer_input,
    cotangent,
    lengths,
    w_qkv,
    bias_qkv,
    w_out,
    bias_out,
    w_in,
    bias_in,
    w_back,
    bias_back,
    norm_gain,
    norm_shift,
    prefix_keys,
    prefix_values,
):
    row_count = first_layer_input.shape[1]
    width = first_layer_input.shape[2]
    layer_count = w_qkv.shape[0]
    offset_rows = lax.axis_index("seq") * row_count
    segment_codes = token_segment_codes(lengths[0], offset_rows, row_count)
    current = first_layer_input[0]
    saved = []
    gathered = []
    for layer_index in range(layer_count):
        matrices = (
            lax.all_gather(w_qkv[layer_index], "dp", axis=0, tiled=True),
            lax.all_gather(w_out[layer_index], "dp", axis=0, tiled=True),
            lax.all_gather(w_in[layer_index], "dp", axis=0, tiled=True),
            lax.all_gather(w_back[layer_index], "dp", axis=0, tiled=True),
        )
        gathered.append(matrices)
        mat_qkv, mat_out, mat_in, mat_back = matrices
        prefix_heads = heads_of(prefix_keys[layer_index])
        prefix_value_heads = heads_of(prefix_values[layer_index])
        gains = norm_gain[layer_index].astype(jnp.float32)
        shifts = norm_shift[layer_index].astype(jnp.float32)
        projected = jnp.dot(current, mat_qkv, preferred_element_type=jnp.float32) + bias_qkv[
            layer_index
        ].astype(jnp.float32)
        queries = projected[:, :width].astype(jnp.bfloat16)
        keys = projected[:, width : 2 * width].astype(jnp.bfloat16)
        values = projected[:, 2 * width :].astype(jnp.bfloat16)
        context, log_total = attend_forward(
            queries, keys, values, segment_codes, prefix_heads, prefix_value_heads
        )
        residual_one = (
            current.astype(jnp.float32)
            + jnp.dot(context.astype(jnp.bfloat16), mat_out, preferred_element_type=jnp.float32)
            + bias_out[layer_index].astype(jnp.float32)
        )
        normed = layer_norm(residual_one, gains[0], shifts[0])
        inner = jnp.dot(
            normed.astype(jnp.bfloat16), mat_in, preferred_element_type=jnp.float32
        ) + bias_in[layer_index].astype(jnp.float32)
        activated = smooth(inner).astype(jnp.bfloat16)
        residual_two = (
            normed
            + jnp.dot(activated, mat_back, preferred_element_type=jnp.float32)
            + bias_back[layer_index].astype(jnp.float32)
        )
        result = layer_norm(residual_two, gains[1], shifts[1])
        saved.append((queries, keys, values, context, log_total, residual_one, inner, residual_two))
        current = result.astype(jnp.bfloat16)
    gradient = cotangent[0].astype(jnp.float32)
    key_grads = []
    value_grads = []
    for layer_index in reversed(range(layer_count)):
        queries, keys, values, context, log_total, residual_one, inner, residual_two = saved[
            layer_index
        ]
        mat_qkv, mat_out, mat_in, mat_back = (
            lax.all_gather(w_qkv[layer_index], "dp", axis=0, tiled=True),
            lax.all_gather(w_out[layer_index], "dp", axis=0, tiled=True),
            lax.all_gather(w_in[layer_index], "dp", axis=0, tiled=True),
            lax.all_gather(w_back[layer_index], "dp", axis=0, tiled=True),
        )
        prefix_heads = heads_of(prefix_keys[layer_index])
        prefix_value_heads = heads_of(prefix_values[layer_index])
        gains = norm_gain[layer_index].astype(jnp.float32)
        shifts = norm_shift[layer_index].astype(jnp.float32)
        unused_two, pull_two = jax.vjp(
            lambda rows: layer_norm(rows, gains[1], shifts[1]), residual_two
        )
        (grad_two,) = pull_two(gradient)
        grad_hidden = back_dot(grad_two.astype(jnp.bfloat16), mat_back)
        unused_inner, pull_smooth = jax.vjp(smooth, inner)
        (grad_inner,) = pull_smooth(grad_hidden)
        grad_normed = grad_two + back_dot(grad_inner.astype(jnp.bfloat16), mat_in)
        unused_one, pull_one = jax.vjp(
            lambda rows: layer_norm(rows, gains[0], shifts[0]), residual_one
        )
        (grad_one,) = pull_one(grad_normed)
        grad_context = back_dot(grad_one.astype(jnp.bfloat16), mat_out).astype(jnp.bfloat16)
        delta_rows = jnp.sum(heads_of(grad_context.astype(jnp.float32) * context), -1)
        grad_query, grad_key, grad_value, grad_prefix_key, grad_prefix_value = attend_backward(
            queries,
            keys,
            values,
            segment_codes,
            prefix_heads,
            prefix_value_heads,
            log_total,
            delta_rows,
            grad_context,
        )
        grad_prefix_key = grad_prefix_key.reshape(grad_prefix_key.shape[0], width)
        grad_prefix_value = grad_prefix_value.reshape(grad_prefix_value.shape[0], width)
        grad_prefix_key, grad_prefix_value = lax.psum(
            (grad_prefix_key, grad_prefix_value), ("dp", "seq")
        )
        key_grads.append(grad_prefix_key)
        value_grads.append(grad_prefix_value)
        grad_projected = jnp.concatenate(
            [
                grad_query.reshape(row_count, width),
                grad_key.reshape(row_count, width),
                grad_value.reshape(row_count, width),
            ],
            1,
        ).astype(jnp.bfloat16)
        gradient = grad_one + back_dot(grad_projected, mat_qkv)
    key_stack = jnp.stack(key_grads[::-1])
    value_stack = jnp.stack(value_grads[::-1])
    return (current[None], gradient.astype(jnp.bfloat16)[None], key_stack, value_stack)


def solution(mesh):
    in_specs = (
        P("dp", "seq", None),
        P("dp", "seq", None),
        P("dp", None),
        P(None, "dp", None),
        P(),
        P(None, "dp", None),
        P(),
        P(None, "dp", None),
        P(),
        P(None, "dp", None),
        P(),
        P(),
        P(),
        P(),
        P(),
    )
    out_specs = (P("dp", "seq", None), P("dp", "seq", None), P(), P())
    return jax.shard_map(local, mesh=mesh, in_specs=in_specs, out_specs=out_specs, check_vma=False)
```

profile of v0, /device:TPU:0, one launch (start us, length us, event | category | flops | bytes accessed | tf_op | source)
XLA Modules:
  0.0 1324.2 jit_solution(15953443894674160546)
XLA Ops:
  11.3 66.4 %all-gather.42.cloned.1.call-done = bf16[1,1024,3072]{2,1,0:T(8,128)(2,1)} async-done(((bf16[1,128,3072]{2,1,0:T(8,128)(2,1)}), bf16[1,1024,3072]{2,1,0:T(8,128)(2,1)}) %all-gather.42.cloned.1.call-update) | async-done | bytes 6291472 | tf_op jit(solution)/shard_map/all_gather | solution.py:200
  114.4 23.1 %all-gather.26.cloned.1.call-done = bf16[2048,1024]{1,0:T(8,128)(2,1)} async-done(((bf16[512,1024]{1,0:T(8,128)(2,1)}), bf16[2048,1024]{1,0:T(8,128)(2,1)}) %all-gather.26.cloned.1.call-update) | async-done | bytes 4194320 | tf_op jit(solution)/shard_map/all_gather | solution.py:60
  144.0 26.9 %fusion.6 = (f32[16,512]{1,0:T(8,128)S(1)}, f32[16,512,2048]{2,1,0:T(8,128)}) fusion(pred[512,2048]{1,0:T(8,128)(4,1)S(1)} %broadcast_compare_fusion.1, bf16[512,16,64]{0,2,1:T(8,128)(2,1)} %bitcast.348, bf16[2048,16,64]{0,2,1:T(8,128)(2,1)} %bitcast.339), kind=kOutput, calls=%fused_computation.16 | convolution fusion | flops 2197807104 | bytes 73433088 | tf_op jit(solution)/shard_map/qhe,khe->hqk/dot_general | solution.py:64
  171.5 21.5 %fusion = f32[16,512]{1,0:T(8,128)S(1)} fusion(f32[16,512,2048]{2,1,0:T(8,128)} %get-tuple-element.67, f32[16,512]{1,0:T(8,128)S(1)} %max.43, pred[512,2048]{1,0:T(8,128)(4,1)S(1)} %broadcast_compare_fusion.1), kind=kLoop, calls=%fused_computation.10 | loop fusion | flops 67100672 | bytes 68222976 | tf_op jit(solution)/shard_map/reduce_sum | solution.py:73
  199.6 27.6 %fusion.14 = f32[16,512,64]{1,2,0:T(8,128)} fusion(bf16[2048,16,64]{0,2,1:T(8,128)(2,1)} %bitcast.361, f32[16,512,2048]{2,1,0:T(8,128)} %get-tuple-element.67, f32[16,512]{1,0:T(8,128)S(1)} %max.43, pred[512,2048]{1,0:T(8,128)(4,1)S(1)} %broadcast_compare_fusion.1), kind=kOutput, calls=%fused_computation.21 | convolution fusion | flops 2214592512 | bytes 74481664 | tf_op jit(solution)/shard_map/hqk,khe->hqe/dot_general | solution.py:74
  237.9 68.4 %all-gather.46.cloned.1.call-done = bf16[1,1024,4096]{2,1,0:T(8,128)(2,1)} async-done(((bf16[1,128,4096]{2,1,0:T(8,128)(2,1)}), bf16[1,1024,4096]{2,1,0:T(8,128)(2,1)}) %all-gather.46.cloned.1.call-update) | async-done | bytes 8388624 | tf_op jit(solution)/shard_map/all_gather | solution.py:202
  306.3 27.0 %fusion.36 = (f32[512,4096]{1,0:T(8,128)}, f32[512,4096]{1,0:T(8,128)}) fusion(f32[4096]{0:T(1024)S(1)} %bitcast.399, bf16[1,1024,4096]{2,1,0:T(8,128)(2,1)} %all-gather.46.cloned.1.call-done, f32[512,1024]{1,0:T(8,128)S(1)} %get-tuple-element.69, f32[1024]{0:T(1024)S(1)} %bitcast.425, f32[1024]{0:T(1024)S(1)} %bitcast.412, f32[512]{0:T(512)S(1)} %fusion.196, ...), kind=kOutput, calls=%fused_computation.40 | convolution fusion | flops 4429709312 | bytes 27291648 | tf_op jit(solution)/shard_map/dot_general | solution.py:226
  333.3 55.7 %all-gather.48.cloned.1.call-done = bf16[1,4096,1024]{2,1,0:T(8,128)(2,1)} async-done(((bf16[1,512,1024]{2,1,0:T(8,128)(2,1)}), bf16[1,4096,1024]{2,1,0:T(8,128)(2,1)}) %all-gather.48.cloned.1.call-update) | async-done | bytes 8388624 | tf_op jit(solution)/shard_map/all_gather | solution.py:203
  389.0 11.2 fusion.246
  402.5 51.4 %all-gather.50.cloned.1.call-done = bf16[1,1024,3072]{2,1,0:T(8,128)(2,1)} async-done(((bf16[1,128,3072]{2,1,0:T(8,128)(2,1)}), bf16[1,1024,3072]{2,1,0:T(8,128)(2,1)}) %all-gather.50.cloned.1.call-update) | async-done | bytes 6291472 | tf_op jit(solution)/shard_map/all_gather | solution.py:200
  470.1 43.9 %all-gather.30.cloned.1.call-done = bf16[2048,1024]{1,0:T(8,128)(2,1)} async-done(((bf16[512,1024]{1,0:T(8,128)(2,1)}), bf16[2048,1024]{1,0:T(8,128)(2,1)}) %all-gather.30.cloned.1.call-update) | async-done | bytes 4194320 | tf_op jit(solution)/shard_map/all_gather | solution.py:60
  520.6 26.9 %fusion.7 = (f32[16,512]{1,0:T(8,128)S(1)}, f32[16,512,2048]{2,1,0:T(8,128)}) fusion(pred[512,2048]{1,0:T(8,128)(4,1)S(1)} %broadcast_compare_fusion.1, bf16[512,16,64]{0,2,1:T(8,128)(2,1)} %bitcast.351, bf16[2048,16,64]{0,2,1:T(8,128)(2,1)} %bitcast.341), kind=kOutput, calls=%fused_computation.17 | convolution fusion | flops 2197807104 | bytes 73433088 | tf_op jit(solution)/shard_map/qhe,khe->hqk/dot_general | solution.py:64
  547.5 21.7 %fusion.2 = f32[16,512]{1,0:T(8,128)S(1)} fusion(f32[16,512,2048]{2,1,0:T(8,128)} %get-tuple-element.77, f32[16,512]{1,0:T(8,128)S(1)} %max.45, pred[512,2048]{1,0:T(8,128)(4,1)S(1)} %broadcast_compare_fusion.1), kind=kLoop, calls=%fused_computation.12 | loop fusion | flops 67100672 | bytes 68222976 | tf_op jit(solution)/shard_map/reduce_sum | solution.py:73
  575.8 27.6 %fusion.12 = f32[16,512,64]{1,2,0:T(8,128)} fusion(bf16[2048,16,64]{0,2,1:T(8,128)(2,1)} %bitcast.363, f32[16,512,2048]{2,1,0:T(8,128)} %get-tuple-element.77, f32[16,512]{1,0:T(8,128)S(1)} %max.45, pred[512,2048]{1,0:T(8,128)(4,1)S(1)} %broadcast_compare_fusion.1), kind=kOutput, calls=%fused_computation.20 | convolution fusion | flops 2214592512 | bytes 74481664 | tf_op jit(solution)/shard_map/hqk,khe->hqe/dot_general | solution.py:74
  615.4 67.7 %all-gather.54.cloned.1.call-done = bf16[1,1024,4096]{2,1,0:T(8,128)(2,1)} async-done(((bf16[1,128,4096]{2,1,0:T(8,128)(2,1)}), bf16[1,1024,4096]{2,1,0:T(8,128)(2,1)}) %all-gather.54.cloned.1.call-update) | async-done | bytes 8388624 | tf_op jit(solution)/shard_map/all_gather | solution.py:202
  683.0 28.2 %fusion.37 = (f32[512,4096]{1,0:T(8,128)}, f32[512,4096]{1,0:T(8,128)}) fusion(f32[4096]{0:T(1024)S(1)} %bitcast.402, bf16[1,1024,4096]{2,1,0:T(8,128)(2,1)} %all-gather.54.cloned.1.call-done, f32[512,1024]{1,0:T(8,128)} %copy-done.24, f32[1024]{0:T(1024)S(1)} %bitcast.421, f32[1024]{0:T(1024)S(1)} %bitcast.418, f32[512]{0:T(512)S(1)} %fusion.198, ...), kind=kOutput, calls=%fused_computation.41 | convolution fusion | flops 4429709312 | bytes 27291648 | tf_op jit(solution)/shard_map/dot_general | solution.py:226
  711.3 54.4 %all-gather.56.cloned.1.call-done = bf16[1,4096,1024]{2,1,0:T(8,128)(2,1)} async-done(((bf16[1,512,1024]{2,1,0:T(8,128)(2,1)}), bf16[1,4096,1024]{2,1,0:T(8,128)(2,1)}) %all-gather.56.cloned.1.call-update) | async-done | bytes 8388624 | tf_op jit(solution)/shard_map/all_gather | solution.py:203
  765.7 15.4 %fusion.249 = (f32[512]{0:T(512)S(1)}, f32[512,1024]{1,0:T(8,128)}) fusion(f32[1024]{0:T(1024)S(1)} %bitcast.408, bf16[1,4096,1024]{2,1,0:T(8,128)(2,1)} %all-gather.56.cloned.1.call-done, f32[512,4096]{1,0:T(8,128)} %get-tuple-element.80, f32[512,4096]{1,0:T(8,128)} %get-tuple-element.81, f32[4096]{0:T(1024)S(1)} %bitcast.403, f32[1024]{0:T(1024)S(1)} %bitcast.422, ...), kind=kOutput, calls=%fused_computation.317 | convolution fusion | flops 4307025408 | bytes 29394944 | tf_op jit(solution)/shard_map/dot_general | solution.py:232
  789.7 30.5 %multiply_reduce_fusion.2 = (f32[512]{0:T(512)S(1)}, f32[512,1024]{1,0:T(8,128)}) fusion(f32[512,1024]{1,0:T(8,128)} %copy-done.24, f32[512]{0:T(512)S(1)} %broadcast_multiply_fusion.1, f32[1024]{0:T(1024)S(1)} %bitcast.420, bf16[1,1024,4096]{2,1,0:T(8,128)(2,1)} %all-gather.54.cloned.1.call-done, f32[512,4096]{1,0:T(8,128)} %get-tuple-element.80, ...), kind=kOutput, calls=%fused_computation.156 | convolution fusion | flops 8632926208 | bytes 40931328 | tf_op jit(solution)/shard_map/dot_general | solution.py:26
  848.5 36.3 %fusion.16 = f32[16,64,512]{2,1,0:T(8,128)} fusion(bf16[2048,16,64]{0,2,1:T(8,128)(2,1)} %bitcast.342, f32[16,512,2048]{2,1,0:T(8,128)} %get-tuple-element.77, f32[16,512]{1,0:T(8,128)S(1)} %bitcast.392, f32[16,512]{1,0:T(8,128)S(1)} %log_add_fusion.1, pred[512,2048]{1,0:T(8,128)(4,1)S(1)} %broadcast_compare_fusion.1, bf16[512,16,64]{0,2,1:T(8,128)(2,1)} %bitcast.357, ...), kind=kOutput, calls=%fused_computation.22 | convolution fusion | flops 4395630592 | bytes 79757312 | tf_op jit(solution)/shard_map/hqk,khe->qhe/dot_general | solution.py:140
  891.3 8.2 all_gather.96
  899.5 8.2 all_gather.94
  916.4 25.4 %fusion.254 = f32[16,2048,512]{2,1,0:T(8,128)} fusion(bf16[2048,16,64]{0,2,1:T(8,128)(2,1)} %bitcast.345, bf16[512,16,64]{0,2,1:T(8,128)(2,1)S(1)} %bitcast.359), kind=kOutput, calls=%fused_computation.318 | convolution fusion | flops 2147483648 | bytes 72351744 | tf_op jit(solution)/shard_map/qhe,khe->hqk/dot_general | solution.py:157
  948.4 26.7 %fusion.153 = bf16[16,64,512]{2,1,0:T(8,128)(2,1)} fusion(bf16[2048,16,64]{0,2,1:T(8,128)(2,1)} %bitcast.367, f32[16,2048,512]{2,1,0:T(8,128)} %fusion.254, f32[16,2048]{1,0:T(8,128)S(1)} %convert_bitcast_fusion.3, pred[2048,512]{1,0:T(8,128)(4,1)S(1)} %copy-done.40), kind=kOutput, calls=%fused_computation.189 | convolution fusion | flops 2215116800 | bytes 73531392 | tf_op jit(solution)/shard_map/hqk,qhe->khe/dot_general | solution.py:167
  975.1 34.0 %multiply_convert_fusion.14 = bf16[16,64,512]{2,1,0:T(8,128)(2,1)} fusion(bf16[2048,16,64]{0,2,1:T(8,128)(2,1)} %bitcast.346, f32[16,2048,512]{2,1,0:T(8,128)} %fusion.254, f32[16,2048]{1,0:T(8,128)S(1)} %convert_bitcast_fusion.2, f32[16,2048]{1,0:T(8,128)S(1)} %convert_bitcast_fusion.3, pred[2048,512]{1,0:T(8,128)(4,1)} %broadcast_compare_fusion, ...), kind=kOutput, calls=%fused_computation.151 | convolution fusion | flops 4396679168 | bytes 78905344 | tf_op jit(solution)/shard_map/hqk,qhe->khe/dot_general | solution.py:165
  1019.2 20.2 %multiply_reduce_fusion = (f32[512]{0:T(512)S(1)}, f32[512,1024]{1,0:T(8,128)}) fusion(f32[512,1024]{1,0:T(8,128)S(1)} %copy-done.21, f32[512]{0:T(512)S(1)} %copy-done.68, f32[1024]{0:T(1024)S(1)} %bitcast.414, bf16[1,1024,4096]{2,1,0:T(8,128)(2,1)} %all-gather.46.cloned.1.call-done, f32[512,4096]{1,0:T(8,128)} %get-tuple-element.70, ...), kind=kOutput, calls=%fused_computation.147 | convolution fusion | flops 8625586176 | bytes 39872512 | tf_op jit(solution)/shard_map/dot_general | solution.py:26
  1069.4 25.9 %fusion.255 = f32[16,2048,512]{2,1,0:T(8,128)} fusion(bf16[2048,16,64]{0,2,1:T(8,128)(2,1)} %bitcast.343, bf16[512,16,64]{0,2,1:T(8,128)(2,1)S(1)} %bitcast.360), kind=kOutput, calls=%fused_computation.319 | convolution fusion | flops 2147483648 | bytes 72351744 | tf_op jit(solution)/shard_map/qhe,khe->hqk/dot_general | solution.py:157
  1111.6 36.3 %fusion.18 = f32[16,64,512]{2,1,0:T(8,128)} fusion(bf16[2048,16,64]{0,2,1:T(8,128)(2,1)} %bitcast.340, f32[16,512,2048]{2,1,0:T(8,128)} %get-tuple-element.67, f32[16,512]{1,0:T(8,128)S(1)} %bitcast.390, f32[16,512]{1,0:T(8,128)S(1)} %copy-done.51, pred[512,2048]{1,0:T(8,128)(4,1)S(1)} %copy-done.1, bf16[512,16,64]{0,2,1:T(8,128)(2,1)S(1)} %bitcast.355, ...), kind=kOutput, calls=%fused_computation.24 | convolution fusion | flops 4395630592 | bytes 79757312 | tf_op jit(solution)/shard_map/hqk,khe->qhe/dot_general | solution.py:140
  1150.0 38.3 %all-reduce.3.cloned.1.call-done = (f32[1,64,1024]{2,1,0:T(8,128)}, f32[1,64,1024]{2,1,0:T(8,128)}, f32[1,64,1024]{2,1,0:T(8,128)}, f32[1,64,1024]{2,1,0:T(8,128)}) async-done(((f32[1,64,1024]{2,1,0:T(8,128)}, f32[1,64,1024]{2,1,0:T(8,128)}, f32[1,64,1024]{2,1,0:T(8,128)}, f32[1,64,1024]{2,1,0:T(8,128)}), (f32[1,64,1024]{2,1,0:T(8,128)}, f32[1,64,1024]{2,1,0:T(8,128)}, f32[1,64,1024]{2,1,0:T(8,128)}, ...) | async-done | bytes 1048592 | tf_op jit(solution)/shard_map/psum | solution.py:282
  1192.0 50.5 %all-gather.40.cloned.1.call-done = bf16[2048,1024]{1,0:T(8,128)(2,1)} async-done(((bf16[512,1024]{1,0:T(8,128)(2,1)}), bf16[2048,1024]{1,0:T(8,128)(2,1)}) %all-gather.40.cloned.1.call-update) | async-done | bytes 4194320 | tf_op jit(solution)/shard_map/all_gather | solution.py:146
  1249.0 26.7 %fusion.156 = bf16[16,64,512]{2,1,0:T(8,128)(2,1)} fusion(bf16[2048,16,64]{0,2,1:T(8,128)(2,1)} %bitcast.365, f32[16,2048,512]{2,1,0:T(8,128)} %fusion.255, f32[16,2048]{1,0:T(8,128)S(1)} %copy-done.58, pred[2048,512]{1,0:T(8,128)(4,1)S(1)} %copy-done.41), kind=kOutput, calls=%fused_computation.190 | convolution fusion | flops 2215116800 | bytes 73531392 | tf_op jit(solution)/shard_map/hqk,qhe->khe/dot_general | solution.py:167
  1275.8 33.7 %multiply_convert_fusion.12 = bf16[16,64,512]{2,1,0:T(8,128)(2,1)} fusion(bf16[2048,16,64]{0,2,1:T(8,128)(2,1)} %bitcast.344, f32[16,2048,512]{2,1,0:T(8,128)} %fusion.255, f32[16,2048]{1,0:T(8,128)S(1)} %convert_bitcast_fusion, f32[16,2048]{1,0:T(8,128)S(1)} %copy-done.58, pred[2048,512]{1,0:T(8,128)(4,1)} %broadcast_compare_fusion, ...), kind=kOutput, calls=%fused_computation.143 | convolution fusion | flops 4396679168 | bytes 78905344 | tf_op jit(solution)/shard_map/hqk,qhe->khe/dot_general | solution.py:165
  (362 shorter events, 243.0 us)
Async XLA Ops:
  7.2 70.5 %all-gather.42.cloned.1.call-start = ((), (), s32[]{:S(2)}) async-start(), calls=%async_computation.8 | async-start | bytes 7077888 | tf_op jit(solution)/shard_map/all_gather | solution.py:200
  9.9 127.6 %all-gather.26.cloned.1.call-start = ((), (), s32[]{:S(2)}) async-start(), calls=%async_computation | async-start | bytes 5242880 | tf_op jit(solution)/shard_map/all_gather | solution.py:60
  85.9 107.1 %all-gather.28.cloned.1.call-start = ((), (), s32[]{:S(2)}) async-start(), calls=%async_computation.1 | async-start | bytes 5242880 | tf_op jit(solution)/shard_map/all_gather | solution.py:61
  86.7 145.3 %all-gather.44.cloned.1.call-start = ((), (), s32[]{:S(2)}) async-start(), calls=%async_computation.9 | async-start | bytes 2359296 | tf_op jit(solution)/shard_map/all_gather | solution.py:201
  87.6 218.7 %all-gather.46.cloned.1.call-start = ((), (), s32[]{:S(2)}) async-start(), calls=%async_computation.10 | async-start | bytes 9437184 | tf_op jit(solution)/shard_map/all_gather | solution.py:202
  90.8 298.2 %all-gather.48.cloned.1.call-start = ((), (), s32[]{:S(2)}) async-start(), calls=%async_computation.11 | async-start | bytes 9437184 | tf_op jit(solution)/shard_map/all_gather | solution.py:203
  94.3 359.5 %all-gather.50.cloned.1.call-start = ((), (), s32[]{:S(2)}) async-start(), calls=%async_computation.12 | async-start | bytes 7077888 | tf_op jit(solution)/shard_map/all_gather | solution.py:200
  95.1 419.0 %all-gather.30.cloned.1.call-start = ((), (), s32[]{:S(2)}) async-start(), calls=%async_computation.2 | async-start | bytes 5242880 | tf_op jit(solution)/shard_map/all_gather | solution.py:60
  104.8 743.7 %copy-start = (pred[512,2048]{1,0:T(8,128)(4,1)}, pred[512,2048]{1,0:T(8,128)(4,1)S(1)}, u32[]{:S(2)}) copy-start(pred[512,2048]{1,0:T(8,128)(4,1)S(1)} %broadcast_compare_fusion.1) | copy-start | bytes 3145732
  108.5 280.4 %copy-start.77 = (f32[1,4096]{1,0:T(1,128)}, f32[1,4096]{1,0:T(1,128)S(1)}, u32[]{:S(2)}) copy-start(f32[1,4096]{1,0:T(1,128)S(1)} %get-tuple-element.43) | copy-start | bytes 49156
  114.0 114.6 %copy-start.2 = (f32[16,512,64]{1,2,0:T(8,128)}, f32[16,512,64]{1,2,0:T(8,128)S(1)}, u32[]{:S(2)}) copy-start(f32[16,512,64]{1,2,0:T(8,128)S(1)} %get-tuple-element.65) | copy-start | bytes 6291460
  114.0 114.6 %copy-start.42 = (f32[16,512]{1,0:T(8,128)}, f32[16,512]{1,0:T(8,128)S(1)}, u32[]{:S(2)}) copy-start(f32[16,512]{1,0:T(8,128)S(1)} %get-tuple-element.64) | copy-start | bytes 98308
  114.4 112.8 %copy-start.52 = (f32[16,512]{1,0:T(8,128)}, f32[16,512]{1,0:T(8,128)S(1)}, u32[]{:S(2)}) copy-start(f32[16,512]{1,0:T(8,128)S(1)} %fusion.115) | copy-start | bytes 98308
  236.7 152.3 %copy-start.20 = (f32[512,1024]{1,0:T(8,128)}, f32[512,1024]{1,0:T(8,128)S(1)}, u32[]{:S(2)}) copy-start(f32[512,1024]{1,0:T(8,128)S(1)} %get-tuple-element.69) | copy-start | bytes 6291460
  236.7 152.2 %copy-start.67 = (f32[512]{0:T(512)}, f32[512]{0:T(512)S(1)}, u32[]{:S(2)}) copy-start(f32[512]{0:T(512)S(1)} %broadcast_multiply_fusion.3) | copy-start | bytes 6148
  237.9 151.0 %copy-start.82 = (f32[512]{0:T(512)}, f32[512]{0:T(512)S(1)}, u32[]{:S(2)}) copy-start(f32[512]{0:T(512)S(1)} %fusion.196) | copy-start | bytes 6148
  306.3 82.7 %copy-start.90 = (f32[1,1024]{1,0:T(1,128)S(1)}, f32[1,1024]{1,0:T(1,128)}, u32[]{:S(2)}) copy-start(f32[1,1024]{1,0:T(1,128)} %get-tuple-element.59) | copy-start | bytes 12292
  400.3 208.0 %copy-start.69 = (f32[512]{0:T(512)}, f32[512]{0:T(512)S(1)}, u32[]{:S(2)}) copy-start(f32[512]{0:T(512)S(1)} %broadcast_multiply_fusion.2) | copy-start | bytes 6148
  402.5 205.8 %copy-start.84 = (f32[512]{0:T(512)}, f32[512]{0:T(512)S(1)}, u32[]{:S(2)}) copy-start(f32[512]{0:T(512)S(1)} %fusion.197) | copy-start | bytes 6148
  462.6 106.7 %all-gather.32.cloned.1.call-start = ((), (), s32[]{:S(2)}) async-start(), calls=%async_computation.3 | async-start | bytes 5242880 | tf_op jit(solution)/shard_map/all_gather | solution.py:61
  463.3 145.0 %all-gather.52.cloned.1.call-start = ((), (), s32[]{:S(2)}) async-start(), calls=%async_computation.13 | async-start | bytes 2359296 | tf_op jit(solution)/shard_map/all_gather | solution.py:201
  463.9 219.1 %all-gather.54.cloned.1.call-start = ((), (), s32[]{:S(2)}) async-start(), calls=%async_computation.14 | async-start | bytes 9437184 | tf_op jit(solution)/shard_map/all_gather | solution.py:202
  464.6 301.0 %all-gather.56.cloned.1.call-start = ((), (), s32[]{:S(2)}) async-start(), calls=%async_computation.15 | async-start | bytes 9437184 | tf_op jit(solution)/shard_map/all_gather | solution.py:203
  465.2 444.3 %all-gather.34.cloned.1.call-start = ((), (), s32[]{:S(2)}) async-start(), calls=%async_computation.4 | async-start | bytes 5242880 | tf_op jit(solution)/shard_map/all_gather | solution.py:145
  467.7 474.1 %all-gather.36.cloned.1.call-start = ((), (), s32[]{:S(2)}) async-start(), calls=%async_computation.5 | async-start | bytes 5242880 | tf_op jit(solution)/shard_map/all_gather | solution.py:146
  470.1 133.3 %copy-start.53 = (f32[16,512]{1,0:T(8,128)}, f32[16,512]{1,0:T(8,128)S(1)}, u32[]{:S(2)}) copy-start(f32[16,512]{1,0:T(8,128)S(1)} %fusion.117) | copy-start | bytes 98308
  608.3 74.7 %copy-start.79 = (f32[1,4096]{1,0:T(1,128)S(1)}, f32[1,4096]{1,0:T(1,128)}, u32[]{:S(2)}) copy-start(f32[1,4096]{1,0:T(1,128)} %get-tuple-element.42) | copy-start | bytes 49156
  608.3 74.7 %copy-start.97 = (f32[1,1,1024]{2,1,0:T(1,128)S(1)}, f32[1,1,1024]{2,1,0:T(1,128)}, u32[]{:S(2)}) copy-start(f32[1,1,1024]{2,1,0:T(1,128)} %get-tuple-element.47) | copy-start | bytes 12292
  683.0 82.6 %copy-start.88 = (f32[1,1024]{1,0:T(1,128)S(1)}, f32[1,1024]{1,0:T(1,128)}, u32[]{:S(2)}) copy-start(f32[1,1024]{1,0:T(1,128)} %get-tuple-element.58) | copy-start | bytes 12292
  826.7 235.9 %all-gather.38.cloned.1.call-start = ((), (), s32[]{:S(2)}) async-start(), calls=%async_computation.6 | async-start | bytes 5242880 | tf_op jit(solution)/shard_map/all_gather | solution.py:145
  828.4 359.8 %all-reduce.3.cloned.1.call-start = ((), (), s32[]{:S(2)}) async-start(), calls=%async_computation.16 | async-start | bytes 2097152 | tf_op jit(solution)/shard_map/psum | solution.py:282
  1060.0 182.5 %all-gather.40.cloned.1.call-start = ((), (), s32[]{:S(2)}) async-start(), calls=%async_computation.7 | async-start | bytes 5242880 | tf_op jit(solution)/shard_map/all_gather | solution.py:146
  (88 other events, 1486.2 us)
Sparse Core Ops, SparseCore 0:
  10.2 67.4 all-gather.41
  86.0 51.4 all-gather.25
  139.4 52.6 all-gather.27
  194.1 29.0 all-gather.43
  224.7 81.5 all-gather.45
  308.3 80.5 all-gather.47
  390.6 63.2 all-gather.49
  462.7 51.3 all-gather.29
  515.9 52.6 all-gather.31
  570.7 29.0 all-gather.51
  601.4 81.5 all-gather.53
  685.1 80.5 all-gather.55
  767.5 51.2 all-gather.33
  826.9 50.7 all-gather.35
  879.4 53.5 all-gather.37
  1060.1 128.1 all-reduce.2
  1190.7 51.7 all-gather.39
where the time goes:
time: 1330 us; the launch traced here: 1320 us
  matrix products  558 us (42%)
  waiting for transfers between devices  524 us (39%)
  local copies, waits for them, and re-layouts  109 us (8%)
  other arithmetic  77 us (6%)
  blocking collectives  40.1 us (3%)
  between operations  15.4 us (1%)
    all_gather x2, waiting for transfers between devices, local(): lax.all_gather(w_in[layer_index], 'dp', axis=0, tiled=True)  136 us
    all_gather x2, waiting for transfers between devices, local(): lax.all_gather(w_qkv[layer_index], 'dp', axis=0, tiled=True)  118 us
    all_gather x2, waiting for transfers between devices, local(): lax.all_gather(w_back[layer_index], 'dp', axis=0, tiled=True)  110 us
    dot_general x6, matrix products, back_dot(): lax.dot_general(left, right, (((1,), (1,)), ((), ())), preferred_element_...  72.7 us
    dot_general x2, matrix products, attend_backward(): jnp.einsum('hqk,khe->qhe', dscore, query_key_heads, preferred_element_typ...  72.6 us
    dot_general x2, matrix products, attend_backward(): jnp.einsum('hqk,qhe->khe', dscore, piece_heads, preferred_element_type=jn...  67.7 us
    all_gather x2, waiting for transfers between devices, attend_forward(): key_piece = lax.all_gather(keys, 'seq', axis=0, tiled=True)  67.1 us
    dot_general x2, matrix products, local(): jnp.dot(normed.astype(jnp.bfloat16), mat_in, preferred_element_type=jnp.f...  55.2 us
  transfers between devices with their start and end apart: 17, of which 10 were waited for; matrix products, arithmetic and copies ran while one was open for 49% of the time, Pallas kernels for 0%

commit v1 on v0

--- a/solution.py
+++ b/solution.py
@@ -29,7 +29,10 @@
 
 
 def token_segment_codes(pair_lengths, offset_rows, row_count):
-    ends_at = jnp.cumsum(pair_lengths, dtype=jnp.int32)
+    pair_at = jnp.arange(pair_lengths.shape[0], dtype=jnp.int32)
+    ends_at = jnp.sum(
+        jnp.where(pair_at[:, None] <= pair_at[None, :], pair_lengths[:, None], 0), 0, dtype=jnp.int32
+    )
     places = offset_rows + jnp.arange(row_count, dtype=jnp.int32)
     return jnp.sum((places[:, None] >= ends_at[None, :]).astype(jnp.int32), 1, dtype=jnp.int32)
 

time: 1330 us -> 1330 us (level)
  no operation moved by 1% of the time
where the time goes in v1:
time: 1330 us; the launch traced here: 1320 us
  matrix products  559 us (42%)
  waiting for transfers between devices  524 us (39%)
  local copies, waits for them, and re-layouts  109 us (8%)
  other arithmetic  76.9 us (6%)
  blocking collectives  40.1 us (3%)
  between operations  15.4 us (1%)
    all_gather x2, waiting for transfers between devices, local(): lax.all_gather(w_in[layer_index], 'dp', axis=0, tiled=True)  136 us
    all_gather x2, waiting for transfers between devices, local(): lax.all_gather(w_qkv[layer_index], 'dp', axis=0, tiled=True)  118 us
    all_gather x2, waiting for transfers between devices, local(): lax.all_gather(w_back[layer_index], 'dp', axis=0, tiled=True)  110 us
    dot_general x6, matrix products, back_dot(): lax.dot_general(left, right, (((1,), (1,)), ((), ())), preferred_element_...  73 us
    dot_general x2, matrix products, attend_backward(): jnp.einsum('hqk,khe->qhe', dscore, query_key_heads, preferred_element_typ...  72.6 us
    dot_general x2, matrix products, attend_backward(): jnp.einsum('hqk,qhe->khe', dscore, piece_heads, preferred_element_type=jn...  67.7 us
    all_gather x2, waiting for transfers between devices, attend_forward(): key_piece = lax.all_gather(keys, 'seq', axis=0, tiled=True)  67.4 us
    dot_general x2, matrix products, local(): jnp.dot(normed.astype(jnp.bfloat16), mat_in, preferred_element_type=jnp.f...  55.4 us
  transfers between devices with their start and end apart: 17, of which 10 were waited for; matrix products, arithmetic and copies ran while one was open for 49% of the time, Pallas kernels for 0%

profile of v1, /device:TPU:0, one launch (start us, length us, event | category | flops | bytes accessed | tf_op | source)
XLA Modules:
  0.0 1324.7 jit_solution(15581510739669614484)
XLA Ops:
  11.3 66.4 %all-gather.42.cloned.1.call-done = bf16[1,1024,3072]{2,1,0:T(8,128)(2,1)} async-done(((bf16[1,128,3072]{2,1,0:T(8,128)(2,1)}), bf16[1,1024,3072]{2,1,0:T(8,128)(2,1)}) %all-gather.42.cloned.1.call-update) | async-done | bytes 6291472 | tf_op jit(solution)/shard_map/all_gather | solution.py:203
  114.1 23.4 %all-gather.26.cloned.1.call-done = bf16[2048,1024]{1,0:T(8,128)(2,1)} async-done(((bf16[512,1024]{1,0:T(8,128)(2,1)}), bf16[2048,1024]{1,0:T(8,128)(2,1)}) %all-gather.26.cloned.1.call-update) | async-done | bytes 4194320 | tf_op jit(solution)/shard_map/all_gather | solution.py:63
  144.0 26.9 %fusion.6 = (f32[16,512]{1,0:T(8,128)S(1)}, f32[16,512,2048]{2,1,0:T(8,128)}) fusion(pred[512,2048]{1,0:T(8,128)(4,1)S(1)} %broadcast_compare_fusion.1, bf16[512,16,64]{0,2,1:T(8,128)(2,1)} %bitcast.348, bf16[2048,16,64]{0,2,1:T(8,128)(2,1)} %bitcast.339), kind=kOutput, calls=%fused_computation.16 | convolution fusion | flops 2197807104 | bytes 73433088 | tf_op jit(solution)/shard_map/qhe,khe->hqk/dot_general | solution.py:67
  171.5 21.5 %fusion = f32[16,512]{1,0:T(8,128)S(1)} fusion(f32[16,512,2048]{2,1,0:T(8,128)} %get-tuple-element.67, f32[16,512]{1,0:T(8,128)S(1)} %max.43, pred[512,2048]{1,0:T(8,128)(4,1)S(1)} %broadcast_compare_fusion.1), kind=kLoop, calls=%fused_computation.10 | loop fusion | flops 67100672 | bytes 68222976 | tf_op jit(solution)/shard_map/reduce_sum | solution.py:76
  199.6 27.6 %fusion.14 = f32[16,512,64]{1,2,0:T(8,128)} fusion(bf16[2048,16,64]{0,2,1:T(8,128)(2,1)} %bitcast.361, f32[16,512,2048]{2,1,0:T(8,128)} %get-tuple-element.67, f32[16,512]{1,0:T(8,128)S(1)} %max.43, pred[512,2048]{1,0:T(8,128)(4,1)S(1)} %broadcast_compare_fusion.1), kind=kOutput, calls=%fused_computation.21 | convolution fusion | flops 2214592512 | bytes 74481664 | tf_op jit(solution)/shard_map/hqk,khe->hqe/dot_general | solution.py:77
  237.9 68.4 %all-gather.46.cloned.1.call-done = bf16[1,1024,4096]{2,1,0:T(8,128)(2,1)} async-done(((bf16[1,128,4096]{2,1,0:T(8,128)(2,1)}), bf16[1,1024,4096]{2,1,0:T(8,128)(2,1)}) %all-gather.46.cloned.1.call-update) | async-done | bytes 8388624 | tf_op jit(solution)/shard_map/all_gather | solution.py:205
  306.3 27.1 %fusion.36 = (f32[512,4096]{1,0:T(8,128)}, f32[512,4096]{1,0:T(8,128)}) fusion(f32[4096]{0:T(1024)S(1)} %bitcast.399, bf16[1,1024,4096]{2,1,0:T(8,128)(2,1)} %all-gather.46.cloned.1.call-done, f32[512,1024]{1,0:T(8,128)S(1)} %get-tuple-element.69, f32[1024]{0:T(1024)S(1)} %bitcast.425, f32[1024]{0:T(1024)S(1)} %bitcast.412, f32[512]{0:T(512)S(1)} %fusion.196, ...), kind=kOutput, calls=%fused_computation.40 | convolution fusion | flops 4429709312 | bytes 27291648 | tf_op jit(solution)/shard_map/dot_general | solution.py:229
  333.4 55.6 %all-gather.48.cloned.1.call-done = bf16[1,4096,1024]{2,1,0:T(8,128)(2,1)} async-done(((bf16[1,512,1024]{2,1,0:T(8,128)(2,1)}), bf16[1,4096,1024]{2,1,0:T(8,128)(2,1)}) %all-gather.48.cloned.1.call-update) | async-done | bytes 8388624 | tf_op jit(solution)/shard_map/all_gather | solution.py:206
  389.0 11.2 fusion.246
  402.5 51.4 %all-gather.50.cloned.1.call-done = bf16[1,1024,3072]{2,1,0:T(8,128)(2,1)} async-done(((bf16[1,128,3072]{2,1,0:T(8,128)(2,1)}), bf16[1,1024,3072]{2,1,0:T(8,128)(2,1)}) %all-gather.50.cloned.1.call-update) | async-done | bytes 6291472 | tf_op jit(solution)/shard_map/all_gather | solution.py:203
  470.1 44.0 %all-gather.30.cloned.1.call-done = bf16[2048,1024]{1,0:T(8,128)(2,1)} async-done(((bf16[512,1024]{1,0:T(8,128)(2,1)}), bf16[2048,1024]{1,0:T(8,128)(2,1)}) %all-gather.30.cloned.1.call-update) | async-done | bytes 4194320 | tf_op jit(solution)/shard_map/all_gather | solution.py:63
  520.6 26.9 %fusion.7 = (f32[16,512]{1,0:T(8,128)S(1)}, f32[16,512,2048]{2,1,0:T(8,128)}) fusion(pred[512,2048]{1,0:T(8,128)(4,1)S(1)} %broadcast_compare_fusion.1, bf16[512,16,64]{0,2,1:T(8,128)(2,1)} %bitcast.351, bf16[2048,16,64]{0,2,1:T(8,128)(2,1)} %bitcast.341), kind=kOutput, calls=%fused_computation.17 | convolution fusion | flops 2197807104 | bytes 73433088 | tf_op jit(solution)/shard_map/qhe,khe->hqk/dot_general | solution.py:67
  547.5 21.7 %fusion.2 = f32[16,512]{1,0:T(8,128)S(1)} fusion(f32[16,512,2048]{2,1,0:T(8,128)} %get-tuple-element.77, f32[16,512]{1,0:T(8,128)S(1)} %max.45, pred[512,2048]{1,0:T(8,128)(4,1)S(1)} %broadcast_compare_fusion.1), kind=kLoop, calls=%fused_computation.12 | loop fusion | flops 67100672 | bytes 68222976 | tf_op jit(solution)/shard_map/reduce_sum | solution.py:76
  575.8 27.6 %fusion.12 = f32[16,512,64]{1,2,0:T(8,128)} fusion(bf16[2048,16,64]{0,2,1:T(8,128)(2,1)} %bitcast.363, f32[16,512,2048]{2,1,0:T(8,128)} %get-tuple-element.77, f32[16,512]{1,0:T(8,128)S(1)} %max.45, pred[512,2048]{1,0:T(8,128)(4,1)S(1)} %broadcast_compare_fusion.1), kind=kOutput, calls=%fused_computation.20 | convolution fusion | flops 2214592512 | bytes 74481664 | tf_op jit(solution)/shard_map/hqk,khe->hqe/dot_general | solution.py:77
  615.4 67.7 %all-gather.54.cloned.1.call-done = bf16[1,1024,4096]{2,1,0:T(8,128)(2,1)} async-done(((bf16[1,128,4096]{2,1,0:T(8,128)(2,1)}), bf16[1,1024,4096]{2,1,0:T(8,128)(2,1)}) %all-gather.54.cloned.1.call-update) | async-done | bytes 8388624 | tf_op jit(solution)/shard_map/all_gather | solution.py:205
  683.1 28.3 %fusion.37 = (f32[512,4096]{1,0:T(8,128)}, f32[512,4096]{1,0:T(8,128)}) fusion(f32[4096]{0:T(1024)S(1)} %bitcast.402, bf16[1,1024,4096]{2,1,0:T(8,128)(2,1)} %all-gather.54.cloned.1.call-done, f32[512,1024]{1,0:T(8,128)} %copy-done.24, f32[1024]{0:T(1024)S(1)} %bitcast.421, f32[1024]{0:T(1024)S(1)} %bitcast.418, f32[512]{0:T(512)S(1)} %fusion.198, ...), kind=kOutput, calls=%fused_computation.41 | convolution fusion | flops 4429709312 | bytes 27291648 | tf_op jit(solution)/shard_map/dot_general | solution.py:229
  711.4 54.3 %all-gather.56.cloned.1.call-done = bf16[1,4096,1024]{2,1,0:T(8,128)(2,1)} async-done(((bf16[1,512,1024]{2,1,0:T(8,128)(2,1)}), bf16[1,4096,1024]{2,1,0:T(8,128)(2,1)}) %all-gather.56.cloned.1.call-update) | async-done | bytes 8388624 | tf_op jit(solution)/shard_map/all_gather | solution.py:206
  765.7 15.4 %fusion.249 = (f32[512]{0:T(512)S(1)}, f32[512,1024]{1,0:T(8,128)}) fusion(f32[1024]{0:T(1024)S(1)} %bitcast.408, bf16[1,4096,1024]{2,1,0:T(8,128)(2,1)} %all-gather.56.cloned.1.call-done, f32[512,4096]{1,0:T(8,128)} %get-tuple-element.80, f32[512,4096]{1,0:T(8,128)} %get-tuple-element.81, f32[4096]{0:T(1024)S(1)} %bitcast.403, f32[1024]{0:T(1024)S(1)} %bitcast.422, ...), kind=kOutput, calls=%fused_computation.319 | convolution fusion | flops 4307025408 | bytes 29394944 | tf_op jit(solution)/shard_map/dot_general | solution.py:235
  789.8 30.8 %multiply_reduce_fusion.2 = (f32[512]{0:T(512)S(1)}, f32[512,1024]{1,0:T(8,128)}) fusion(f32[512,1024]{1,0:T(8,128)} %copy-done.24, f32[512]{0:T(512)S(1)} %broadcast_multiply_fusion.1, f32[1024]{0:T(1024)S(1)} %bitcast.420, bf16[1,1024,4096]{2,1,0:T(8,128)(2,1)} %all-gather.54.cloned.1.call-done, f32[512,4096]{1,0:T(8,128)} %get-tuple-element.80, ...), kind=kOutput, calls=%fused_computation.156 | convolution fusion | flops 8632926208 | bytes 40931328 | tf_op jit(solution)/shard_map/dot_general | solution.py:26
  848.9 36.3 %fusion.16 = f32[16,64,512]{2,1,0:T(8,128)} fusion(bf16[2048,16,64]{0,2,1:T(8,128)(2,1)} %bitcast.342, f32[16,512,2048]{2,1,0:T(8,128)} %get-tuple-element.77, f32[16,512]{1,0:T(8,128)S(1)} %bitcast.392, f32[16,512]{1,0:T(8,128)S(1)} %log_add_fusion.1, pred[512,2048]{1,0:T(8,128)(4,1)S(1)} %broadcast_compare_fusion.1, bf16[512,16,64]{0,2,1:T(8,128)(2,1)} %bitcast.357, ...), kind=kOutput, calls=%fused_computation.22 | convolution fusion | flops 4395630592 | bytes 79757312 | tf_op jit(solution)/shard_map/hqk,khe->qhe/dot_general | solution.py:143
  891.7 8.2 all_gather.96
  899.9 8.2 all_gather.94
  916.8 25.4 %fusion.254 = f32[16,2048,512]{2,1,0:T(8,128)} fusion(bf16[2048,16,64]{0,2,1:T(8,128)(2,1)} %bitcast.345, bf16[512,16,64]{0,2,1:T(8,128)(2,1)S(1)} %bitcast.359), kind=kOutput, calls=%fused_computation.320 | convolution fusion | flops 2147483648 | bytes 72351744 | tf_op jit(solution)/shard_map/qhe,khe->hqk/dot_general | solution.py:160
  948.8 26.7 %fusion.153 = bf16[16,64,512]{2,1,0:T(8,128)(2,1)} fusion(bf16[2048,16,64]{0,2,1:T(8,128)(2,1)} %bitcast.367, f32[16,2048,512]{2,1,0:T(8,128)} %fusion.254, f32[16,2048]{1,0:T(8,128)S(1)} %convert_bitcast_fusion.3, pred[2048,512]{1,0:T(8,128)(4,1)S(1)} %copy-done.40), kind=kOutput, calls=%fused_computation.189 | convolution fusion | flops 2215116800 | bytes 73531392 | tf_op jit(solution)/shard_map/hqk,qhe->khe/dot_general | solution.py:170
  975.5 34.0 %multiply_convert_fusion.14 = bf16[16,64,512]{2,1,0:T(8,128)(2,1)} fusion(bf16[2048,16,64]{0,2,1:T(8,128)(2,1)} %bitcast.346, f32[16,2048,512]{2,1,0:T(8,128)} %fusion.254, f32[16,2048]{1,0:T(8,128)S(1)} %convert_bitcast_fusion.2, f32[16,2048]{1,0:T(8,128)S(1)} %convert_bitcast_fusion.3, pred[2048,512]{1,0:T(8,128)(4,1)} %broadcast_compare_fusion, ...), kind=kOutput, calls=%fused_computation.151 | convolution fusion | flops 4396679168 | bytes 78905344 | tf_op jit(solution)/shard_map/hqk,qhe->khe/dot_general | solution.py:168
  1019.6 20.2 %multiply_reduce_fusion = (f32[512]{0:T(512)S(1)}, f32[512,1024]{1,0:T(8,128)}) fusion(f32[512,1024]{1,0:T(8,128)S(1)} %copy-done.21, f32[512]{0:T(512)S(1)} %copy-done.68, f32[1024]{0:T(1024)S(1)} %bitcast.414, bf16[1,1024,4096]{2,1,0:T(8,128)(2,1)} %all-gather.46.cloned.1.call-done, f32[512,4096]{1,0:T(8,128)} %get-tuple-element.70, ...), kind=kOutput, calls=%fused_computation.147 | convolution fusion | flops 8625586176 | bytes 39872512 | tf_op jit(solution)/shard_map/dot_general | solution.py:26
  1069.8 25.9 %fusion.255 = f32[16,2048,512]{2,1,0:T(8,128)} fusion(bf16[2048,16,64]{0,2,1:T(8,128)(2,1)} %bitcast.343, bf16[512,16,64]{0,2,1:T(8,128)(2,1)S(1)} %bitcast.360), kind=kOutput, calls=%fused_computation.321 | convolution fusion | flops 2147483648 | bytes 72351744 | tf_op jit(solution)/shard_map/qhe,khe->hqk/dot_general | solution.py:160
  1112.0 36.3 %fusion.18 = f32[16,64,512]{2,1,0:T(8,128)} fusion(bf16[2048,16,64]{0,2,1:T(8,128)(2,1)} %bitcast.340, f32[16,512,2048]{2,1,0:T(8,128)} %get-tuple-element.67, f32[16,512]{1,0:T(8,128)S(1)} %bitcast.390, f32[16,512]{1,0:T(8,128)S(1)} %copy-done.51, pred[512,2048]{1,0:T(8,128)(4,1)S(1)} %copy-done.1, bf16[512,16,64]{0,2,1:T(8,128)(2,1)S(1)} %bitcast.355, ...), kind=kOutput, calls=%fused_computation.24 | convolution fusion | flops 4395630592 | bytes 79757312 | tf_op jit(solution)/shard_map/hqk,khe->qhe/dot_general | solution.py:143
  1150.4 38.3 %all-reduce.3.cloned.1.call-done = (f32[1,64,1024]{2,1,0:T(8,128)}, f32[1,64,1024]{2,1,0:T(8,128)}, f32[1,64,1024]{2,1,0:T(8,128)}, f32[1,64,1024]{2,1,0:T(8,128)}) async-done(((f32[1,64,1024]{2,1,0:T(8,128)}, f32[1,64,1024]{2,1,0:T(8,128)}, f32[1,64,1024]{2,1,0:T(8,128)}, f32[1,64,1024]{2,1,0:T(8,128)}), (f32[1,64,1024]{2,1,0:T(8,128)}, f32[1,64,1024]{2,1,0:T(8,128)}, f32[1,64,1024]{2,1,0:T(8,128)}, ...) | async-done | bytes 1048592 | tf_op jit(solution)/shard_map/psum | solution.py:285
  1192.5 50.5 %all-gather.40.cloned.1.call-done = bf16[2048,1024]{1,0:T(8,128)(2,1)} async-done(((bf16[512,1024]{1,0:T(8,128)(2,1)}), bf16[2048,1024]{1,0:T(8,128)(2,1)}) %all-gather.40.cloned.1.call-update) | async-done | bytes 4194320 | tf_op jit(solution)/shard_map/all_gather | solution.py:149
  1249.5 26.7 %fusion.156 = bf16[16,64,512]{2,1,0:T(8,128)(2,1)} fusion(bf16[2048,16,64]{0,2,1:T(8,128)(2,1)} %bitcast.365, f32[16,2048,512]{2,1,0:T(8,128)} %fusion.255, f32[16,2048]{1,0:T(8,128)S(1)} %copy-done.58, pred[2048,512]{1,0:T(8,128)(4,1)S(1)} %copy-done.41), kind=kOutput, calls=%fused_computation.190 | convolution fusion | flops 2215116800 | bytes 73531392 | tf_op jit(solution)/shard_map/hqk,qhe->khe/dot_general | solution.py:170
  1276.2 33.7 %multiply_convert_fusion.12 = bf16[16,64,512]{2,1,0:T(8,128)(2,1)} fusion(bf16[2048,16,64]{0,2,1:T(8,128)(2,1)} %bitcast.344, f32[16,2048,512]{2,1,0:T(8,128)} %fusion.255, f32[16,2048]{1,0:T(8,128)S(1)} %convert_bitcast_fusion, f32[16,2048]{1,0:T(8,128)S(1)} %copy-done.58, pred[2048,512]{1,0:T(8,128)(4,1)} %broadcast_compare_fusion, ...), kind=kOutput, calls=%fused_computation.143 | convolution fusion | flops 4396679168 | bytes 78905344 | tf_op jit(solution)/shard_map/hqk,qhe->khe/dot_general | solution.py:168
  (360 shorter events, 242.7 us)
Async XLA Ops:
  7.2 70.5 %all-gather.42.cloned.1.call-start = ((), (), s32[]{:S(2)}) async-start(), calls=%async_computation.8 | async-start | bytes 7077888 | tf_op jit(solution)/shard_map/all_gather | solution.py:203
  9.9 127.6 %all-gather.26.cloned.1.call-start = ((), (), s32[]{:S(2)}) async-start(), calls=%async_computation | async-start | bytes 5242880 | tf_op jit(solution)/shard_map/all_gather | solution.py:63
  85.9 107.1 %all-gather.28.cloned.1.call-start = ((), (), s32[]{:S(2)}) async-start(), calls=%async_computation.1 | async-start | bytes 5242880 | tf_op jit(solution)/shard_map/all_gather | solution.py:64
  86.7 145.3 %all-gather.44.cloned.1.call-start = ((), (), s32[]{:S(2)}) async-start(), calls=%async_computation.9 | async-start | bytes 2359296 | tf_op jit(solution)/shard_map/all_gather | solution.py:204
  87.6 218.7 %all-gather.46.cloned.1.call-start = ((), (), s32[]{:S(2)}) async-start(), calls=%async_computation.10 | async-start | bytes 9437184 | tf_op jit(solution)/shard_map/all_gather | solution.py:205
  90.8 298.1 %all-gather.48.cloned.1.call-start = ((), (), s32[]{:S(2)}) async-start(), calls=%async_computation.11 | async-start | bytes 9437184 | tf_op jit(solution)/shard_map/all_gather | solution.py:206
  94.4 359.5 %all-gather.50.cloned.1.call-start = ((), (), s32[]{:S(2)}) async-start(), calls=%async_computation.12 | async-start | bytes 7077888 | tf_op jit(solution)/shard_map/all_gather | solution.py:203
  95.1 419.0 %all-gather.30.cloned.1.call-start = ((), (), s32[]{:S(2)}) async-start(), calls=%async_computation.2 | async-start | bytes 5242880 | tf_op jit(solution)/shard_map/all_gather | solution.py:63
  104.6 744.3 %copy-start = (pred[512,2048]{1,0:T(8,128)(4,1)}, pred[512,2048]{1,0:T(8,128)(4,1)S(1)}, u32[]{:S(2)}) copy-start(pred[512,2048]{1,0:T(8,128)(4,1)S(1)} %broadcast_compare_fusion.1) | copy-start | bytes 3145732
  108.4 280.5 %copy-start.77 = (f32[1,4096]{1,0:T(1,128)}, f32[1,4096]{1,0:T(1,128)S(1)}, u32[]{:S(2)}) copy-start(f32[1,4096]{1,0:T(1,128)S(1)} %get-tuple-element.43) | copy-start | bytes 49156
  113.6 114.9 %copy-start.2 = (f32[16,512,64]{1,2,0:T(8,128)}, f32[16,512,64]{1,2,0:T(8,128)S(1)}, u32[]{:S(2)}) copy-start(f32[16,512,64]{1,2,0:T(8,128)S(1)} %get-tuple-element.65) | copy-start | bytes 6291460
  113.7 114.9 %copy-start.42 = (f32[16,512]{1,0:T(8,128)}, f32[16,512]{1,0:T(8,128)S(1)}, u32[]{:S(2)}) copy-start(f32[16,512]{1,0:T(8,128)S(1)} %get-tuple-element.64) | copy-start | bytes 98308
  114.1 113.1 %copy-start.52 = (f32[16,512]{1,0:T(8,128)}, f32[16,512]{1,0:T(8,128)S(1)}, u32[]{:S(2)}) copy-start(f32[16,512]{1,0:T(8,128)S(1)} %fusion.115) | copy-start | bytes 98308
  236.7 152.3 %copy-start.20 = (f32[512,1024]{1,0:T(8,128)}, f32[512,1024]{1,0:T(8,128)S(1)}, u32[]{:S(2)}) copy-start(f32[512,1024]{1,0:T(8,128)S(1)} %get-tuple-element.69) | copy-start | bytes 6291460
  236.7 152.2 %copy-start.67 = (f32[512]{0:T(512)}, f32[512]{0:T(512)S(1)}, u32[]{:S(2)}) copy-start(f32[512]{0:T(512)S(1)} %broadcast_multiply_fusion.3) | copy-start | bytes 6148
  237.9 151.0 %copy-start.82 = (f32[512]{0:T(512)}, f32[512]{0:T(512)S(1)}, u32[]{:S(2)}) copy-start(f32[512]{0:T(512)S(1)} %fusion.196) | copy-start | bytes 6148
  306.3 82.7 %copy-start.90 = (f32[1,1024]{1,0:T(1,128)S(1)}, f32[1,1024]{1,0:T(1,128)}, u32[]{:S(2)}) copy-start(f32[1,1024]{1,0:T(1,128)} %get-tuple-element.59) | copy-start | bytes 12292
  400.3 208.0 %copy-start.69 = (f32[512]{0:T(512)}, f32[512]{0:T(512)S(1)}, u32[]{:S(2)}) copy-start(f32[512]{0:T(512)S(1)} %broadcast_multiply_fusion.2) | copy-start | bytes 6148
  402.5 205.8 %copy-start.84 = (f32[512]{0:T(512)}, f32[512]{0:T(512)S(1)}, u32[]{:S(2)}) copy-start(f32[512]{0:T(512)S(1)} %fusion.197) | copy-start | bytes 6148
  462.6 106.7 %all-gather.32.cloned.1.call-start = ((), (), s32[]{:S(2)}) async-start(), calls=%async_computation.3 | async-start | bytes 5242880 | tf_op jit(solution)/shard_map/all_gather | solution.py:64
  463.3 145.0 %all-gather.52.cloned.1.call-start = ((), (), s32[]{:S(2)}) async-start(), calls=%async_computation.13 | async-start | bytes 2359296 | tf_op jit(solution)/shard_map/all_gather | solution.py:204
  463.9 219.1 %all-gather.54.cloned.1.call-start = ((), (), s32[]{:S(2)}) async-start(), calls=%async_computation.14 | async-start | bytes 9437184 | tf_op jit(solution)/shard_map/all_gather | solution.py:205
  464.6 301.1 %all-gather.56.cloned.1.call-start = ((), (), s32[]{:S(2)}) async-start(), calls=%async_computation.15 | async-start | bytes 9437184 | tf_op jit(solution)/shard_map/all_gather | solution.py:206
  465.2 444.7 %all-gather.34.cloned.1.call-start = ((), (), s32[]{:S(2)}) async-start(), calls=%async_computation.4 | async-start | bytes 5242880 | tf_op jit(solution)/shard_map/all_gather | solution.py:148
  467.7 474.5 %all-gather.36.cloned.1.call-start = ((), (), s32[]{:S(2)}) async-start(), calls=%async_computation.5 | async-start | bytes 5242880 | tf_op jit(solution)/shard_map/all_gather | solution.py:149
  470.1 133.2 %copy-start.53 = (f32[16,512]{1,0:T(8,128)}, f32[16,512]{1,0:T(8,128)S(1)}, u32[]{:S(2)}) copy-start(f32[16,512]{1,0:T(8,128)S(1)} %fusion.117) | copy-start | bytes 98308
  608.3 74.7 %copy-start.79 = (f32[1,4096]{1,0:T(1,128)S(1)}, f32[1,4096]{1,0:T(1,128)}, u32[]{:S(2)}) copy-start(f32[1,4096]{1,0:T(1,128)} %get-tuple-element.42) | copy-start | bytes 49156
  608.3 74.7 %copy-start.97 = (f32[1,1,1024]{2,1,0:T(1,128)S(1)}, f32[1,1,1024]{2,1,0:T(1,128)}, u32[]{:S(2)}) copy-start(f32[1,1,1024]{2,1,0:T(1,128)} %get-tuple-element.47) | copy-start | bytes 12292
  683.1 82.6 %copy-start.88 = (f32[1,1024]{1,0:T(1,128)S(1)}, f32[1,1024]{1,0:T(1,128)}, u32[]{:S(2)}) copy-start(f32[1,1024]{1,0:T(1,128)} %get-tuple-element.58) | copy-start | bytes 12292
  827.1 236.0 %all-gather.38.cloned.1.call-start = ((), (), s32[]{:S(2)}) async-start(), calls=%async_computation.6 | async-start | bytes 5242880 | tf_op jit(solution)/shard_map/all_gather | solution.py:148
  828.8 359.9 %all-reduce.3.cloned.1.call-start = ((), (), s32[]{:S(2)}) async-start(), calls=%async_computation.16 | async-start | bytes 2097152 | tf_op jit(solution)/shard_map/psum | solution.py:285
  1060.4 182.5 %all-gather.40.cloned.1.call-start = ((), (), s32[]{:S(2)}) async-start(), calls=%async_computation.7 | async-start | bytes 5242880 | tf_op jit(solution)/shard_map/all_gather | solution.py:149
  (88 other events, 1485.0 us)
Sparse Core Ops, SparseCore 0:
  10.2 67.4 all-gather.41
  86.1 51.4 all-gather.25
  139.4 52.6 all-gather.27
  194.1 29.0 all-gather.43
  224.7 81.5 all-gather.45
  308.3 80.5 all-gather.47
  390.6 63.2 all-gather.49
  462.7 51.3 all-gather.29
  516.0 52.6 all-gather.31
  570.7 29.0 all-gather.51
  601.5 81.5 all-gather.53
  685.1 80.5 all-gather.55
  767.5 51.2 all-gather.33
  827.2 50.7 all-gather.35
  879.8 53.5 all-gather.37
  1060.5 128.1 all-reduce.2
  1191.1 51.7 all-gather.39

commit v2 on v0

v2 whole, which is shorter than its diff:
```python
import functools
import math

import jax
import jax.numpy as jnp
from jax import lax
from jax.experimental import pallas as pl
from jax.experimental.pallas import tpu as pltpu
from jax.sharding import PartitionSpec as P

HEADS = 16
HEAD = 64

SCALE = 0.125
LOG2_E = math.log2(math.e)
LN_2 = math.log(2.0)
EPS = 1e-05
BLOCK = 256
VMEM_BYTES = 48 * 2**20


def dot(left, right):
    return jnp.dot(left, right, preferred_element_type=jnp.float32)


def back_dot(left, right):
    return lax.dot_general(
        left, right, (((1,), (1,)), ((), ())), preferred_element_type=jnp.float32
    )


def normalize(values):
    center = jnp.mean(values, -1, keepdims=True)
    centered = values - center
    spread = jnp.mean(centered * centered, -1, keepdims=True)
    inverse = lax.rsqrt(spread + EPS)
    return centered * inverse, inverse


def normalize_back(gradient, normal, inverse, gain_row):
    scaled = gradient * gain_row
    first = jnp.mean(scaled, -1, keepdims=True)
    second = jnp.mean(scaled * normal, -1, keepdims=True)
    return (scaled - first - normal * second) * inverse


def gelu_pair(inner):
    bell = jnp.exp(inner * inner * -0.5)
    phi = 0.5 + 0.5 * lax.erf(inner * (0.5**0.5))
    return inner * phi, phi + inner * bell * ((2.0 * math.pi) ** -0.5)


def head_rows(step_heads, head, block):
    if step_heads == 1:
        return block
    parts = [
        block[other * HEAD : (other + 1) * HEAD]
        if other == head
        else jnp.zeros((HEAD, block.shape[1]), block.dtype)
        for other in range(step_heads)
    ]
    return jnp.concatenate(parts, 0)


def same_pair(code_columns, code_row):
    columns = jnp.concatenate([code_columns] * (code_row.shape[1] // code_columns.shape[1]), 1)
    return columns == code_row


def forward_kernel(
    step_heads,
    low_ref,
    high_ref,
    q_ref,
    k_ref,
    v_ref,
    pk_ref,
    pv_ref,
    columns_ref,
    row_ref,
    context_ref,
    turned_ref,
    total_ref,
    q_turned,
    v_turned,
):
    blocks = q_ref.shape[0] // BLOCK
    q_turned[...] = q_ref[...].T
    v_turned[...] = v_ref[...].T
    prefix_turned = pv_ref[...].T

    def query_step(i, carry):
        at = pl.ds(pl.multiple_of(i * BLOCK, BLOCK), BLOCK)
        code_row = row_ref[:, at]
        q_block = q_turned[:, at]
        rows = [head_rows(step_heads, h, q_block) for h in range(step_heads)]
        state = []
        for h in range(step_heads):
            scores = dot(pk_ref[...], rows[h])
            top = jnp.max(scores, 0, keepdims=True)
            weights = jnp.exp2(scores - top)
            total = jnp.sum(weights, 0, keepdims=True)
            values = prefix_turned[h * HEAD : (h + 1) * HEAD]
            state.append((top, total, dot(values, weights.astype(jnp.bfloat16))))

        def key_step(j, state):
            place = pl.ds(pl.multiple_of(j * BLOCK, BLOCK), BLOCK)
            keys = k_ref[place, :]
            seen = same_pair(columns_ref[place, :], code_row)
            result = []
            for h in range(step_heads):
                top, total, summed = state[h]
                scores = jnp.where(seen, dot(keys, rows[h]), -jnp.inf)
                new_top = jnp.maximum(top, jnp.max(scores, 0, keepdims=True))
                factor = jnp.exp2(top - new_top)
                weights = jnp.exp2(scores - new_top)
                total = total * factor + jnp.sum(weights, 0, keepdims=True)
                values = v_turned[h * HEAD : (h + 1) * HEAD, place]
                summed = summed * factor + dot(values, weights.astype(jnp.bfloat16))
                result.append((new_top, total, summed))
            return tuple(result)

        state = lax.fori_loop(low_ref[i], high_ref[i], key_step, tuple(state))
        parts = []
        for h in range(step_heads):
            top, total, summed = state[h]
            parts.append(summed / total)
            total_ref[0, h : h + 1, at] = top + jnp.log2(total)
        turned = parts[0] if step_heads == 1 else jnp.concatenate(parts, 0)
        turned_ref[:, at] = turned
        context_ref[at, :] = turned.T.astype(jnp.bfloat16)
        return carry

    lax.fori_loop(0, blocks, query_step, 0)


def backward_kernel(
    step_heads,
    low_ref,
    high_ref,
    q_ref,
    k_ref,
    v_ref,
    g_ref,
    pk_ref,
    pv_ref,
    turned_ref,
    total_ref,
    columns_ref,
    row_ref,
    grads_ref,
    pk_grad_ref,
    pv_grad_ref,
    q_turned,
    g_turned,
    q_alone,
    g_alone,
    k_turned,
    q_sum,
    delta_ref,
    k_sum,
    v_sum,
    pk_sum,
    pv_sum,
):
    row_count, width = q_ref.shape
    blocks = row_count // BLOCK
    q_all = q_ref[...].T
    g_all = g_ref[...].T
    k_turned[...] = k_ref[...].T
    prefix_turned = pk_ref[...].T
    lane = lax.broadcasted_iota(jnp.int32, (1, width), 1)
    for h in range(step_heads):
        q_turned[h] = head_rows(step_heads, h, q_all)
        g_turned[h] = head_rows(step_heads, h, g_all)
        own = (lane // HEAD == h).astype(jnp.bfloat16)
        q_alone[h] = q_ref[...] * own
        g_alone[h] = g_ref[...] * own
        part = slice(h * HEAD, (h + 1) * HEAD)
        delta_ref[h : h + 1, :] = jnp.sum(
            g_all[part].astype(jnp.float32) * turned_ref[part, :], 0, keepdims=True
        )
    q_sum[...] = jnp.zeros_like(q_sum)
    pk_sum[...] = jnp.zeros_like(pk_sum)
    pv_sum[...] = jnp.zeros_like(pv_sum)

    def pair_of_blocks(i, keys, values, keys_turned, seen, key_total, value_total):
        at = pl.ds(pl.multiple_of(i * BLOCK, BLOCK), BLOCK)
        if seen is not None:
            seen = same_pair(seen, row_ref[:, at])
        for h in range(step_heads):
            part = slice(h * HEAD, (h + 1) * HEAD)
            scores = dot(keys, q_turned[h, :, at])
            weights = jnp.exp2(scores - total_ref[0, h : h + 1, at])
            if seen is not None:
                weights = jnp.where(seen, weights, 0.0)
            grad_weights = dot(values, g_turned[h, :, at])
            grad_scores = (weights * (grad_weights - delta_ref[h : h + 1, at])).astype(jnp.bfloat16)
            value_total[...] += dot(weights.astype(jnp.bfloat16), g_alone[h, at, :])
            key_total[...] += dot(grad_scores, q_alone[h, at, :])
            q_sum[part, at] += dot(keys_turned[part, :], grad_scores)

    def prefix_step(i, carry):
        pair_of_blocks(i, pk_ref[...], pv_ref[...], prefix_turned, None, pk_sum, pv_sum)
        return carry

    lax.fori_loop(0, blocks, prefix_step, 0)
    pk_grad_ref[...] = pk_sum[...] * LN_2
    pv_grad_ref[...] = pv_sum[...]

    def key_step(j, carry):
        place = pl.ds(pl.multiple_of(j * BLOCK, BLOCK), BLOCK)
        k_sum[...] = jnp.zeros_like(k_sum)
        v_sum[...] = jnp.zeros_like(v_sum)
        keys, values = k_ref[place, :], v_ref[place, :]
        keys_turned = k_turned[:, place]
        seen = columns_ref[place, :]

        def query_step(i, carry):
            pair_of_blocks(i, keys, values, keys_turned, seen, k_sum, v_sum)
            return carry

        lax.fori_loop(low_ref[j], high_ref[j], query_step, 0)
        grads_ref[1, place, :] = (k_sum[...] * LN_2).astype(jnp.bfloat16)
        grads_ref[2, place, :] = v_sum[...].astype(jnp.bfloat16)
        return carry

    lax.fori_loop(0, blocks, key_step, 0)
    grads_ref[0] = (q_sum[...] * SCALE).T.astype(jnp.bfloat16)


def attend(queries, keys, values, prefix_k, prefix_v, low, high, columns, row):
    rows, width = queries.shape
    step_heads = 2 if width % (2 * HEAD) == 0 else 1
    part = step_heads * HEAD
    steps = width // part
    prefix = prefix_k.shape[0]
    whole = pl.BlockSpec((rows, part), lambda p, *_: (0, p))
    few = pl.BlockSpec((prefix, part), lambda p, *_: (0, p))
    return pl.pallas_call(
        functools.partial(forward_kernel, step_heads),
        grid_spec=pltpu.PrefetchScalarGridSpec(
            num_scalar_prefetch=2,
            grid=(steps,),
            in_specs=[
                whole,
                whole,
                whole,
                few,
                few,
                pl.BlockSpec(columns.shape, lambda p, *_: (0, 0)),
                pl.BlockSpec(row.shape, lambda p, *_: (0, 0)),
            ],
            out_specs=[
                whole,
                pl.BlockSpec((part, rows), lambda p, *_: (p, 0)),
                pl.BlockSpec((1, 8, rows), lambda p, *_: (p, 0, 0)),
            ],
            scratch_shapes=[pltpu.VMEM((part, rows), jnp.bfloat16)] * 2,
        ),
        out_shape=[
            jax.ShapeDtypeStruct((rows, width), jnp.bfloat16),
            jax.ShapeDtypeStruct((width, rows), jnp.float32),
            jax.ShapeDtypeStruct((steps, 8, rows), jnp.float32),
        ],
        compiler_params=pltpu.CompilerParams(vmem_limit_bytes=VMEM_BYTES),
        name="attend",
    )(low, high, queries, keys, values, prefix_k, prefix_v, columns, row)


def attend_back(
    queries, keys, values, grads, prefix_k, prefix_v, turned, total, low, high, columns, row
):
    rows, width = queries.shape
    step_heads = 2 if width % (2 * HEAD) == 0 else 1
    part = step_heads * HEAD
    steps = width // part
    prefix = prefix_k.shape[0]
    whole = pl.BlockSpec((rows, part), lambda p, *_: (0, p))
    few = pl.BlockSpec((prefix, part), lambda p, *_: (0, p))
    return pl.pallas_call(
        functools.partial(backward_kernel, step_heads),
        grid_spec=pltpu.PrefetchScalarGridSpec(
            num_scalar_prefetch=2,
            grid=(steps,),
            in_specs=[
                whole,
                whole,
                whole,
                whole,
                few,
                few,
                pl.BlockSpec((part, rows), lambda p, *_: (p, 0)),
                pl.BlockSpec((1, 8, rows), lambda p, *_: (p, 0, 0)),
                pl.BlockSpec(columns.shape, lambda p, *_: (0, 0)),
                pl.BlockSpec(row.shape, lambda p, *_: (0, 0)),
            ],
            out_specs=[
                pl.BlockSpec((3, rows, part), lambda p, *_: (0, 0, p)),
                few,
                few,
            ],
            scratch_shapes=[
                pltpu.VMEM((step_heads, part, rows), jnp.bfloat16),
                pltpu.VMEM((step_heads, part, rows), jnp.bfloat16),
                pltpu.VMEM((step_heads, rows, part), jnp.bfloat16),
                pltpu.VMEM((step_heads, rows, part), jnp.bfloat16),
                pltpu.VMEM((part, rows), jnp.bfloat16),
                pltpu.VMEM((part, rows), jnp.float32),
                pltpu.VMEM((8, rows), jnp.float32),
                pltpu.VMEM((BLOCK, part), jnp.float32),
                pltpu.VMEM((BLOCK, part), jnp.float32),
                pltpu.VMEM((prefix, part), jnp.float32),
                pltpu.VMEM((prefix, part), jnp.float32),
            ],
        ),
        out_shape=[
            jax.ShapeDtypeStruct((3, rows, width), jnp.bfloat16),
            jax.ShapeDtypeStruct((prefix, width), jnp.float32),
            jax.ShapeDtypeStruct((prefix, width), jnp.float32),
        ],
        compiler_params=pltpu.CompilerParams(vmem_limit_bytes=VMEM_BYTES),
        name="attend_back",
    )(
        low,
        high,
        queries,
        keys,
        values,
        grads,
        prefix_k,
        prefix_v,
        turned,
        total,
        columns,
        row,
    )


def local(
    dp_count,
    seq_count,
    first_layer_input,
    cotangent,
    lengths,
    w_qkv,
    bias_qkv,
    w_out,
    bias_out,
    w_in,
    bias_in,
    w_back,
    bias_back,
    norm_gain,
    norm_shift,
    prefix_keys,
    prefix_values,
):
    row_count = first_layer_input.shape[1]
    width = first_layer_input.shape[2]
    layer_count = w_qkv.shape[0]
    all_rows = row_count * seq_count
    own_width = width // seq_count
    me = lax.axis_index("seq")

    def swap(value, step):
        if step == 0:
            return value
        return lax.ppermute(value, "seq", [(i, i ^ step) for i in range(seq_count)])

    def partner(step):
        return me ^ step

    def spread(matrix):
        share = matrix.shape[0] // seq_count
        piece = lax.dynamic_slice_in_dim(matrix, me * share, share, 0)
        return lax.all_gather(piece, ("dp", "seq"), axis=0, tiled=True)

    def own_columns(values, axis):
        return lax.dynamic_slice_in_dim(values, me * own_width, own_width, axis)

    pair_at = jnp.arange(lengths.shape[1], dtype=jnp.int32)
    ends = jnp.sum(
        jnp.where(pair_at[:, None] <= pair_at[None, :], lengths[0][:, None], 0), 0, dtype=jnp.int32
    )
    starts = ends - lengths[0]
    places = jnp.arange(all_rows, dtype=jnp.int32)
    codes = jnp.sum((places[:, None] >= ends[None, :]).astype(jnp.int32), 1, dtype=jnp.int32)
    columns = jnp.broadcast_to(codes[:, None], (all_rows, 128))
    row = codes[None, :]
    first = jnp.arange(all_rows // BLOCK, dtype=jnp.int32) * BLOCK
    after = first + BLOCK
    low = jnp.max(jnp.where(starts[None, :] <= first[:, None], starts[None, :], 0), 1) // BLOCK
    high = jnp.min(jnp.where(ends[None, :] >= after[:, None], ends[None, :], all_rows), 1)
    high = (high + BLOCK - 1) // BLOCK

    def in_swap_order(blocks, axis):
        return jnp.concatenate(
            [
                lax.dynamic_slice_in_dim(blocks, partner(step), 1, axis)
                for step in range(seq_count)
            ],
            axis,
        )

    current = first_layer_input[0]
    saved = []
    for layer in range(layer_count):
        gains = norm_gain[layer].astype(jnp.float32)
        shifts = norm_shift[layer].astype(jnp.float32)
        shard = w_qkv[layer].reshape(-1, 3, width)
        mat_own = lax.all_gather(
            own_columns(shard, 2).reshape(-1, 3 * own_width), "dp", axis=0, tiled=True
        )
        mat_out = spread(w_out[layer])
        mat_in = spread(w_in[layer])
        mat_back = spread(w_back[layer])
        out_blocks = in_swap_order(mat_out.reshape(seq_count, own_width, width), 0)
        mat_out = out_blocks.reshape(width, width)
        bias_own = own_columns(bias_qkv[layer].reshape(3, width).astype(jnp.float32), 1)
        prefix_k = own_columns(prefix_keys[layer], 1)
        prefix_v = own_columns(prefix_values[layer], 1)

        tokens = jnp.zeros((all_rows, width), jnp.bfloat16)
        for step in range(seq_count):
            tokens = lax.dynamic_update_slice_in_dim(
                tokens, swap(current, step), partner(step) * row_count, 0
            )
        projected = [
            dot(tokens, mat_own[:, n * own_width : (n + 1) * own_width]) + bias_own[n]
            for n in range(3)
        ]
        queries = (projected[0] * (SCALE * LOG2_E)).astype(jnp.bfloat16)
        keys = projected[1].astype(jnp.bfloat16)
        values = projected[2].astype(jnp.bfloat16)
        context, turned, total = attend(
            queries, keys, values, prefix_k, prefix_v, low, high, columns, row
        )
        pieces = [
            swap(
                lax.dynamic_slice_in_dim(context, partner(step) * row_count, row_count, 0), step
            )
            for step in range(seq_count)
        ]
        residual_one = (
            current.astype(jnp.float32)
            + dot(jnp.concatenate(pieces, 1), mat_out)
            + bias_out[layer].astype(jnp.float32)
        )
        normal_one, inverse_one = normalize(residual_one)
        normed = normal_one * gains[0] + shifts[0]
        inner = dot(normed.astype(jnp.bfloat16), mat_in) + bias_in[layer].astype(jnp.float32)
        activated, slope = gelu_pair(inner)
        slope = slope.astype(jnp.bfloat16)
        residual_two = (
            normed
            + dot(activated.astype(jnp.bfloat16), mat_back)
            + bias_back[layer].astype(jnp.float32)
        )
        normal_two, inverse_two = normalize(residual_two)
        result = normal_two * gains[1] + shifts[1]
        current = result.astype(jnp.bfloat16)
        saved.append(
            (
                (queries, keys, values, prefix_k, prefix_v, turned, total),
                (normal_one, inverse_one, slope, normal_two, inverse_two),
                (mat_out, mat_in, mat_back),
            )
        )

    gradient = cotangent[0].astype(jnp.float32)
    prefix_grads = []
    for layer in reversed(range(layer_count)):
        heads, norms, matrices = saved[layer]
        queries, keys, values, prefix_k, prefix_v, turned, total = heads
        normal_one, inverse_one, slope, normal_two, inverse_two = norms
        mat_out, mat_in, mat_back = matrices
        mat_qkv = spread(w_qkv[layer])
        qkv_blocks = in_swap_order(mat_qkv.reshape(width, 3, seq_count, own_width), 2)
        gains = norm_gain[layer].astype(jnp.float32)
        grad_two = normalize_back(gradient, normal_two, inverse_two, gains[1])
        grad_inner = back_dot(grad_two.astype(jnp.bfloat16), mat_back) * slope.astype(jnp.float32)
        grad_normed = grad_two + back_dot(grad_inner.astype(jnp.bfloat16), mat_in)
        grad_one = normalize_back(grad_normed, normal_one, inverse_one, gains[0])
        grad_context = back_dot(grad_one.astype(jnp.bfloat16), mat_out).astype(jnp.bfloat16)
        grads = jnp.zeros((all_rows, own_width), jnp.bfloat16)
        for step in range(seq_count):
            piece = grad_context[:, step * own_width : (step + 1) * own_width]
            grads = lax.dynamic_update_slice_in_dim(
                grads, swap(piece, step), partner(step) * row_count, 0
            )
        grad_heads, pk_grad, pv_grad = attend_back(
            queries, keys, values, grads, prefix_k, prefix_v, turned, total, low, high, columns, row
        )
        prefix_grads.append(jnp.stack([pk_grad, pv_grad]))
        gradient = grad_one
        for step in range(seq_count):
            piece = swap(
                lax.dynamic_slice_in_dim(grad_heads, partner(step) * row_count, row_count, 1), step
            )
            for n in range(3):
                gradient = gradient + back_dot(piece[n], qkv_blocks[:, n, step])

    def everywhere(share):
        stride = 1
        while stride < dp_count:
            share = share + lax.ppermute(share, "dp", [(i, i ^ stride) for i in range(dp_count)])
            stride *= 2
        return lax.all_gather(share, "seq", axis=2, tiled=True)

    sums = [everywhere(item) for item in prefix_grads[::-1]]
    key_stack = jnp.stack([item[0] for item in sums])
    value_stack = jnp.stack([item[1] for item in sums])
    return (current[None], gradient.astype(jnp.bfloat16)[None], key_stack, value_stack)


def solution(mesh):
    in_specs = (
        P("dp", "seq", None),
        P("dp", "seq", None),
        P("dp", None),
        P(None, "dp", None),
        P(),
        P(None, "dp", None),
        P(),
        P(None, "dp", None),
        P(),
        P(None, "dp", None),
        P(),
        P(),
        P(),
        P(),
        P(),
    )
    out_specs = (P("dp", "seq", None), P("dp", "seq", None), P(), P())
    return jax.shard_map(
        functools.partial(local, mesh.shape["dp"], mesh.shape["seq"]),
        mesh=mesh,
        in_specs=in_specs,
        out_specs=out_specs,
        check_vma=False,
    )
```

time: 1330 us -> 1060 us (0.80)
  matrix products: 558 us -> 161 us
  Pallas kernels: 0 us -> 311 us
  waiting for transfers between devices: 524 us -> 402 us
  other arithmetic: 77 us -> 11.1 us
  starting transfers between devices: 0.86 us -> 37.3 us
  local copies, waits for them, and re-layouts: 109 us -> 77 us
    dot_general x32 -> x12, matrix products: 485 us -> 60 us  [dot(): return jnp.dot(left, right, preferred_element_type=jnp.float32)]
    pallas_call x0 -> x4, Pallas kernels: none -> 311 us  [the longest x2 158 us: attend(): pl.pallas_call(functools.partial(forward_kernel, step_heads), grid_spec=p...]
    all_gather x16 -> x10, waiting for transfers between devices: 481 us -> 263 us  [the longest x8 263 us: spread(): return lax.all_gather(piece, ('dp', 'seq'), axis=0, tiled=True)]
    ppermute x0 -> x30, waiting for transfers between devices: none -> 139 us  [the longest x24 124 us: swap(): return lax.ppermute(value, 'seq', [(i, i ^ step) for i in range(seq_count)])]
    reduce_sum x15 -> x7, other arithmetic: 61.8 us -> 3.39 us  [the longest x1 1.83 us: normalize_back(): first = jnp.mean(scaled, -1, keepdims=True)]
    psum x1 -> x0, waiting for transfers between devices: 38.3 us -> none  [local(): lax.psum((grad_prefix_key, grad_prefix_value), ('dp', 'seq'))]
    ppermute x0 -> x30, starting transfers between devices: none -> 36.9 us  [the longest x24 29.7 us: swap(): return lax.ppermute(value, 'seq', [(i, i ^ step) for i in range(seq_count)])]
    all_gather x8 -> x2, local copies, waits for them, and re-layouts: 52.7 us -> 17.3 us  [spread(): return lax.all_gather(piece, ('dp', 'seq'), axis=0, tiled=True)]
  transfers between devices with their start and end apart: 17 -> 40, of which waited for: 10 -> 22; matrix products, arithmetic and copies ran while one was open for 49% -> 17% of each run, Pallas kernels for 0% -> 15%
where the time goes in v2:
time: 1060 us; the launch traced here: 1050 us
  waiting for transfers between devices  402 us (38%)
  Pallas kernels  311 us (29%)
  matrix products  161 us (15%)
  local copies, waits for them, and re-layouts  77 us (7%)
  starting transfers between devices  37.3 us (4%)
  blocking collectives  37.3 us (4%)
  between operations  15.7 us (1%)
  other arithmetic  11.1 us (1%)
    all_gather x8, waiting for transfers between devices, spread(): return lax.all_gather(piece, ('dp', 'seq'), axis=0, tiled=True)  263 us
    pallas_call x2, Pallas kernels, attend(): pl.pallas_call(functools.partial(forward_kernel, step_heads), grid_spec=p...  158 us
    pallas_call x2, Pallas kernels, attend_back(): pl.pallas_call(functools.partial(backward_kernel, step_heads), grid_spec=...  153 us
    ppermute x24, waiting for transfers between devices, swap(): return lax.ppermute(value, 'seq', [(i, i ^ step) for i in range(seq_count)])  124 us
    dot_general x28, matrix products, back_dot(): lax.dot_general(left, right, (((1,), (1,)), ((), ())), preferred_element_...  101 us
    dot_general x12, matrix products, dot(): return jnp.dot(left, right, preferred_element_type=jnp.float32)  60 us
    all_gather x2, blocking collectives, everywhere(): return lax.all_gather(share, 'seq', axis=2, tiled=True)  37.3 us
    ppermute x24, starting transfers between devices, swap(): return lax.ppermute(value, 'seq', [(i, i ^ step) for i in range(seq_count)])  29.7 us
  transfers between devices with their start and end apart: 40, of which 22 were waited for; matrix products, arithmetic and copies ran while one was open for 17% of the time, Pallas kernels for 15%

profile of v2, /device:TPU:0, one launch (start us, length us, event | category | flops | bytes accessed | tf_op | source)
XLA Modules:
  0.0 1052.8 jit_solution(17117493955186901076)
XLA Ops:
  36.4 12.2 %collective-permute-done = bf16[512,1024]{1,0:T(8,128)(2,1)} collective-permute-done((bf16[512,1024]{1,0:T(8,128)(2,1)}, bf16[512,1024]{1,0:T(8,128)(2,1)}, u32[]{:S(2)}, u32[]{:S(2)}) %collective-permute-start) | collective-permute-done | bytes 1048608 | tf_op jit(solution)/shard_map/ppermute | solution.py:369
  50.9 20.4 %collective-permute-done.1 = bf16[512,1024]{1,0:T(8,128)(2,1)} collective-permute-done((bf16[512,1024]{1,0:T(8,128)(2,1)}, bf16[512,1024]{1,0:T(8,128)(2,1)}, u32[]{:S(2)}, u32[]{:S(2)}) %collective-permute-start.1) | collective-permute-done | bytes 1048608 | tf_op jit(solution)/shard_map/ppermute | solution.py:369
  81.7 79.0 %attend.2 = (bf16[2048,256]{1,0:T(8,128)(2,1)S(1)}, f32[256,2048]{1,0:T(8,128)}, f32[2,8,2048]{2,1,0:T(8,128)S(1)}) custom-call(s32[8]{0:T(128)S(1)} %and_select_fusion.1.low_ref, s32[8]{0:T(128)S(1)} %and_select_fusion.high_ref, bf16[2048,256]{1,0:T(8,128)(2,1)S(1)} %fusion.34.q_ref, bf16[2048,256]{1,0:T(8,128)(2,1)S(1)} %fusion.35.k_ref, ...), custom_call_target="tpu_custom_call" | custom-call | tf_op jit(solution)/shard_map/attend/pallas_call | solution.py:240
  170.7 5.7 collective-permute-done.4
  181.4 19.5 %all-gather.25.cloned.1.call-done = bf16[1,1024,4096]{2,1,0:T(8,128)(2,1)} async-done(((bf16[1,32,4096]{2,1,0:T(8,128)(2,1)}), bf16[1,1024,4096]{2,1,0:T(8,128)(2,1)}) %all-gather.25.cloned.1.call-update) | async-done | bytes 8388624 | tf_op jit(solution)/shard_map/all_gather | solution.py:377
  200.9 10.3 fusion.14
  211.2 70.1 %all-gather.27.cloned.1.call-done = bf16[1,4096,1024]{2,1,0:T(8,128)(2,1)} async-done(((bf16[1,128,1024]{2,1,0:T(8,128)(2,1)}), bf16[1,4096,1024]{2,1,0:T(8,128)(2,1)}) %all-gather.27.cloned.1.call-update) | async-done | bytes 8388624 | tf_op jit(solution)/shard_map/all_gather | solution.py:377
  281.3 10.0 fusion.195
  300.8 20.6 %collective-permute-done.6 = bf16[512,1024]{1,0:T(8,128)(2,1)} collective-permute-done((bf16[512,1024]{1,0:T(8,128)(2,1)S(1)}, bf16[512,1024]{1,0:T(8,128)(2,1)}, u32[]{:S(2)}, u32[]{:S(2)}) %collective-permute-start.6) | collective-permute-done | bytes 1048608 | tf_op jit(solution)/shard_map/ppermute | solution.py:369
  323.6 21.1 %collective-permute-done.7 = bf16[512,1024]{1,0:T(8,128)(2,1)} collective-permute-done((bf16[512,1024]{1,0:T(8,128)(2,1)S(1)}, bf16[512,1024]{1,0:T(8,128)(2,1)}, u32[]{:S(2)}, u32[]{:S(2)}) %collective-permute-start.7) | collective-permute-done | bytes 1048608 | tf_op jit(solution)/shard_map/ppermute | solution.py:369
  356.1 79.1 %attend.3 = (bf16[2048,256]{1,0:T(8,128)(2,1)S(1)}, f32[256,2048]{1,0:T(8,128)}, f32[2,8,2048]{2,1,0:T(8,128)S(1)}) custom-call(s32[8]{0:T(128)S(1)} %and_select_fusion.1.low_ref, s32[8]{0:T(128)S(1)} %and_select_fusion.high_ref, bf16[2048,256]{1,0:T(8,128)(2,1)S(1)} %fusion.37.q_ref, bf16[2048,256]{1,0:T(8,128)(2,1)S(1)} %fusion.38.k_ref, ...), custom_call_target="tpu_custom_call" | custom-call | tf_op jit(solution)/shard_map/attend/pallas_call | solution.py:240
  441.7 11.1 %collective-permute-done.10 = bf16[512,256]{1,0:T(8,128)(2,1)} collective-permute-done((bf16[512,256]{1,0:T(8,128)(2,1)}, bf16[512,256]{1,0:T(8,128)(2,1)}, u32[]{:S(2)}, u32[]{:S(2)}) %collective-permute-start.10) | collective-permute-done | bytes 262176 | tf_op jit(solution)/shard_map/ppermute | solution.py:369
  452.8 7.8 collective-permute-done.9
  464.9 11.4 %all-gather.31.cloned.1.call-done = bf16[1,1024,4096]{2,1,0:T(8,128)(2,1)} async-done(((bf16[1,32,4096]{2,1,0:T(8,128)(2,1)}), bf16[1,1024,4096]{2,1,0:T(8,128)(2,1)}) %all-gather.31.cloned.1.call-update) | async-done | bytes 8388624 | tf_op jit(solution)/shard_map/all_gather | solution.py:377
  476.3 11.9 %fusion.6 = f32[512,4096]{1,0:T(8,128)} fusion(bf16[1,1024,4096]{2,1,0:T(8,128)(2,1)} %all-gather.31.cloned.1.call-done, f32[512,1024]{1,0:T(8,128)} %copy-done.16, f32[1024]{0:T(1024)} %bitcast.386, f32[1024]{0:T(1024)} %bitcast.383, f32[512]{0:T(512)S(1)} %add_rsqrt_fusion.1, f32[512]{0:T(512)S(1)} %broadcast_multiply_fusion.9), kind=kOutput, calls=%fused_computation.6 | convolution fusion | flops 4297588736 | bytes 18886656 | tf_op jit(solution)/shard_map/dot_general | solution.py:23
  488.3 67.6 %all-gather.33.cloned.1.call-done = bf16[1,4096,1024]{2,1,0:T(8,128)(2,1)} async-done(((bf16[1,128,1024]{2,1,0:T(8,128)(2,1)}), bf16[1,4096,1024]{2,1,0:T(8,128)(2,1)}) %all-gather.33.cloned.1.call-update) | async-done | bytes 8388624 | tf_op jit(solution)/shard_map/all_gather | solution.py:377
  555.8 10.0 fusion.197
  570.9 24.2 %fusion.177 = (f32[512]{0:T(512)}, f32[512]{0:T(512)}, f32[512,1024]{1,0:T(8,128)}) fusion(f32[512]{0:T(512)} %copy-done.47, f32[512,1024]{1,0:T(8,128)} %copy-done.16, f32[512]{0:T(512)S(1)} %broadcast_multiply_fusion.9, f32[1024]{0:T(1024)} %bitcast.385, bf16[1,1024,4096]{2,1,0:T(8,128)(2,1)} %all-gather.31.cloned.1.call-done, ...), kind=kOutput, calls=%fused_computation.338 | convolution fusion | flops 8629780480 | bytes 32546816 | tf_op jit(solution)/shard_map/dot_general | solution.py:27
  606.3 30.5 %all-gather.35.cloned.1.call-done = bf16[1,1024,3072]{2,1,0:T(8,128)(2,1)} async-done(((bf16[1,32,3072]{2,1,0:T(8,128)(2,1)}), bf16[1,1024,3072]{2,1,0:T(8,128)(2,1)}) %all-gather.35.cloned.1.call-update) | async-done | bytes 6291472 | tf_op jit(solution)/shard_map/all_gather | solution.py:377
  636.9 8.6 copy.66
  645.5 63.6 %all-gather.37.cloned.1.call-done = bf16[1,1024,3072]{2,1,0:T(8,128)(2,1)} async-done(((bf16[1,32,3072]{2,1,0:T(8,128)(2,1)}), bf16[1,1024,3072]{2,1,0:T(8,128)(2,1)}) %all-gather.37.cloned.1.call-update) | async-done | bytes 6291472 | tf_op jit(solution)/shard_map/all_gather | solution.py:377
  709.1 8.7 copy.80
  723.0 76.5 %attend_back.2 = (bf16[3,2048,256]{2,1,0:T(8,128)(2,1)}, f32[64,256]{1,0:T(8,128)S(1)}, f32[64,256]{1,0:T(8,128)S(1)}) custom-call(s32[8]{0:T(128)S(1)} %and_select_fusion.1.low_ref, s32[8]{0:T(128)S(1)} %and_select_fusion.high_ref, bf16[2048,256]{1,0:T(8,128)(2,1)S(1)} %copy-done.7, bf16[2048,256]{1,0:T(8,128)(2,1)S(1)} %fusion.38.k_ref, ...), custom_call_target="tpu_custom_call" | custom-call | tf_op jit(solution)/shard_map/attend_back/pallas_call | solution.py:281
  815.7 5.6 collective-permute-done.29
  825.7 13.3 %collective-permute-done.16 = bf16[3,512,256]{2,1,0:T(8,128)(2,1)S(1)} collective-permute-done((bf16[3,512,256]{2,1,0:T(8,128)(2,1)S(1)}, bf16[3,512,256]{2,1,0:T(8,128)(2,1)S(1)}, u32[]{:S(2)}, u32[]{:S(2)}) %collective-permute-start.16) | collective-permute-done | bytes 786464 | tf_op jit(solution)/shard_map/ppermute | solution.py:369
  848.2 8.1 fusion.176
  856.4 22.6 %fusion.175 = (f32[512]{0:T(512)S(1)}, f32[512]{0:T(512)S(1)}, f32[512,1024]{1,0:T(8,128)}) fusion(f32[512]{0:T(512)S(1)} %add_rsqrt_fusion.3, f32[512,1024]{1,0:T(8,128)} %copy-done.14, f32[512]{0:T(512)S(1)} %broadcast_multiply_fusion.11, f32[1024]{0:T(1024)S(1)} %bitcast.382, bf16[1,1024,4096]{2,1,0:T(8,128)(2,1)} %all-gather.25.cloned.1.call-done, ...), kind=kOutput, calls=%fused_computation.336 | convolution fusion | flops 8627683328 | bytes 33591296 | tf_op jit(solution)/shard_map/dot_general | solution.py:27
  884.2 12.2 %all_gather.47 = f32[2,64,1024]{2,1,0:T(8,128)S(1)} all-gather(f32[2,64,256]{2,1,0:T(8,128)S(1)} %add.538), channel_id=1, replica_groups=mesh['dp'=8,'seq'=4] {'seq'}, dimensions={2}, use_global_device_ids=true | all-gather | bytes 655360 | tf_op jit(solution)/shard_map/all_gather | solution.py:509
  899.4 6.2 collective-permute-done.19
  905.7 76.2 %attend_back.3 = (bf16[3,2048,256]{2,1,0:T(8,128)(2,1)}, f32[64,256]{1,0:T(8,128)S(1)}, f32[64,256]{1,0:T(8,128)S(1)}) custom-call(s32[8]{0:T(128)S(1)} %and_select_fusion.1.low_ref, s32[8]{0:T(128)S(1)} %and_select_fusion.high_ref, bf16[2048,256]{1,0:T(8,128)(2,1)S(1)} %copy-done.5, bf16[2048,256]{1,0:T(8,128)(2,1)S(1)} %copy-done.1, ...), custom_call_target="tpu_custom_call" | custom-call | tf_op jit(solution)/shard_map/attend_back/pallas_call | solution.py:281
  1001.8 25.1 %all_gather.46 = f32[2,64,1024]{2,1,0:T(8,128)S(1)} all-gather(f32[2,64,256]{2,1,0:T(8,128)S(1)} %add.535), channel_id=1, replica_groups=mesh['dp'=8,'seq'=4] {'seq'}, dimensions={2}, use_global_device_ids=true | all-gather | bytes 655360 | tf_op jit(solution)/shard_map/all_gather | solution.py:509
  1039.0 6.5 fusion.111
  (356 shorter events, 181.3 us)
Async XLA Ops:
  7.2 67.4 %all-gather.19.cloned.1.call-start = ((), (), s32[]{:S(2)}) async-start(), calls=%async_computation | async-start | bytes 1769472 | tf_op jit(solution)/shard_map/all_gather | solution.py:412
  9.9 154.8 %all-gather.23.cloned.1.call-start = ((), (), s32[]{:S(2)}) async-start(), calls=%async_computation.2 | async-start | bytes 2162688 | tf_op jit(solution)/shard_map/all_gather | solution.py:377
  10.7 190.2 %all-gather.25.cloned.1.call-start = ((), (), s32[]{:S(2)}) async-start(), calls=%async_computation.3 | async-start | bytes 8650752 | tf_op jit(solution)/shard_map/all_gather | solution.py:377
  13.2 268.2 %all-gather.27.cloned.1.call-start = ((), (), s32[]{:S(2)}) async-start(), calls=%async_computation.4 | async-start | bytes 8650752 | tf_op jit(solution)/shard_map/all_gather | solution.py:377
  16.7 332.7 %all-gather.21.cloned.1.call-start = ((), (), s32[]{:S(2)}) async-start(), calls=%async_computation.1 | async-start | bytes 1769472 | tf_op jit(solution)/shard_map/all_gather | solution.py:412
  17.8 421.9 %all-gather.29.cloned.1.call-start = ((), (), s32[]{:S(2)}) async-start(), calls=%async_computation.5 | async-start | bytes 2162688 | tf_op jit(solution)/shard_map/all_gather | solution.py:377
  18.5 457.8 %all-gather.31.cloned.1.call-start = ((), (), s32[]{:S(2)}) async-start(), calls=%async_computation.6 | async-start | bytes 8650752 | tf_op jit(solution)/shard_map/all_gather | solution.py:377
  19.4 536.4 %all-gather.33.cloned.1.call-start = ((), (), s32[]{:S(2)}) async-start(), calls=%async_computation.7 | async-start | bytes 8650752 | tf_op jit(solution)/shard_map/all_gather | solution.py:377
  21.2 615.6 %all-gather.35.cloned.1.call-start = ((), (), s32[]{:S(2)}) async-start(), calls=%async_computation.8 | async-start | bytes 6488064 | tf_op jit(solution)/shard_map/all_gather | solution.py:377
  21.3 27.3 %collective-permute-start = (bf16[512,1024]{1,0:T(8,128)(2,1)}, bf16[512,1024]{1,0:T(8,128)(2,1)}, u32[]{:S(2)}, u32[]{:S(2)}) collective-permute-start(bf16[512,1024]{1,0:T(8,128)(2,1)} %bitcast.361), channel_id=1, source_target_pairs={{0,1},{1,0},{2,3},{3,2},{4,5},{5,4},{6,7},{7,6},{8,9},{9,8},{10,11... | collective-permute-start | bytes 3145736 | tf_op jit(solution)/shard_map/ppermute | solution.py:369
  24.3 47.0 %collective-permute-start.1 = (bf16[512,1024]{1,0:T(8,128)(2,1)}, bf16[512,1024]{1,0:T(8,128)(2,1)}, u32[]{:S(2)}, u32[]{:S(2)}) collective-permute-start(bf16[512,1024]{1,0:T(8,128)(2,1)} %bitcast.362), channel_id=1, source_target_pairs={{0,2},{1,3},{2,0},{3,1},{4,6},{5,7},{6,4},{7,5},{8,10},{9,11},{10,... | collective-permute-start | bytes 3145736 | tf_op jit(solution)/shard_map/ppermute | solution.py:369
  25.8 47.7 %collective-permute-start.2 = (bf16[512,1024]{1,0:T(8,128)(2,1)}, bf16[512,1024]{1,0:T(8,128)(2,1)S(1)}, u32[]{:S(2)}, u32[]{:S(2)}) collective-permute-start(bf16[512,1024]{1,0:T(8,128)(2,1)} %bitcast.363), channel_id=1, source_target_pairs={{0,3},{1,2},{2,1},{3,0},{4,7},{5,6},{6,5},{7,4},{8,11},{9,10},{10,... | collective-permute-start | bytes 3145736 | tf_op jit(solution)/shard_map/ppermute | solution.py:369
  27.1 682.0 %all-gather.37.cloned.1.call-start = ((), (), s32[]{:S(2)}) async-start(), calls=%async_computation.9 | async-start | bytes 6488064 | tf_op jit(solution)/shard_map/all_gather | solution.py:377
  160.7 10.0 collective-permute-start.3
  160.8 15.6 %collective-permute-start.4 = (bf16[512,256]{1,0:T(8,128)(2,1)S(1)}, bf16[512,256]{1,0:T(8,128)(2,1)S(1)}, u32[]{:S(2)}, u32[]{:S(2)}) collective-permute-start(bf16[512,256]{1,0:T(8,128)(2,1)S(1)} %get-tuple-element.75), channel_id=1, source_target_pairs={{0,2},{1,3},{2,0},{3,1},{4,6},{5,7},{6,4},{7,5},{8,10},{9,11},{10,... | collective-permute-start | bytes 786440 | tf_op jit(solution)/shard_map/ppermute | solution.py:369
  163.3 14.5 %collective-permute-start.5 = (bf16[512,256]{1,0:T(8,128)(2,1)S(1)}, bf16[512,256]{1,0:T(8,128)(2,1)S(1)}, u32[]{:S(2)}, u32[]{:S(2)}) collective-permute-start(bf16[512,256]{1,0:T(8,128)(2,1)S(1)} %get-tuple-element.74), channel_id=1, source_target_pairs={{0,3},{1,2},{2,1},{3,0},{4,7},{5,6},{6,5},{7,4},{8,11},{9,10},{10,... | collective-permute-start | bytes 786440 | tf_op jit(solution)/shard_map/ppermute | solution.py:369
  295.3 26.1 %collective-permute-start.6 = (bf16[512,1024]{1,0:T(8,128)(2,1)S(1)}, bf16[512,1024]{1,0:T(8,128)(2,1)}, u32[]{:S(2)}, u32[]{:S(2)}) collective-permute-start(bf16[512,1024]{1,0:T(8,128)(2,1)S(1)} %get-tuple-element.39), channel_id=1, source_target_pairs={{0,1},{1,0},{2,3},{3,2},{4,5},{5,4},{6,7},{7,6},{8,9},{9,8},{10,11... | collective-permute-start | bytes 3145736 | tf_op jit(solution)/shard_map/ppermute | solution.py:369
  296.7 48.1 %collective-permute-start.7 = (bf16[512,1024]{1,0:T(8,128)(2,1)S(1)}, bf16[512,1024]{1,0:T(8,128)(2,1)}, u32[]{:S(2)}, u32[]{:S(2)}) collective-permute-start(bf16[512,1024]{1,0:T(8,128)(2,1)S(1)} %get-tuple-element.39), channel_id=1, source_target_pairs={{0,2},{1,3},{2,0},{3,1},{4,6},{5,7},{6,4},{7,5},{8,10},{9,11},{10,... | collective-permute-start | bytes 3145736 | tf_op jit(solution)/shard_map/ppermute | solution.py:369
  297.3 49.8 %collective-permute-start.8 = (bf16[512,1024]{1,0:T(8,128)(2,1)S(1)}, bf16[512,1024]{1,0:T(8,128)(2,1)}, u32[]{:S(2)}, u32[]{:S(2)}) collective-permute-start(bf16[512,1024]{1,0:T(8,128)(2,1)S(1)} %get-tuple-element.39), channel_id=1, source_target_pairs={{0,3},{1,2},{2,1},{3,0},{4,7},{5,6},{6,5},{7,4},{8,11},{9,10},{10,... | collective-permute-start | bytes 3145736 | tf_op jit(solution)/shard_map/ppermute | solution.py:369
  436.2 16.6 %collective-permute-start.10 = (bf16[512,256]{1,0:T(8,128)(2,1)}, bf16[512,256]{1,0:T(8,128)(2,1)}, u32[]{:S(2)}, u32[]{:S(2)}) collective-permute-start(bf16[512,256]{1,0:T(8,128)(2,1)} %get-tuple-element.71), channel_id=1, source_target_pairs={{0,2},{1,3},{2,0},{3,1},{4,6},{5,7},{6,4},{7,5},{8,10},{9,11},{10,... | collective-permute-start | bytes 786440 | tf_op jit(solution)/shard_map/ppermute | solution.py:369
  436.8 16.1 %collective-permute-start.11 = (bf16[512,256]{1,0:T(8,128)(2,1)}, bf16[512,256]{1,0:T(8,128)(2,1)}, u32[]{:S(2)}, u32[]{:S(2)}) collective-permute-start(bf16[512,256]{1,0:T(8,128)(2,1)} %get-tuple-element.70), channel_id=1, source_target_pairs={{0,3},{1,2},{2,1},{3,0},{4,7},{5,6},{6,5},{7,4},{8,11},{9,10},{10,... | collective-permute-start | bytes 786440 | tf_op jit(solution)/shard_map/ppermute | solution.py:369
  437.7 23.0 %collective-permute-start.9 = (bf16[512,256]{1,0:T(8,128)(2,1)}, bf16[512,256]{1,0:T(8,128)(2,1)}, u32[]{:S(2)}, u32[]{:S(2)}) collective-permute-start(bf16[512,256]{1,0:T(8,128)(2,1)} %get-tuple-element.72), channel_id=1, source_target_pairs={{0,1},{1,0},{2,3},{3,2},{4,5},{5,4},{6,7},{7,6},{8,9},{9,8},{10,11... | collective-permute-start | bytes 786440 | tf_op jit(solution)/shard_map/ppermute | solution.py:369
  602.8 114.9 %collective-permute-start.12 = (bf16[512,256]{1,0:T(8,128)(2,1)}, bf16[512,256]{1,0:T(8,128)(2,1)}, u32[]{:S(2)}, u32[]{:S(2)}) collective-permute-start(bf16[512,256]{1,0:T(8,128)(2,1)} %get-tuple-element.67), channel_id=1, source_target_pairs={{0,1},{1,0},{2,3},{3,2},{4,5},{5,4},{6,7},{7,6},{8,9},{9,8},{10,11... | collective-permute-start | bytes 786440 | tf_op jit(solution)/shard_map/ppermute | solution.py:369
  604.3 115.3 %collective-permute-start.13 = (bf16[512,256]{1,0:T(8,128)(2,1)}, bf16[512,256]{1,0:T(8,128)(2,1)}, u32[]{:S(2)}, u32[]{:S(2)}) collective-permute-start(bf16[512,256]{1,0:T(8,128)(2,1)} %get-tuple-element.66), channel_id=1, source_target_pairs={{0,2},{1,3},{2,0},{3,1},{4,6},{5,7},{6,4},{7,5},{8,10},{9,11},{10,... | collective-permute-start | bytes 786440 | tf_op jit(solution)/shard_map/ppermute | solution.py:369
  604.9 116.3 %collective-permute-start.14 = (bf16[512,256]{1,0:T(8,128)(2,1)}, bf16[512,256]{1,0:T(8,128)(2,1)}, u32[]{:S(2)}, u32[]{:S(2)}) collective-permute-start(bf16[512,256]{1,0:T(8,128)(2,1)} %get-tuple-element.65), channel_id=1, source_target_pairs={{0,3},{1,2},{2,1},{3,0},{4,7},{5,6},{6,5},{7,4},{8,11},{9,10},{10,... | collective-permute-start | bytes 786440 | tf_op jit(solution)/shard_map/ppermute | solution.py:369
  801.3 20.5 %collective-permute-start.15 = (bf16[3,512,256]{2,1,0:T(8,128)(2,1)S(1)}, bf16[3,512,256]{2,1,0:T(8,128)(2,1)S(1)}, u32[]{:S(2)}, u32[]{:S(2)}) collective-permute-start(bf16[3,512,256]{2,1,0:T(8,128)(2,1)S(1)} %get-tuple-element.43), channel_id=1, source_target_pairs={{0,1},{1,0},{2,3},{3,2},{4,5},{5,4},{6,7},{7,6},{8,9},{9,8},{10,11... | collective-permute-start | bytes 2359304 | tf_op jit(solution)/shard_map/ppermute | solution.py:369
  802.8 36.2 %collective-permute-start.16 = (bf16[3,512,256]{2,1,0:T(8,128)(2,1)S(1)}, bf16[3,512,256]{2,1,0:T(8,128)(2,1)S(1)}, u32[]{:S(2)}, u32[]{:S(2)}) collective-permute-start(bf16[3,512,256]{2,1,0:T(8,128)(2,1)S(1)} %get-tuple-element.45), channel_id=1, source_target_pairs={{0,2},{1,3},{2,0},{3,1},{4,6},{5,7},{6,4},{7,5},{8,10},{9,11},{10,... | collective-permute-start | bytes 2359304 | tf_op jit(solution)/shard_map/ppermute | solution.py:369
  803.4 40.8 %collective-permute-start.17 = (bf16[3,512,256]{2,1,0:T(8,128)(2,1)S(1)}, bf16[3,512,256]{2,1,0:T(8,128)(2,1)S(1)}, u32[]{:S(2)}, u32[]{:S(2)}) collective-permute-start(bf16[3,512,256]{2,1,0:T(8,128)(2,1)S(1)} %get-tuple-element.44), channel_id=1, source_target_pairs={{0,3},{1,2},{2,1},{3,0},{4,7},{5,6},{6,5},{7,4},{8,11},{9,10},{10,... | collective-permute-start | bytes 2359304 | tf_op jit(solution)/shard_map/ppermute | solution.py:369
  883.5 15.8 %collective-permute-start.18 = (bf16[512,256]{1,0:T(8,128)(2,1)S(1)}, bf16[512,256]{1,0:T(8,128)(2,1)S(1)}, u32[]{:S(2)}, u32[]{:S(2)}) collective-permute-start(bf16[512,256]{1,0:T(8,128)(2,1)S(1)} %get-tuple-element.63), channel_id=1, source_target_pairs={{0,1},{1,0},{2,3},{3,2},{4,5},{5,4},{6,7},{7,6},{8,9},{9,8},{10,11... | collective-permute-start | bytes 786440 | tf_op jit(solution)/shard_map/ppermute | solution.py:369
  983.7 44.9 %collective-permute-start.21 = (bf16[3,512,256]{2,1,0:T(8,128)(2,1)S(1)}, bf16[3,512,256]{2,1,0:T(8,128)(2,1)S(1)}, u32[]{:S(2)}, u32[]{:S(2)}) collective-permute-start(bf16[3,512,256]{2,1,0:T(8,128)(2,1)S(1)} %get-tuple-element.40), channel_id=1, source_target_pairs={{0,1},{1,0},{2,3},{3,2},{4,5},{5,4},{6,7},{7,6},{8,9},{9,8},{10,11... | collective-permute-start | bytes 2359304 | tf_op jit(solution)/shard_map/ppermute | solution.py:369
  985.3 44.7 %collective-permute-start.22 = (bf16[3,512,256]{2,1,0:T(8,128)(2,1)S(1)}, bf16[3,512,256]{2,1,0:T(8,128)(2,1)S(1)}, u32[]{:S(2)}, u32[]{:S(2)}) collective-permute-start(bf16[3,512,256]{2,1,0:T(8,128)(2,1)S(1)} %get-tuple-element.42), channel_id=1, source_target_pairs={{0,2},{1,3},{2,0},{3,1},{4,6},{5,7},{6,4},{7,5},{8,10},{9,11},{10,... | collective-permute-start | bytes 2359304 | tf_op jit(solution)/shard_map/ppermute | solution.py:369
  985.8 49.4 %collective-permute-start.23 = (bf16[3,512,256]{2,1,0:T(8,128)(2,1)S(1)}, bf16[3,512,256]{2,1,0:T(8,128)(2,1)S(1)}, u32[]{:S(2)}, u32[]{:S(2)}) collective-permute-start(bf16[3,512,256]{2,1,0:T(8,128)(2,1)S(1)} %get-tuple-element.41), channel_id=1, source_target_pairs={{0,3},{1,2},{2,1},{3,0},{4,7},{5,6},{6,5},{7,4},{8,11},{9,10},{10,... | collective-permute-start | bytes 2359304 | tf_op jit(solution)/shard_map/ppermute | solution.py:369
  (80 other events, 1649.9 us)
Sparse Core Ops, SparseCore 0:
  10.0 29.8 all-gather.18
  42.8 73.7 all-gather.22
  119.5 81.3 all-gather.24
  203.6 77.6 all-gather.26
  282.8 25.7 all-gather.20
  311.3 76.2 all-gather.28
  391.0 85.2 all-gather.30
  479.8 76.0 all-gather.32
  558.7 78.0 all-gather.34
  639.6 69.4 all-gather.36

commit v3 on v0

v3 whole, which is shorter than its diff:
```python
import functools
import math

import jax
import jax.numpy as jnp
from jax import lax
from jax.experimental import pallas as pl
from jax.experimental.pallas import tpu as pltpu
from jax.sharding import PartitionSpec as P

HEAD = 64

SCALE = 0.125
LOG2_E = math.log2(math.e)
LN_2 = math.log(2.0)
EPS = 1e-05
BLOCK = 256
VMEM_BYTES = 56 * 2**20
FLOPS_A_MICRO = 1.1e9


def dot(left, right):
    return jnp.dot(left, right, preferred_element_type=jnp.float32)


def back_dot(left, right):
    return lax.dot_general(
        left, right, (((1,), (1,)), ((), ())), preferred_element_type=jnp.float32
    )


def normalize(values):
    center = jnp.mean(values, -1, keepdims=True)
    centered = values - center
    spread = jnp.mean(centered * centered, -1, keepdims=True)
    inverse = lax.rsqrt(spread + EPS)
    return centered * inverse, inverse


def normalize_back(gradient, normal, inverse, gain_row):
    scaled = gradient * gain_row
    first = jnp.mean(scaled, -1, keepdims=True)
    second = jnp.mean(scaled * normal, -1, keepdims=True)
    return (scaled - first - normal * second) * inverse


def gelu_pair(inner):
    size = jnp.abs(inner)
    bell = jnp.exp2(inner * inner * (-0.5 * LOG2_E))
    t = 1.0 / (1.0 + (0.3275911 * 0.5**0.5) * size)
    tail = 0.5 * 1.061405429
    for factor in (-1.453152027, 1.421413741, -0.284496736, 0.254829592):
        tail = tail * t + 0.5 * factor
    tail = tail * t * bell
    phi = jnp.where(inner >= 0.0, 1.0 - tail, tail)
    return inner * phi, phi + inner * bell * ((2.0 * math.pi) ** -0.5)


def scalar_call(kernel, name, micros, scalars, operands, out_shapes, scratch, specs=None, outs=None):
    whole = pl.BlockSpec(memory_space=pltpu.VMEM)
    specs = specs or {}
    outs = outs or {}
    return pl.pallas_call(
        kernel,
        grid_spec=pltpu.PrefetchScalarGridSpec(
            num_scalar_prefetch=len(scalars),
            grid=(1,),
            in_specs=[specs.get(at, whole) for at in range(len(operands))],
            out_specs=[outs.get(at, whole) for at in range(len(out_shapes))],
            scratch_shapes=scratch,
        ),
        out_shape=[jax.ShapeDtypeStruct(*item) for item in out_shapes],
        compiler_params=pltpu.CompilerParams(vmem_limit_bytes=VMEM_BYTES),
        cost_estimate=pl.CostEstimate(
            flops=int(micros * FLOPS_A_MICRO), bytes_accessed=0, transcendentals=0
        ),
        name=name,
    )(*scalars, *operands)


def head_of(index):
    return slice(index * HEAD, (index + 1) * HEAD)


def lanes_of(index):
    return slice(index * BLOCK, (index + 1) * BLOCK)


def heads_apart(block, count):
    if count == 1:
        return block
    rows = []
    for h in range(count):
        parts = [jnp.zeros((HEAD, BLOCK), block.dtype)] * count
        parts[h] = block[head_of(h)]
        rows.append(jnp.concatenate(parts, 1))
    return jnp.concatenate(rows, 0)


def same_pair(code_columns, code_row):
    columns = jnp.concatenate([code_columns] * (code_row.shape[1] // code_columns.shape[1]), 1)
    return columns == code_row


def attend_kernel(count, devices, low_ref, high_ref, me_ref, *refs):
    tokens, refs = refs[: 2 * devices], refs[2 * devices :]
    (matrix_ref, bias_ref, pk_ref, pv_ref, columns_ref, row_ref), refs = refs[:6], refs[6:]
    contexts, refs = refs[:devices], refs[devices:]
    turned_ref, total_ref, q_ref, k_ref, v_ref, q_turned, v_turned = refs
    me = me_ref[0]
    width = count * HEAD
    half = tokens[0].shape[0]
    own_rows = 2 * half
    blocks = q_ref.shape[0] // BLOCK
    groups = total_ref.shape[0]
    group_lanes = count // groups * BLOCK
    for at, token_ref in enumerate(tokens):
        device = me ^ (at // 2)
        place = pl.ds(pl.multiple_of(device * own_rows + (at % 2) * half, half), half)
        projected = dot(token_ref[...], matrix_ref[...]) + bias_ref[...]
        queries = projected[:, :width] * (SCALE * LOG2_E)
        q_ref[place, :] = queries.astype(jnp.bfloat16)
        k_ref[place, :] = projected[:, width : 2 * width].astype(jnp.bfloat16)
        v_ref[place, :] = projected[:, 2 * width :].astype(jnp.bfloat16)
    q_turned[...] = q_ref[...].T
    v_turned[...] = v_ref[...].T
    prefix_turned = pv_ref[...].T

    def query_step(i, carry):
        at = pl.ds(pl.multiple_of(i * BLOCK, BLOCK), BLOCK)
        code_row = row_ref[:, at]
        rows = heads_apart(q_turned[:, at], count)

        def weigh(values, weights):
            low_weights = weights.astype(jnp.bfloat16)
            return jnp.concatenate(
                [dot(values[head_of(h)], low_weights[:, lanes_of(h)]) for h in range(count)], 1
            )

        scores = dot(pk_ref[...], rows)
        top = jnp.max(scores, 0, keepdims=True)
        weights = jnp.exp2(scores - top)
        total = jnp.sum(weights, 0, keepdims=True)
        summed = weigh(prefix_turned, weights)

        def key_step(place, state):
            top, total, summed = state
            seen = same_pair(columns_ref[place, :], code_row)
            seen = jnp.concatenate([seen] * count, 1)
            scores = jnp.where(seen, dot(k_ref[place, :], rows), -jnp.inf)
            new_top = jnp.maximum(top, jnp.max(scores, 0, keepdims=True))
            factor = jnp.exp2(top - new_top)
            weights = jnp.exp2(scores - new_top)
            total = total * factor + jnp.sum(weights, 0, keepdims=True)
            summed = summed * factor + weigh(v_turned[:, place], weights)
            return new_top, total, summed

        low, high = low_ref[i], high_ref[i]
        twos = (high - low) // 2

        def two_blocks(j, state):
            start = pl.multiple_of((low + 2 * j) * BLOCK, BLOCK)
            return key_step(pl.ds(start, 2 * BLOCK), state)

        def one_block(j, state):
            return key_step(pl.ds(pl.multiple_of(j * BLOCK, BLOCK), BLOCK), state)

        state = lax.fori_loop(0, twos, two_blocks, (top, total, summed))
        top, total, summed = lax.fori_loop(low + 2 * twos, high, one_block, state)
        logs = top + jnp.log2(total)
        group_place = pl.ds(pl.multiple_of(i * group_lanes, group_lanes), group_lanes)
        for group in range(groups):
            lanes = slice(group * group_lanes, (group + 1) * group_lanes)
            total_ref[group, :, group_place] = logs[:, lanes]
        summed = summed / total
        turned = jnp.concatenate([summed[:, lanes_of(h)] for h in range(count)], 0)
        turned_ref[:, at] = turned
        context = turned.T.astype(jnp.bfloat16)
        share = min(BLOCK, own_rows)
        for part in range(BLOCK // share):
            first = i * BLOCK + part * share
            device, start = first // own_rows, first % own_rows
            for step, context_ref in enumerate(contexts):

                @pl.when(device ^ me == step)
                def _(context_ref=context_ref, start=start, part=part):
                    inside = pl.ds(pl.multiple_of(start, share), share)
                    context_ref[inside, :] = context[part * share : (part + 1) * share]

        return carry

    lax.fori_loop(0, blocks, query_step, 0)


def groups_of(width):
    return max(width // (2 * HEAD), 1)


def attend(low, high, me, tokens, matrix, bias, prefix_k, prefix_v, columns, row):
    devices = len(tokens) // 2
    rows = row.shape[1]
    width = prefix_k.shape[1]
    count = width // HEAD
    groups = groups_of(width)
    own_rows = rows // devices
    results = scalar_call(
        functools.partial(attend_kernel, count, devices),
        "attend",
        40,
        (low, high, me),
        (*tokens, matrix, bias, prefix_k, prefix_v, columns, row),
        [((own_rows, width), jnp.bfloat16)] * devices
        + [
            ((width, rows), jnp.float32),
            ((groups, 1, count // groups * rows), jnp.float32),
        ]
        + [((rows, width), jnp.bfloat16)] * 3,
        [pltpu.VMEM((width, rows), jnp.bfloat16)] * 2,
    )
    return results[:devices], results[devices:]


def attend_back_kernel(count, devices, low_ref, high_ref, me_ref, *refs):
    pieces, refs = refs[:devices], refs[devices:]
    (q_ref, k_ref, v_ref, pk_ref, pv_ref, turned_ref, total_ref, columns_ref, row_ref), refs = (
        refs[:9],
        refs[9:],
    )
    results, refs = refs[:devices], refs[devices:]
    prefix_ref, refs = refs[0], refs[1:]
    (
        g_ref,
        grads_ref,
        q_turned,
        g_turned,
        q_alone,
        g_alone,
        k_turned,
        q_sum,
        delta_ref,
        k_sum,
        v_sum,
        pk_sum,
        pv_sum,
    ) = refs
    me = me_ref[0]
    width = count * HEAD
    blocks = q_ref.shape[0] // BLOCK
    own_rows = pieces[0].shape[0]

    def rows_of(step):
        return pl.ds(pl.multiple_of((me ^ step) * own_rows, own_rows), own_rows)

    for step, piece_ref in enumerate(pieces):
        g_ref[rows_of(step), :] = piece_ref[...]
    k_turned[...] = k_ref[...].T
    prefix_turned = pk_ref[...].T
    q_sum[...] = jnp.zeros_like(q_sum)
    pk_sum[...] = jnp.zeros_like(pk_sum)
    pv_sum[...] = jnp.zeros_like(pv_sum)

    def wide(i):
        return pl.ds(pl.multiple_of(i * count * BLOCK, count * BLOCK), count * BLOCK)

    def query_part(i):
        return pl.ds(pl.multiple_of(i * BLOCK, BLOCK), BLOCK)

    def pair_of_blocks(i, keys, values, keys_turned, seen, key_total, value_total):
        at = query_part(i)
        scores = dot(keys, q_turned[:, wide(i)])
        grad_weights = dot(values, g_turned[:, wide(i)])
        weights = jnp.exp2(scores - total_ref[0, :, wide(i)])
        if seen is not None:
            seen = jnp.concatenate([same_pair(seen, row_ref[:, at])] * count, 1)
            weights = jnp.where(seen, weights, 0.0)
        grad_scores = weights * (grad_weights - delta_ref[:, wide(i)])
        grad_scores = grad_scores.astype(jnp.bfloat16)
        value_total[...] += dot(weights.astype(jnp.bfloat16), g_alone[wide(i), :])
        key_total[...] += dot(grad_scores, q_alone[wide(i), :])
        for h in range(count):
            q_sum[head_of(h), at] += dot(keys_turned[head_of(h)], grad_scores[:, lanes_of(h)])

    def prepare(i, carry):
        at = query_part(i)
        q_block = q_ref[at, :].T
        g_block = g_ref[at, :].T
        delta = g_block.astype(jnp.float32) * turned_ref[:, at]
        delta_ref[:, wide(i)] = jnp.concatenate(
            [jnp.sum(delta[head_of(h)], 0, keepdims=True) for h in range(count)], 1
        )
        q_apart, g_apart = heads_apart(q_block, count), heads_apart(g_block, count)
        q_turned[:, wide(i)] = q_apart
        g_turned[:, wide(i)] = g_apart
        q_alone[wide(i), :] = q_apart.T
        g_alone[wide(i), :] = g_apart.T
        pair_of_blocks(i, pk_ref[...], pv_ref[...], prefix_turned, None, pk_sum, pv_sum)
        return carry

    lax.fori_loop(0, blocks, prepare, 0)
    prefix_ref[0] = pk_sum[...] * LN_2
    prefix_ref[1] = pv_sum[...]

    def key_step(j, carry):
        place = pl.ds(pl.multiple_of(j * 2 * BLOCK, 2 * BLOCK), 2 * BLOCK)
        k_sum[...] = jnp.zeros_like(k_sum)
        v_sum[...] = jnp.zeros_like(v_sum)
        keys = k_ref[place, :]
        values = v_ref[place, :]
        keys_turned = k_turned[:, place]
        seen = columns_ref[place, :]

        def query_step(i, carry):
            pair_of_blocks(i, keys, values, keys_turned, seen, k_sum, v_sum)
            return carry

        lax.fori_loop(low_ref[2 * j], high_ref[2 * j + 1], query_step, 0)
        grads_ref[place, width : 2 * width] = (k_sum[...] * LN_2).astype(jnp.bfloat16)
        grads_ref[place, 2 * width :] = v_sum[...].astype(jnp.bfloat16)
        return carry

    lax.fori_loop(0, blocks // 2, key_step, 0)
    grads_ref[:, :width] = (q_sum[...] * SCALE).T.astype(jnp.bfloat16)
    for step, result_ref in enumerate(results):
        result_ref[...] = grads_ref[rows_of(step), :]


def attend_back(low, high, me, group, pieces, attended, prefix_k, prefix_v, columns, row):
    devices = len(pieces)
    turned, total, queries, keys, values = attended
    own_rows, all_width = pieces[0].shape
    rows, width = own_rows * devices, all_width // groups_of(all_width)
    prefix = prefix_k.shape[0]
    count = width // HEAD
    specs = {
        at: pl.BlockSpec((few, width), lambda t, *_: (0, group))
        for at, few in enumerate([own_rows] * devices + [rows, rows, rows, prefix, prefix])
    }
    specs[devices + 5] = pl.BlockSpec((width, rows), lambda t, *_: (group, 0))
    specs[devices + 6] = pl.BlockSpec((1, 1, total.shape[2]), lambda t, *_: (group, 0, 0))
    results = scalar_call(
        functools.partial(attend_back_kernel, count, devices),
        "attend_back",
        30,
        (low, high, me),
        (*pieces, queries, keys, values, prefix_k, prefix_v, turned, total, columns, row),
        [((rows // devices, 3 * width), jnp.bfloat16)] * devices
        + [((2, prefix, width), jnp.float32)],
        [
            pltpu.VMEM((rows, width), jnp.bfloat16),
            pltpu.VMEM((rows, 3 * width), jnp.bfloat16),
            pltpu.VMEM((width, count * rows), jnp.bfloat16),
            pltpu.VMEM((width, count * rows), jnp.bfloat16),
            pltpu.VMEM((count * rows, width), jnp.bfloat16),
            pltpu.VMEM((count * rows, width), jnp.bfloat16),
            pltpu.VMEM((width, rows), jnp.bfloat16),
            pltpu.VMEM((width, rows), jnp.float32),
            pltpu.VMEM((1, count * rows), jnp.float32),
            pltpu.VMEM((2 * BLOCK, width), jnp.float32),
            pltpu.VMEM((2 * BLOCK, width), jnp.float32),
            pltpu.VMEM((prefix, width), jnp.float32),
            pltpu.VMEM((prefix, width), jnp.float32),
        ],
        specs=specs,
    )
    return results[:devices], results[devices]


def own_block(me, step, size):
    return pl.ds(pl.multiple_of((me ^ step) * size, size), size)


def mix_kernel(devices, me_ref, *refs):
    contexts, refs = refs[:devices], refs[devices:]
    upper_ref, lower_ref, matrix_ref, bias_ref, normal_ref, inverse_ref = refs
    me = me_ref[0]
    width = contexts[0].shape[1]
    tokens = jnp.concatenate([upper_ref[...], lower_ref[...]], 0)
    total = tokens.astype(jnp.float32) + bias_ref[...]
    for step, context_ref in enumerate(contexts):
        total += dot(context_ref[...], matrix_ref[own_block(me, step, width), :])
    normal_ref[...], inverse_ref[...] = normalize(total)


def mix(me, contexts, upper, lower, matrix, bias):
    rows, width = contexts[0].shape[0], upper.shape[1]
    return scalar_call(
        functools.partial(mix_kernel, len(contexts)),
        "mix",
        5,
        (me,),
        (*contexts, upper, lower, matrix, bias),
        [((rows, width), jnp.float32), ((rows, 1), jnp.float32)],
        [],
    )


def copy_in(sources, targets, sems):
    copies = [
        pltpu.make_async_copy(source, target, sems.at[at])
        for at, (source, target) in enumerate(zip(sources, targets, strict=True))
    ]
    for item in copies:
        item.start()
    return copies


def feed_kernel(parts, pieces, me_ref, core_ref, *refs):
    in_refs, back_refs, refs = refs[:parts], refs[parts : 2 * parts], refs[2 * parts :]
    (normal_ref, gain_one, shift_one, bias_in, bias_back, gain_two, shift_two), refs = (
        refs[:7],
        refs[7:],
    )
    outputs, refs = refs[:pieces], refs[pieces:]
    slope_ref, normal_two, inverse_two, held, total, in_held, back_held, slope_held = refs[:8]
    in_sems, back_sems, slope_sems = refs[8:]
    hidden = in_held.shape[2]
    in_copies = copy_in(in_refs, [in_held.at[t] for t in range(parts)], in_sems)
    back_copies = copy_in(back_refs, [back_held.at[t] for t in range(parts)], back_sems)
    normed = normal_ref[...] * gain_one[...] + shift_one[...]
    held[...] = normed.astype(jnp.bfloat16)
    total[...] = normed + bias_back[...]

    def inner_of(t):
        in_copies[t].wait()
        back_copies[t].wait()
        bias = bias_in[(t % 2) ^ core_ref[0], me_ref[0] ^ (t // 2)]
        return dot(held[...], in_held[t]) + bias

    slopes = []
    following = inner_of(0)
    for t in range(parts):
        inner = following
        if t + 1 < parts:
            following = inner_of(t + 1)
        activated, slope = gelu_pair(inner)
        slope_held[t] = slope.astype(jnp.bfloat16)
        target = slope_ref.at[:, t * hidden : (t + 1) * hidden]
        slopes.append(pltpu.make_async_copy(slope_held.at[t], target, slope_sems.at[t]))
        slopes[-1].start()
        total[...] += dot(activated.astype(jnp.bfloat16), back_held[t])
    normal, inverse = normalize(total[...])
    normal_two[...] = normal
    inverse_two[...] = inverse
    result = (normal * gain_two[...] + shift_two[...]).astype(jnp.bfloat16)
    size = result.shape[0] // pieces
    for at, output_ref in enumerate(outputs):
        output_ref[...] = result[at * size : (at + 1) * size]
    for item in slopes:
        item.wait()


def feed(me, core, ins, backs, normal, gain_one, shift_one, bias_in, bias_back, gain_two, shift_two, pieces):
    parts = len(ins)
    rows, width = normal.shape
    hidden = ins[0].shape[1]
    anywhere = pl.BlockSpec(memory_space=pl.ANY)
    results = scalar_call(
        functools.partial(feed_kernel, parts, pieces),
        "feed",
        22,
        (me, core),
        (*ins, *backs, normal, gain_one, shift_one, bias_in, bias_back, gain_two, shift_two),
        [((rows // pieces, width), jnp.bfloat16)] * pieces
        + [
            ((rows, parts * hidden), jnp.bfloat16),
            ((rows, width), jnp.float32),
            ((rows, 1), jnp.float32),
        ],
        [
            pltpu.VMEM((rows, width), jnp.bfloat16),
            pltpu.VMEM((rows, width), jnp.float32),
            pltpu.VMEM((parts, width, hidden), jnp.bfloat16),
            pltpu.VMEM((parts, hidden, width), jnp.bfloat16),
            pltpu.VMEM((parts, rows, hidden), jnp.bfloat16),
            pltpu.SemaphoreType.DMA((parts,)),
            pltpu.SemaphoreType.DMA((parts,)),
            pltpu.SemaphoreType.DMA((parts,)),
        ],
        specs={at: anywhere for at in range(2 * parts)},
        outs={pieces: anywhere},
    )
    return results[:pieces], results[pieces:]


def feed_back_kernel(parts, devices, me_ref, *refs):
    in_refs, back_refs, refs = refs[:parts], refs[parts : 2 * parts], refs[2 * parts :]
    (
        slope_ref,
        normal_one,
        matrix_ref,
        gradient_ref,
        normal_two,
        inverse_two,
        gain_two,
        inverse_one,
        gain_one,
    ), refs = refs[:9], refs[9:]
    grad_one_ref, refs = refs[0], refs[1:]
    results, refs = refs[:-11], refs[-11:]
    held, total, in_held, back_held, slope_held, normal_held, matrix_held = refs[:7]
    in_sems, back_sems, slope_sems, late_sems = refs[7:]
    hidden = in_held.shape[2]
    back_copies = copy_in(back_refs, [back_held.at[t] for t in range(parts)], back_sems)
    slope_copies = copy_in(
        [slope_ref.at[:, t * hidden : (t + 1) * hidden] for t in range(parts)],
        [slope_held.at[t] for t in range(parts)],
        slope_sems,
    )
    in_copies = copy_in(in_refs, [in_held.at[t] for t in range(parts)], in_sems)
    late_copies = copy_in([normal_one, matrix_ref], [normal_held, matrix_held], late_sems)
    gradient = gradient_ref[...].astype(jnp.float32)
    grad_two = normalize_back(gradient, normal_two[...], inverse_two[...], gain_two[...])
    held[...] = grad_two.astype(jnp.bfloat16)
    total[...] = grad_two

    def inner_of(t):
        back_copies[t].wait()
        slope_copies[t].wait()
        in_copies[t].wait()
        return back_dot(held[...], back_held[t])

    following = inner_of(0)
    for t in range(parts):
        inner = following
        if t + 1 < parts:
            following = inner_of(t + 1)
        grad_inner = (inner * slope_held[t].astype(jnp.float32)).astype(jnp.bfloat16)
        total[...] += back_dot(grad_inner, in_held[t])
    for item in late_copies:
        item.wait()
    grad_one = normalize_back(total[...], normal_held[...], inverse_one[...], gain_one[...])
    grad_one_ref[...] = grad_one
    rounded = grad_one.astype(jnp.bfloat16)
    size = results[0].shape[1]
    for step, result_ref in enumerate(results):
        product = back_dot(rounded, matrix_held[own_block(me_ref[0], step, size), :])
        result_ref[...] = product.astype(jnp.bfloat16)


def feed_back(me, devices, ins, backs, gradient, slope, norms, gain_two, gain_one, matrix):
    normal_one, inverse_one, normal_two, inverse_two = norms
    parts = len(ins)
    rows, width = gradient.shape
    hidden = ins[0].shape[1]
    anywhere = pl.BlockSpec(memory_space=pl.ANY)
    results = scalar_call(
        functools.partial(feed_back_kernel, parts, devices),
        "feed_back",
        18,
        (me,),
        (
            *ins,
            *backs,
            slope,
            normal_one,
            matrix,
            gradient,
            normal_two,
            inverse_two,
            gain_two,
            inverse_one,
            gain_one,
        ),
        [((rows, width), jnp.float32)]
        + [((rows, width // devices), jnp.bfloat16)] * devices,
        [
            pltpu.VMEM((rows, width), jnp.bfloat16),
            pltpu.VMEM((rows, width), jnp.float32),
            pltpu.VMEM((parts, width, hidden), jnp.bfloat16),
            pltpu.VMEM((parts, hidden, width), jnp.bfloat16),
            pltpu.VMEM((parts, rows, hidden), jnp.bfloat16),
            pltpu.VMEM(normal_one.shape, normal_one.dtype),
            pltpu.VMEM(matrix.shape, matrix.dtype),
            pltpu.SemaphoreType.DMA((parts,)),
            pltpu.SemaphoreType.DMA((parts,)),
            pltpu.SemaphoreType.DMA((parts,)),
            pltpu.SemaphoreType.DMA((2,)),
        ],
        specs={at: anywhere for at in range(2 * parts + 3)},
    )
    return results[0], results[1:]


def collect_kernel(devices, *refs):
    pieces, (grad_ref, matrix_ref, result_ref) = refs[:devices], refs[devices:]
    total = grad_ref[...]
    width = pieces[0].shape[1]
    for step, piece_ref in enumerate(pieces):
        total += back_dot(piece_ref[...], matrix_ref[:, step * width : (step + 1) * width])
    result_ref[...] = total.astype(result_ref.dtype)


def collect(pieces, grad_one, matrix, dtype):
    return scalar_call(
        functools.partial(collect_kernel, len(pieces)),
        "collect",
        9,
        (),
        (*pieces, grad_one, matrix),
        [(grad_one.shape, dtype)],
        [],
    )[0]


def local(
    dp_count,
    seq_count,
    first_layer_input,
    cotangent,
    lengths,
    w_qkv,
    bias_qkv,
    w_out,
    bias_out,
    w_in,
    bias_in,
    w_back,
    bias_back,
    norm_gain,
    norm_shift,
    prefix_keys,
    prefix_values,
):
    row_count = first_layer_input.shape[1]
    width = first_layer_input.shape[2]
    layer_count = w_qkv.shape[0]
    hidden = w_in.shape[2]
    all_rows = row_count * seq_count
    own_width = width // seq_count
    me = lax.axis_index("seq")
    core = lax.axis_index("dp") % 2
    me_at = me[None].astype(jnp.int32)
    core_at = core[None].astype(jnp.int32)
    bits = [1 << n for n in range(seq_count.bit_length() - 1)]

    def swap(value, step):
        return lax.ppermute(value, "seq", [(i, i ^ step) for i in range(seq_count)])

    def widen(found, order):
        for bit in order:
            found = found | {
                k | bit: swap(item, bit) for k, item in found.items() if k | bit not in found
            }
        return found

    def exchange(value, order):
        found = widen({0: value}, order)
        return [found[k] for k in range(seq_count)]

    def other_core(value):
        return lax.ppermute(value, "dp", [(i, i ^ 1) for i in range(dp_count)])

    def gather(value):
        return lax.all_gather(value, "dp", axis=0, tiled=True)

    def own_columns(values, axis):
        return lax.dynamic_slice_in_dim(values, me * own_width, own_width, axis)

    pair_at = jnp.arange(lengths.shape[1], dtype=jnp.int32)
    ends = jnp.sum(
        jnp.where(pair_at[:, None] <= pair_at[None, :], lengths[0][:, None], 0), 0, dtype=jnp.int32
    )
    starts = ends - lengths[0]
    places = jnp.arange(all_rows, dtype=jnp.int32)
    codes = jnp.sum((places[:, None] >= ends[None, :]).astype(jnp.int32), 1, dtype=jnp.int32)
    columns = jnp.broadcast_to(codes[:, None], (all_rows, 128))
    row = codes[None, :]
    first = jnp.arange(all_rows // BLOCK, dtype=jnp.int32) * BLOCK
    after = first + BLOCK
    low = jnp.max(jnp.where(starts[None, :] <= first[:, None], starts[None, :], 0), 1) // BLOCK
    high = jnp.min(jnp.where(ends[None, :] >= after[:, None], ends[None, :], all_rows), 1)
    high = (high + BLOCK - 1) // BLOCK

    groups = groups_of(own_width)
    half_rows = row_count // 2
    upper, lower = first_layer_input[0, :half_rows], first_layer_input[0, half_rows:]
    first_tokens = exchange(upper, bits), exchange(lower, bits[::-1])

    share = hidden // dp_count // seq_count

    def after(value, *others):
        return lax.optimization_barrier((value, *others))[0]

    def own_qkv(matrix):
        shard = matrix.reshape(-1, 3, seq_count, own_width)
        return lax.dynamic_slice_in_dim(shard, me, 1, 2).reshape(-1, 3 * own_width)

    def all_qkv(matrix):
        shard = matrix.reshape(-1, 3, seq_count, groups, own_width // groups)
        shard = jnp.transpose(shard, (2, 0, 3, 1, 4))
        blocks = [lax.dynamic_slice_in_dim(shard, me ^ step, 1, 0)[0] for step in range(seq_count)]
        return jnp.concatenate([block.reshape(-1, 3 * own_width) for block in blocks], 1)

    def hidden_share(into, back):
        into = into.reshape(-1, dp_count, seq_count, share)
        into = lax.dynamic_slice_in_dim(into, me, 1, 2).reshape(-1, dp_count * share)
        back = lax.dynamic_slice_in_dim(back, me * share, share, 0).reshape(into.shape)
        both = lax.all_gather(jnp.stack([into, back]), "dp")
        into = both[:, 0].reshape(width, dp_count * share)
        back = both[:, 1].reshape(dp_count * share, width)
        return into, back

    def hidden_first(into, back, both):
        half = dp_count * share // 2
        ins, backs = (
            [
                lax.dynamic_slice_in_dim(item, side * half, half, axis)
                for side in (core, 1 - core)
            ]
            for item, axis in ((into, 1), (back, 0))
        )
        in_found, back_found = {0: ins[0]}, {0: backs[0]}
        for bit in bits if both else bits[:1]:
            in_found[bit] = swap(ins[0], bit)
        for bit in bits if both else bits[-1:]:
            back_found[bit] = swap(backs[0], bit)
        return ins[1], backs[1], in_found, back_found

    def hidden_rest(in_other, back_other, in_found, back_found):
        return in_other, back_other, widen(in_found, bits), widen(back_found, bits[::-1])

    def hidden_all(in_other, back_other, in_found, back_found):
        ins, backs = [in_found[0], in_other], [back_found[0], back_other]
        for step in range(1, seq_count):
            ins += [in_found[step], other_core(in_found[step])]
            backs += [back_found[step], other_core(back_found[step])]
        return ins, backs

    def row_of(values):
        return values.astype(jnp.float32)[None, :]

    def over_dp_swap(value, bit):
        return lax.ppermute(value, "dp", [(i, i ^ bit) for i in range(dp_count)])

    saved = []
    tokens = first_tokens
    mat_own = [gather(own_qkv(w_qkv[0]))]
    came = [mat_own[0]] + [found[bit] for found in first_tokens for bit in bits]
    shares = [hidden_share(*after((w_in[0], w_back[0]), came))]
    mat_outs = [gather(after(w_out[0], came))]
    for layer in range(1, layer_count):
        shares.append(hidden_share(*after((w_in[layer], w_back[layer]), came)))
        mat_own.append(gather(own_qkv(after(w_qkv[layer], came))))
        mat_outs.append(gather(after(w_out[layer], came)))
    parts = hidden_first(*shares[0], True)
    for layer in range(layer_count):
        last = layer + 1 == layer_count
        bias_own = own_columns(bias_qkv[layer].reshape(3, width).astype(jnp.float32), 1)
        bias_own = bias_own.reshape(1, 3 * own_width)
        prefix_k = own_columns(prefix_keys[layer], 1)
        prefix_v = own_columns(prefix_values[layer], 1)
        bias_hidden = bias_in[layer].astype(jnp.float32).reshape(2, dp_count // 2, seq_count, share)
        bias_hidden = jnp.transpose(bias_hidden, (0, 2, 1, 3)).reshape(2, seq_count, 1, -1)
        tokens = [item for pair in zip(*tokens, strict=True) for item in pair]
        contexts, attended = attend(
            low, high, me_at, tokens, mat_own[layer], bias_own, prefix_k, prefix_v, columns, row
        )
        if layer:
            parts = hidden_rest(*parts)
            contexts = after(contexts, parts)
        else:
            contexts = after(contexts, parts)
            parts = hidden_rest(*parts)
        contexts = [contexts[0]] + [swap(contexts[k], k) for k in range(1, seq_count)]
        ins, backs = hidden_all(*parts)
        normal_one, inverse_one = mix(
            me_at, contexts, upper, lower, mat_outs[layer], row_of(bias_out[layer])
        )
        if not last:
            parts = hidden_first(*shares[layer + 1], False)
        outputs, (slope, normal_two, inverse_two) = feed(
            me_at,
            core_at,
            ins,
            backs,
            normal_one,
            row_of(norm_gain[layer, 0]),
            row_of(norm_shift[layer, 0]),
            bias_hidden,
            row_of(bias_back[layer]),
            row_of(norm_gain[layer, 1]),
            row_of(norm_shift[layer, 1]),
            1 if last else 2,
        )
        saved.append(
            (
                (attended, prefix_k, prefix_v),
                (normal_one, inverse_one, normal_two, inverse_two),
                (ins, backs, slope, mat_outs[layer]),
            )
        )
        if last:
            hidden_out = outputs[0]
        else:
            upper, lower = after(outputs, parts)
            tokens = exchange(upper, bits), exchange(lower, bits[::-1])
            if not layer:
                mat_qkv = [gather(all_qkv(after(matrix, upper))) for matrix in w_qkv]

    def over_dp(own):
        stride = 1
        while stride < dp_count:
            own = own + over_dp_swap(own, stride)
            stride *= 2
        return own

    gradient = cotangent[0]
    prefix_grads = []
    for layer in reversed(range(layer_count)):
        (attended, prefix_k, prefix_v), norms, (ins, backs, slope, mat_out) = saved[layer]
        grad_one, pieces = feed_back(
            me_at,
            seq_count,
            ins,
            backs,
            gradient,
            slope,
            norms,
            row_of(norm_gain[layer, 1]),
            row_of(norm_gain[layer, 0]),
            mat_out,
        )
        pieces = [pieces[0]] + [swap(pieces[k], k) for k in range(1, seq_count)]
        grads, layer_grads = [], []
        for group in range(groups):
            found, prefix_grad = attend_back(
                low,
                high,
                me_at,
                group,
                pieces,
                attended,
                prefix_k,
                prefix_v,
                columns,
                row,
            )
            layer_grads.append(prefix_grad)
            if grads:
                found = after(found, grads[-1])
            grads.append([found[0]] + [swap(found[k], k) for k in range(1, seq_count)])
        layer_grads = over_dp(jnp.concatenate(layer_grads, 2))
        layer_grads = after(layer_grads, grads[-1])
        prefix_grads.append([layer_grads] + [swap(layer_grads, k) for k in range(1, seq_count)])
        grads = [grads[group][k] for k in range(seq_count) for group in range(groups)]
        gradient = collect(grads, grad_one, mat_qkv[layer], jnp.float32 if layer else jnp.bfloat16)

    found = [jnp.stack(items) for items in zip(*prefix_grads[::-1], strict=True)]
    for bit in bits:
        found = [jnp.where(me & bit, found[k ^ bit], found[k]) for k in range(seq_count)]
    whole = jnp.concatenate(found, 3)
    return (hidden_out[None], gradient[None], whole[:, 0], whole[:, 1])


def solution(mesh):
    in_specs = (
        P("dp", "seq", None),
        P("dp", "seq", None),
        P("dp", None),
        P(None, "dp", None),
        P(),
        P(None, "dp", None),
        P(),
        P(None, "dp", None),
        P(),
        P(None, "dp", None),
        P(),
        P(),
        P(),
        P(),
        P(),
    )
    out_specs = (P("dp", "seq", None), P("dp", "seq", None), P(), P())
    return jax.shard_map(
        functools.partial(local, mesh.shape["dp"], mesh.shape["seq"]),
        mesh=mesh,
        in_specs=in_specs,
        out_specs=out_specs,
        check_vma=False,
    )
```

time: 1330 us -> 634 us (0.48)
  matrix products: 558 us -> 0 us
  waiting for transfers between devices: 524 us -> 180 us
  Pallas kernels: 0 us -> 315 us
  other arithmetic: 77 us -> 5.53 us
  local copies, waits for them, and re-layouts: 109 us -> 40 us
  starting transfers between devices: 0.86 us -> 69 us
  blocking collectives: 40.1 us -> 0 us
    dot_general x38 -> x0, matrix products: 558 us -> none  [the longest x6 72.7 us: back_dot(): lax.dot_general(left, right, (((1,), (1,)), ((), ())), preferred_element_...]
    all_gather x16 -> x8, waiting for transfers between devices: 481 us -> 39.3 us  [the longest x2 39.2 us: hidden_share(): both = lax.all_gather(jnp.stack([into, back]), 'dp')]
    pallas_call x0 -> x14, Pallas kernels: none -> 315 us  [scalar_call(): pl.pallas_call(kernel, grid_spec=pltpu.PrefetchScalarGridSpec(num_scalar_...]
    ppermute x0 -> x72, waiting for transfers between devices: none -> 141 us  [the longest x54 127 us: swap(): return lax.ppermute(value, 'seq', [(i, i ^ step) for i in range(seq_count)])]
    ppermute x0 -> x72, starting transfers between devices: none -> 68.5 us  [the longest x54 64.5 us: swap(): return lax.ppermute(value, 'seq', [(i, i ^ step) for i in range(seq_count)])]
    reduce_sum x15 -> x2, other arithmetic: 61.8 us -> 0.18 us  [the longest x1 0.1 us: local(): jnp.sum((places[:, None] >= ends[None, :]).astype(jnp.int32), 1, dtype=jn...]
    all_gather x8 -> x0, local copies, waits for them, and re-layouts: 52.7 us -> none  [the longest x2 13.4 us: attend_backward(): query_piece = lax.all_gather(queries, 'seq', axis=0, tiled=True)]
    all_gather x5 -> x0, blocking collectives: 40.1 us -> none  [the longest x2 16.4 us: attend_backward(): lax.all_gather(delta_rows.astype(jnp.bfloat16), 'seq', axis=0, tiled=True)]
  transfers between devices with their start and end apart: 17 -> 80, of which waited for: 10 -> 30; matrix products, arithmetic and copies ran while one was open for 49% -> 5% of each run, Pallas kernels for 0% -> 50%
where the time goes in v3:
time: 634 us; the launch traced here: 625 us
  Pallas kernels  315 us (50%)
  waiting for transfers between devices  180 us (28%)
  starting transfers between devices  69 us (11%)
  local copies, waits for them, and re-layouts  40 us (6%)
  between operations  15.5 us (2%)
    pallas_call x14, Pallas kernels, scalar_call(): pl.pallas_call(kernel, grid_spec=pltpu.PrefetchScalarGridSpec(num_scalar_...  315 us
    ppermute x54, waiting for transfers between devices, swap(): return lax.ppermute(value, 'seq', [(i, i ^ step) for i in range(seq_count)])  127 us
    ppermute x54, starting transfers between devices, swap(): return lax.ppermute(value, 'seq', [(i, i ^ step) for i in range(seq_count)])  64.5 us
    all_gather x2, waiting for transfers between devices, hidden_share(): both = lax.all_gather(jnp.stack([into, back]), 'dp')  39.2 us
    ppermute x6, waiting for transfers between devices, over_dp_swap(): return lax.ppermute(value, 'dp', [(i, i ^ bit) for i in range(dp_count)])  13.5 us
  transfers between devices with their start and end apart: 80, of which 30 were waited for; matrix products, arithmetic and copies ran while one was open for 5% of the time, Pallas kernels for 50%

profile of v3, /device:TPU:0, one launch (start us, length us, event | category | flops | bytes accessed | tf_op | source)
XLA Modules:
  0.0 625.1 jit_solution(31618371624763574)
XLA Ops:
  21.9 6.2 collective-permute-done.refs_2_
  30.2 8.3 %collective-permute-done.2.refs_3_ = bf16[256,1024]{1,0:T(8,128)(2,1)} collective-permute-done((bf16[256,1024]{1,0:T(8,128)(2,1)}, bf16[256,1024]{1,0:T(8,128)(2,1)}, u32[]{:S(2)}, u32[]{:S(2)}) %collective-permute-start.2) | collective-permute-done | bytes 524320 | tf_op jit(solution)/shard_map/ppermute | solution.py:637
  51.6 39.2 %all-gather.25.cloned.1.call-done = bf16[16,128,1024]{2,1,0:T(8,128)(2,1)} async-done(((bf16[2,128,1024]{2,1,0:T(8,128)(2,1)}), bf16[16,128,1024]{2,1,0:T(8,128)(2,1)}) %all-gather.25.cloned.1.call-update) | async-done | bytes 4194320 | tf_op jit(solution)/shard_map/all_gather | solution.py:698
  101.3 39.7 %attend.2 = (bf16[512,256]{1,0:T(8,128)(2,1)}, bf16[512,256]{1,0:T(8,128)(2,1)}, bf16[512,256]{1,0:T(8,128)(2,1)}, bf16[512,256]{1,0:T(8,128)(2,1)}, f32[256,204...) custom-call(s32[8]{0:T(128)} %get-tuple-element.241.low_ref, ...), custom_call_target="tpu_custom_call" | custom-call | flops 44000002048 | tf_op jit(solution)/shard_map/attend/pallas_call | solution.py:63
  148.4 4.7 collective-permute-done.30.refs_1_
  156.8 25.7 %collective-permute-done.31.refs_2_ = bf16[512,256]{1,0:T(8,128)(2,1)S(1)} collective-permute-done((bf16[512,256]{1,0:T(8,128)(2,1)}, bf16[512,256]{1,0:T(8,128)(2,1)S(1)}, u32[]{:S(2)}, u32[]{:S(2)}) %collective-permute-start.31) | collective-permute-done | bytes 262176 | tf_op jit(solution)/shard_map/ppermute | solution.py:637
  189.2 5.5 mix.2
  196.8 22.7 %feed.2 = (bf16[256,1024]{1,0:T(8,128)(2,1)}, bf16[256,1024]{1,0:T(8,128)(2,1)}, bf16[512,4096]{1,0:T(8,128)(2,1)}, f32[512,1024]{1,0:T(8,128)}, f32[512,1]{1,0:T(8,128)}) custom-call(s32[1]{0:T(128)} %bitcast.me_ref, s32[1]{0:T(128)} %bitcast.1.core_ref, bf16[1024,512]{1,0:T(8,128)(2,1)} %copy-done.2, bf16[1024,512]{1,0:T(8,128)(2,1)} %get-tuple-element.192.refs_1_, ...), custom_call_target="tpu_custom_call" | custom-call | flops 24199999488 | tf_op jit(solution)/shard_map/feed/pallas_call | solution.py:63
  227.1 11.0 %collective-permute-done.33.refs_2_ = bf16[256,1024]{1,0:T(8,128)(2,1)S(1)} collective-permute-done((bf16[256,1024]{1,0:T(8,128)(2,1)}, bf16[256,1024]{1,0:T(8,128)(2,1)S(1)}, u32[]{:S(2)}, u32[]{:S(2)}) %collective-permute-start.33) | collective-permute-done | bytes 524320 | tf_op jit(solution)/shard_map/ppermute | solution.py:637
  242.8 6.5 %collective-permute-done.34.refs_3_ = bf16[256,1024]{1,0:T(8,128)(2,1)S(1)} collective-permute-done((bf16[256,1024]{1,0:T(8,128)(2,1)}, bf16[256,1024]{1,0:T(8,128)(2,1)S(1)}, u32[]{:S(2)}, u32[]{:S(2)}) %collective-permute-start.34) | collective-permute-done | bytes 524320 | tf_op jit(solution)/shard_map/ppermute | solution.py:637
  250.3 11.2 %collective-permute-done.37.refs_6_ = bf16[256,1024]{1,0:T(8,128)(2,1)S(1)} collective-permute-done((bf16[256,1024]{1,0:T(8,128)(2,1)S(1)}, bf16[256,1024]{1,0:T(8,128)(2,1)S(1)}, u32[]{:S(2)}, u32[]{:S(2)}) %collective-permute-start.37) | collective-permute-done | bytes 524320 | tf_op jit(solution)/shard_map/ppermute | solution.py:637
  264.9 39.5 %attend.3 = (bf16[512,256]{1,0:T(8,128)(2,1)}, bf16[512,256]{1,0:T(8,128)(2,1)}, bf16[512,256]{1,0:T(8,128)(2,1)}, bf16[512,256]{1,0:T(8,128)(2,1)}, f32[256,204...) custom-call(s32[8]{0:T(128)} %get-tuple-element.241.low_ref, ...), custom_call_target="tpu_custom_call" | custom-call | flops 44000002048 | tf_op jit(solution)/shard_map/attend/pallas_call | solution.py:63
  308.9 5.6 collective-permute-done.39.refs_1_
  314.5 4.0 collective-permute-done.40.refs_2_
  320.4 5.3 mix.3
  327.1 22.7 %feed.3 = (bf16[512,1024]{1,0:T(8,128)(2,1)}, bf16[512,4096]{1,0:T(8,128)(2,1)}, f32[512,1024]{1,0:T(8,128)}, f32[512,1]{1,0:T(8,128)}) custom-call(s32[1]{0:T(128)} %bitcast.me_ref, s32[1]{0:T(128)} %bitcast.1.core_ref, bf16[1024,512]{1,0:T(8,128)(2,1)} %copy-done.4, bf16[1024,512]{1,0:T(8,128)(2,1)} %get-tuple-element.200.refs_1_, ...), custom_call_target="tpu_custom_call" | custom-call | flops 24199999488 | tf_op jit(solution)/shard_map/feed/pallas_call | solution.py:63
  349.8 17.3 %feed_back.2 = (f32[512,1024]{1,0:T(8,128)}, bf16[512,256]{1,0:T(8,128)(2,1)}, bf16[512,256]{1,0:T(8,128)(2,1)}, bf16[512,256]{1,0:T(8,128)(2,1)}, bf16[512,256]{1,0:T(8,128)(2,1)}) custom-call(s32[1]{0:T(128)} %bitcast.me_ref, bf16[1024,512]{1,0:T(8,128)(2,1)} %copy-done.4, bf16[1024,512]{1,0:T(8,128)(2,1)} %get-tuple-element.200.refs_1_, ...), custom_call_target="tpu_custom_call" | custom-call | flops 19800000512 | tf_op jit(solution)/shard_map/feed_back/pallas_call | solution.py:63
  371.6 4.9 collective-permute-done.42.refs_1_
  376.5 4.1 collective-permute-done.43.refs_2_
  382.8 31.1 %attend_back.4 = (bf16[512,384]{1,0:T(8,128)(2,1)}, bf16[512,384]{1,0:T(8,128)(2,1)}, bf16[512,384]{1,0:T(8,128)(2,1)}, bf16[512,384]{1,0:T(8,128)(2,1)}, f32[2,64,128]{2,1,0:T(8,128)}) custom-call(s32[8]{0:T(128)} %get-tuple-element.241.low_ref, s32[8]{0:T(128)} %get-tuple-element.240.high_ref, s32[1]{0:T(128)} %bitcast.me_ref, ...), custom_call_target="tpu_custom_call" | custom-call | flops 32999999488 | tf_op jit(solution)/shard_map/attend_back/pallas_call | solution.py:63
  417.4 31.1 %attend_back.5 = (bf16[512,384]{1,0:T(8,128)(2,1)}, bf16[512,384]{1,0:T(8,128)(2,1)}, bf16[512,384]{1,0:T(8,128)(2,1)}, bf16[512,384]{1,0:T(8,128)(2,1)}, f32[2,64,128]{2,1,0:T(8,128)}) custom-call(s32[8]{0:T(128)} %get-tuple-element.241.low_ref, s32[8]{0:T(128)} %get-tuple-element.240.high_ref, s32[1]{0:T(128)} %bitcast.me_ref, ...), custom_call_target="tpu_custom_call" | custom-call | flops 32999999488 | tf_op jit(solution)/shard_map/attend_back/pallas_call | solution.py:63
  452.1 8.8 %collective-permute-done.48.refs_3_ = bf16[512,384]{1,0:T(8,128)(2,1)S(1)} collective-permute-done((bf16[512,384]{1,0:T(8,128)(2,1)}, bf16[512,384]{1,0:T(8,128)(2,1)S(1)}, u32[]{:S(2)}, u32[]{:S(2)}) %collective-permute-start.48) | collective-permute-done | bytes 393248 | tf_op jit(solution)/shard_map/ppermute | solution.py:637
  460.9 6.1 collective-permute-done.49.refs_5_
  467.9 10.3 %collect.2.refs_19_ = f32[512,1024]{1,0:T(8,128)} custom-call(bf16[512,384]{1,0:T(8,128)(2,1)} %get-tuple-element.138.refs_0_, bf16[512,384]{1,0:T(8,128)(2,1)} %get-tuple-element.146.refs_1_, bf16[512,384]{1,0:T(8,128)(2,1)} %copy-done.37, bf16[512,384]{1,0:T(8,128)(2,1)} %copy-done.40, bf16[512,384]{1,0:T(8,128)(2,1)} %copy-done.38, ...), custom_call_target="tpu_custom_call" | custom-call | flops 9900000256 | tf_op jit(solution)/shard_map/collect/pallas_call | solution.py:63
  478.2 17.6 %feed_back.3 = (f32[512,1024]{1,0:T(8,128)}, bf16[512,256]{1,0:T(8,128)(2,1)}, bf16[512,256]{1,0:T(8,128)(2,1)}, bf16[512,256]{1,0:T(8,128)(2,1)}, bf16[512,256]{1,0:T(8,128)(2,1)}) custom-call(s32[1]{0:T(128)} %bitcast.me_ref, bf16[1024,512]{1,0:T(8,128)(2,1)} %copy-done.2, bf16[1024,512]{1,0:T(8,128)(2,1)} %get-tuple-element.192.refs_1_, ...), custom_call_target="tpu_custom_call" | custom-call | flops 19800000512 | tf_op jit(solution)/shard_map/feed_back/pallas_call | solution.py:63
  504.2 4.2 collective-permute-done.52.refs_2_
  509.2 31.1 %attend_back.6 = (bf16[512,384]{1,0:T(8,128)(2,1)}, bf16[512,384]{1,0:T(8,128)(2,1)}, bf16[512,384]{1,0:T(8,128)(2,1)}, bf16[512,384]{1,0:T(8,128)(2,1)}, f32[2,64,128]{2,1,0:T(8,128)}) custom-call(s32[8]{0:T(128)} %get-tuple-element.241.low_ref, s32[8]{0:T(128)} %get-tuple-element.240.high_ref, s32[1]{0:T(128)} %bitcast.me_ref, ...), custom_call_target="tpu_custom_call" | custom-call | flops 32999999488 | tf_op jit(solution)/shard_map/attend_back/pallas_call | solution.py:63
  543.7 31.2 %attend_back.7 = (bf16[512,384]{1,0:T(8,128)(2,1)}, bf16[512,384]{1,0:T(8,128)(2,1)}, bf16[512,384]{1,0:T(8,128)(2,1)}, bf16[512,384]{1,0:T(8,128)(2,1)}, f32[2,64,128]{2,1,0:T(8,128)}) custom-call(s32[8]{0:T(128)} %get-tuple-element.241.low_ref, s32[8]{0:T(128)} %get-tuple-element.240.high_ref, s32[1]{0:T(128)} %bitcast.me_ref, ...), custom_call_target="tpu_custom_call" | custom-call | flops 32999999488 | tf_op jit(solution)/shard_map/attend_back/pallas_call | solution.py:63
  581.1 5.6 collective-permute-done.61
  586.8 5.0 collective-permute-done.66
  603.2 3.3 collective-permute-start.70
  606.5 9.9 %collect.3 = bf16[512,1024]{1,0:T(8,128)(2,1)} custom-call(bf16[512,384]{1,0:T(8,128)(2,1)} %get-tuple-element.164.refs_0_, bf16[512,384]{1,0:T(8,128)(2,1)} %get-tuple-element.172.refs_1_, bf16[512,384]{1,0:T(8,128)(2,1)} %copy-done.32, bf16[512,384]{1,0:T(8,128)(2,1)} %copy-done.35, bf16[512,384]{1,0:T(8,128)(2,1)} %copy-done.33, ...), custom_call_target="tpu_custom_call" | custom-call | flops 9900000256 | tf_op jit(solution)/shard_map/collect/pallas_call | solution.py:63
  (340 shorter events, 130.1 us)
Async XLA Ops:
  7.2 32.8 %all-gather.11.cloned.1.call-start = ((), (), s32[]{:S(2)}) async-start(), calls=%async_computation | async-start | bytes 1769472 | tf_op jit(solution)/shard_map/all_gather | solution.py:654
  10.9 79.9 %all-gather.25.cloned.1.call-start = ((), (), s32[]{:S(2)}) async-start(), calls=%async_computation.7 | async-start | bytes 4718592 | tf_op jit(solution)/shard_map/all_gather | solution.py:698
  43.2 140.4 %all-gather.23.cloned.1.call-start = ((), (), s32[]{:S(2)}) async-start(), calls=%async_computation.6 | async-start | bytes 4718592 | tf_op jit(solution)/shard_map/all_gather | solution.py:698
  44.6 144.7 %all-gather.13.cloned.1.call-start = ((), (), s32[]{:S(2)}) async-start(), calls=%async_computation.1 | async-start | bytes 2359296 | tf_op jit(solution)/shard_map/all_gather | solution.py:654
  45.5 219.4 %all-gather.15.cloned.1.call-start = ((), (), s32[]{:S(2)}) async-start(), calls=%async_computation.2 | async-start | bytes 1769472 | tf_op jit(solution)/shard_map/all_gather | solution.py:654
  48.6 50.8 %collective-permute-start.28 = (bf16[256,1024]{1,0:T(8,128)(2,1)}, bf16[256,1024]{1,0:T(8,128)(2,1)S(1)}, u32[]{:S(2)}, u32[]{:S(2)}) collective-permute-start(bf16[256,1024]{1,0:T(8,128)(2,1)} %collective-permute-done.refs_2_), channel_id=1, source_target_pairs={{0,2},{1,3},{2,0},{3,1},{4,6},{5,7},{6,4},{7,5},{8,10},{9,11},{10,... | collective-permute-start | bytes 1572872 | tf_op jit(solution)/shard_map/ppermute | solution.py:637
  50.1 49.8 %collective-permute-start.29 = (bf16[256,1024]{1,0:T(8,128)(2,1)}, bf16[256,1024]{1,0:T(8,128)(2,1)}, u32[]{:S(2)}, u32[]{:S(2)}) collective-permute-start(bf16[256,1024]{1,0:T(8,128)(2,1)} %collective-permute-done.3.refs_5_), channel_id=1, source_target_pairs={{0,1},{1,0},{2,3},{3,2},{4,5},{5,4},{6,7},{7,6},{8,9},{9,8},{10,11... | collective-permute-start | bytes 1572872 | tf_op jit(solution)/shard_map/ppermute | solution.py:637
  51.5 268.9 %all-gather.17.cloned.1.call-start = ((), (), s32[]{:S(2)}) async-start(), calls=%async_computation.3 | async-start | bytes 2359296 | tf_op jit(solution)/shard_map/all_gather | solution.py:654
  94.7 46.3 %collective-permute-start.16 = (bf16[1024,512]{1,0:T(8,128)(2,1)S(1)}, bf16[1024,512]{1,0:T(8,128)(2,1)S(1)}, u32[]{:S(2)}, u32[]{:S(2)}) collective-permute-start(bf16[1024,512]{1,0:T(8,128)(2,1)S(1)} %get-tuple-element.193.refs_0_), channel_id=1, source_target_pairs={{0,1},{1,0},{2,3},{3,2},{4,5},{5,4},{6,7},{7,6},{8,9},{9,8},{10,11... | collective-permute-start | bytes 3145736 | tf_op jit(solution)/shard_map/ppermute | solution.py:637
  96.2 44.9 %collective-permute-start.18 = (bf16[1024,512]{1,0:T(8,128)(2,1)S(1)}, bf16[1024,512]{1,0:T(8,128)(2,1)}, u32[]{:S(2)}, u32[]{:S(2)}) collective-permute-start(bf16[1024,512]{1,0:T(8,128)(2,1)S(1)} %get-tuple-element.193.refs_0_), channel_id=1, source_target_pairs={{0,2},{1,3},{2,0},{3,1},{4,6},{5,7},{6,4},{7,5},{8,10},{9,11},{10,... | collective-permute-start | bytes 3145736 | tf_op jit(solution)/shard_map/ppermute | solution.py:637
  98.9 43.8 %collective-permute-start.22 = (bf16[512,1024]{1,0:T(8,128)(2,1)S(1)}, bf16[512,1024]{1,0:T(8,128)(2,1)}, u32[]{:S(2)}, u32[]{:S(2)}) collective-permute-start(bf16[512,1024]{1,0:T(8,128)(2,1)S(1)} %get-tuple-element.191.refs_8_), channel_id=1, source_target_pairs={{0,1},{1,0},{2,3},{3,2},{4,5},{5,4},{6,7},{7,6},{8,9},{9,8},{10,11... | collective-permute-start | bytes 3145736 | tf_op jit(solution)/shard_map/ppermute | solution.py:637
  99.4 44.3 %collective-permute-start.24 = (bf16[512,1024]{1,0:T(8,128)(2,1)S(1)}, bf16[512,1024]{1,0:T(8,128)(2,1)S(1)}, u32[]{:S(2)}, u32[]{:S(2)}) collective-permute-start(bf16[512,1024]{1,0:T(8,128)(2,1)S(1)} %get-tuple-element.191.refs_8_), channel_id=1, source_target_pairs={{0,2},{1,3},{2,0},{3,1},{4,6},{5,7},{6,4},{7,5},{8,10},{9,11},{10,... | collective-permute-start | bytes 3145736 | tf_op jit(solution)/shard_map/ppermute | solution.py:637
  144.3 38.7 %collective-permute-start.17 = (bf16[1024,512]{1,0:T(8,128)(2,1)S(1)}, bf16[1024,512]{1,0:T(8,128)(2,1)}, u32[]{:S(2)}, u32[]{:S(2)}) collective-permute-start(bf16[1024,512]{1,0:T(8,128)(2,1)S(1)} %collective-permute-done.16.refs_2_), channel_id=1, source_target_pairs={{0,4},{4,0},{8,12},{12,8},{16,20},{20,16},{24,28},{28,24},{1,5},{5... | collective-permute-start | bytes 3145736 | tf_op jit(solution)/shard_map/ppermute | solution.py:651
  144.3 38.8 %collective-permute-start.20 = (bf16[1024,512]{1,0:T(8,128)(2,1)}, bf16[1024,512]{1,0:T(8,128)(2,1)}, u32[]{:S(2)}, u32[]{:S(2)}) collective-permute-start(bf16[1024,512]{1,0:T(8,128)(2,1)} %collective-permute-done.18.refs_4_), channel_id=1, source_target_pairs={{0,1},{1,0},{2,3},{3,2},{4,5},{5,4},{6,7},{7,6},{8,9},{9,8},{10,11... | collective-permute-start | bytes 3145736 | tf_op jit(solution)/shard_map/ppermute | solution.py:637
  145.7 37.8 %collective-permute-start.26 = (bf16[512,1024]{1,0:T(8,128)(2,1)}, bf16[512,1024]{1,0:T(8,128)(2,1)}, u32[]{:S(2)}, u32[]{:S(2)}) collective-permute-start(bf16[512,1024]{1,0:T(8,128)(2,1)} %collective-permute-done.22.refs_10_), channel_id=1, source_target_pairs={{0,2},{1,3},{2,0},{3,1},{4,6},{5,7},{6,4},{7,5},{8,10},{9,11},{10,... | collective-permute-start | bytes 3145736 | tf_op jit(solution)/shard_map/ppermute | solution.py:637
  147.9 34.6 %collective-permute-start.31 = (bf16[512,256]{1,0:T(8,128)(2,1)}, bf16[512,256]{1,0:T(8,128)(2,1)S(1)}, u32[]{:S(2)}, u32[]{:S(2)}) collective-permute-start(bf16[512,256]{1,0:T(8,128)(2,1)} %get-tuple-element.104), channel_id=1, source_target_pairs={{0,2},{1,3},{2,0},{3,1},{4,6},{5,7},{6,4},{7,5},{8,10},{9,11},{10,... | collective-permute-start | bytes 786440 | tf_op jit(solution)/shard_map/ppermute | solution.py:637
  153.2 29.3 %collective-permute-start.32 = (bf16[512,256]{1,0:T(8,128)(2,1)}, bf16[512,256]{1,0:T(8,128)(2,1)}, u32[]{:S(2)}, u32[]{:S(2)}) collective-permute-start(bf16[512,256]{1,0:T(8,128)(2,1)} %get-tuple-element.105), channel_id=1, source_target_pairs={{0,3},{1,2},{2,1},{3,0},{4,7},{5,6},{6,5},{7,4},{8,11},{9,10},{10,... | collective-permute-start | bytes 786440 | tf_op jit(solution)/shard_map/ppermute | solution.py:637
  156.5 310.5 %all-gather.19.cloned.1.call-start = ((), (), s32[]{:S(2)}) async-start(), calls=%async_computation.4 | async-start | bytes 7077888 | tf_op jit(solution)/shard_map/all_gather | solution.py:654
  194.7 25.5 %collective-permute-start.4 = (bf16[1024,512]{1,0:T(8,128)(2,1)S(1)}, bf16[1024,512]{1,0:T(8,128)(2,1)S(1)}, u32[]{:S(2)}, u32[]{:S(2)}) collective-permute-start(bf16[1024,512]{1,0:T(8,128)(2,1)S(1)} %get-tuple-element.201.refs_0_), channel_id=1, source_target_pairs={{0,1},{1,0},{2,3},{3,2},{4,5},{5,4},{6,7},{7,6},{8,9},{9,8},{10,11... | collective-permute-start | bytes 3145736 | tf_op jit(solution)/shard_map/ppermute | solution.py:637
  222.9 383.6 %all-gather.21.cloned.1.call-start = ((), (), s32[]{:S(2)}) async-start(), calls=%async_computation.5 | async-start | bytes 7077888 | tf_op jit(solution)/shard_map/all_gather | solution.py:654
  241.8 62.7 %collective-permute-start.6 = (bf16[1024,512]{1,0:T(8,128)(2,1)S(1)}, bf16[1024,512]{1,0:T(8,128)(2,1)}, u32[]{:S(2)}, u32[]{:S(2)}) collective-permute-start(bf16[1024,512]{1,0:T(8,128)(2,1)S(1)} %get-tuple-element.201.refs_0_), channel_id=1, source_target_pairs={{0,2},{1,3},{2,0},{3,1},{4,6},{5,7},{6,4},{7,5},{8,10},{9,11},{10,... | collective-permute-start | bytes 3145736 | tf_op jit(solution)/shard_map/ppermute | solution.py:637
  249.3 55.2 %collective-permute-start.10 = (bf16[512,1024]{1,0:T(8,128)(2,1)}, bf16[512,1024]{1,0:T(8,128)(2,1)}, u32[]{:S(2)}, u32[]{:S(2)}) collective-permute-start(bf16[512,1024]{1,0:T(8,128)(2,1)} %get-tuple-element.199.refs_8_), channel_id=1, source_target_pairs={{0,1},{1,0},{2,3},{3,2},{4,5},{5,4},{6,7},{7,6},{8,9},{9,8},{10,11... | collective-permute-start | bytes 3145736 | tf_op jit(solution)/shard_map/ppermute | solution.py:637
  250.3 58.1 %collective-permute-start.5 = (bf16[1024,512]{1,0:T(8,128)(2,1)}, bf16[1024,512]{1,0:T(8,128)(2,1)}, u32[]{:S(2)}, u32[]{:S(2)}) collective-permute-start(bf16[1024,512]{1,0:T(8,128)(2,1)} %copy-done.22), channel_id=1, source_target_pairs={{0,4},{4,0},{8,12},{12,8},{16,20},{20,16},{24,28},{28,24},{1,5},{5... | collective-permute-start | bytes 3145736 | tf_op jit(solution)/shard_map/ppermute | solution.py:651
  261.5 43.4 %collective-permute-start.8 = (bf16[1024,512]{1,0:T(8,128)(2,1)}, bf16[1024,512]{1,0:T(8,128)(2,1)}, u32[]{:S(2)}, u32[]{:S(2)}) collective-permute-start(bf16[1024,512]{1,0:T(8,128)(2,1)} %copy-done.22), channel_id=1, source_target_pairs={{0,2},{1,3},{2,0},{3,1},{4,6},{5,7},{6,4},{7,5},{8,10},{9,11},{10,... | collective-permute-start | bytes 3145736 | tf_op jit(solution)/shard_map/ppermute | solution.py:637
  263.8 41.1 %collective-permute-start.14 = (bf16[512,1024]{1,0:T(8,128)(2,1)}, bf16[512,1024]{1,0:T(8,128)(2,1)}, u32[]{:S(2)}, u32[]{:S(2)}) collective-permute-start(bf16[512,1024]{1,0:T(8,128)(2,1)} %collective-permute-done.12.refs_12_), channel_id=1, source_target_pairs={{0,1},{1,0},{2,3},{3,2},{4,5},{5,4},{6,7},{7,6},{8,9},{9,8},{10,11... | collective-permute-start | bytes 3145736 | tf_op jit(solution)/shard_map/ppermute | solution.py:637
  413.9 34.6 %collective-permute-start.45 = (bf16[512,384]{1,0:T(8,128)(2,1)}, bf16[512,384]{1,0:T(8,128)(2,1)S(1)}, u32[]{:S(2)}, u32[]{:S(2)}) collective-permute-start(bf16[512,384]{1,0:T(8,128)(2,1)} %get-tuple-element.143), channel_id=1, source_target_pairs={{0,1},{1,0},{2,3},{3,2},{4,5},{5,4},{6,7},{7,6},{8,9},{9,8},{10,11... | collective-permute-start | bytes 1179656 | tf_op jit(solution)/shard_map/ppermute | solution.py:637
  414.8 33.7 %collective-permute-start.46 = (bf16[512,384]{1,0:T(8,128)(2,1)}, bf16[512,384]{1,0:T(8,128)(2,1)S(1)}, u32[]{:S(2)}, u32[]{:S(2)}) collective-permute-start(bf16[512,384]{1,0:T(8,128)(2,1)} %get-tuple-element.144), channel_id=1, source_target_pairs={{0,2},{1,3},{2,0},{3,1},{4,6},{5,7},{6,4},{7,5},{8,10},{9,11},{10,... | collective-permute-start | bytes 1179656 | tf_op jit(solution)/shard_map/ppermute | solution.py:637
  416.3 32.3 %collective-permute-start.47 = (bf16[512,384]{1,0:T(8,128)(2,1)}, bf16[512,384]{1,0:T(8,128)(2,1)S(1)}, u32[]{:S(2)}, u32[]{:S(2)}) collective-permute-start(bf16[512,384]{1,0:T(8,128)(2,1)} %get-tuple-element.145), channel_id=1, source_target_pairs={{0,3},{1,2},{2,1},{3,0},{4,7},{5,6},{6,5},{7,4},{8,11},{9,10},{10,... | collective-permute-start | bytes 1179656 | tf_op jit(solution)/shard_map/ppermute | solution.py:637
  500.8 78.7 %collective-permute-start.65 = (f32[2,64,256]{2,1,0:T(8,128)S(1)}, f32[2,64,256]{2,1,0:T(8,128)S(1)}, u32[]{:S(2)}, u32[]{:S(2)}) collective-permute-start(f32[2,64,256]{2,1,0:T(8,128)S(1)} %add.92), channel_id=1, source_target_pairs={{0,8},{4,12},{8,0},{12,4},{16,24},{20,28},{24,16},{28,20},{1,9},{5... | collective-permute-start | bytes 393224 | tf_op jit(solution)/shard_map/ppermute | solution.py:733
  540.2 35.5 %collective-permute-start.54 = (bf16[512,384]{1,0:T(8,128)(2,1)}, bf16[512,384]{1,0:T(8,128)(2,1)S(1)}, u32[]{:S(2)}, u32[]{:S(2)}) collective-permute-start(bf16[512,384]{1,0:T(8,128)(2,1)} %get-tuple-element.169), channel_id=1, source_target_pairs={{0,1},{1,0},{2,3},{3,2},{4,5},{5,4},{6,7},{7,6},{8,9},{9,8},{10,11... | collective-permute-start | bytes 1179656 | tf_op jit(solution)/shard_map/ppermute | solution.py:637
  540.6 35.2 %collective-permute-start.55 = (bf16[512,384]{1,0:T(8,128)(2,1)}, bf16[512,384]{1,0:T(8,128)(2,1)S(1)}, u32[]{:S(2)}, u32[]{:S(2)}) collective-permute-start(bf16[512,384]{1,0:T(8,128)(2,1)} %get-tuple-element.170), channel_id=1, source_target_pairs={{0,2},{1,3},{2,0},{3,1},{4,6},{5,7},{6,4},{7,5},{8,10},{9,11},{10,... | collective-permute-start | bytes 1179656 | tf_op jit(solution)/shard_map/ppermute | solution.py:637
  542.4 33.4 %collective-permute-start.56 = (bf16[512,384]{1,0:T(8,128)(2,1)}, bf16[512,384]{1,0:T(8,128)(2,1)S(1)}, u32[]{:S(2)}, u32[]{:S(2)}) collective-permute-start(bf16[512,384]{1,0:T(8,128)(2,1)} %get-tuple-element.171), channel_id=1, source_target_pairs={{0,3},{1,2},{2,1},{3,0},{4,7},{5,6},{6,5},{7,4},{8,11},{9,10},{10,... | collective-permute-start | bytes 1179656 | tf_op jit(solution)/shard_map/ppermute | solution.py:637
  (100 other events, 1574.7 us)
Sparse Core Ops, SparseCore 0:
  11.0 27.7 all-gather.10
  43.3 47.4 all-gather.24
  93.0 45.8 all-gather.22
  140.4 27.8 all-gather.12
  169.7 24.5 all-gather.14
  195.7 28.6 all-gather.16
  226.0 64.2 all-gather.18
  371.7 62.5 all-gather.20

commit v4 on v3

--- a/solution.py
+++ b/solution.py
@@ -280,6 +280,8 @@
         for h in range(count):
             q_sum[head_of(h), at] += dot(keys_turned[head_of(h)], grad_scores[:, lanes_of(h)])
 
+    lane = lax.broadcasted_iota(jnp.int32, (1, width), 1)
+
     def prepare(i, carry):
         at = query_part(i)
         q_block = q_ref[at, :].T
@@ -291,8 +293,11 @@
         q_apart, g_apart = heads_apart(q_block, count), heads_apart(g_block, count)
         q_turned[:, wide(i)] = q_apart
         g_turned[:, wide(i)] = g_apart
-        q_alone[wide(i), :] = q_apart.T
-        g_alone[wide(i), :] = g_apart.T
+        for h in range(count):
+            own = (lane // HEAD == h).astype(jnp.bfloat16)
+            alone = pl.ds(pl.multiple_of((i * count + h) * BLOCK, BLOCK), BLOCK)
+            q_alone[alone, :] = q_ref[at, :] * own
+            g_alone[alone, :] = g_ref[at, :] * own
         pair_of_blocks(i, pk_ref[...], pv_ref[...], prefix_turned, None, pk_sum, pv_sum)
         return carry
 
@@ -482,24 +487,90 @@
     return results[:pieces], results[pieces:]
 
 
-def feed_back_kernel(parts, devices, me_ref, *refs):
+def collect_copies(pieces, matrix_ref, grad_ref, held):
+    piece_held, matrix_held, grad_held, piece_sems, matrix_sems, grad_sem = held
+    width = pieces[0].shape[1]
+    every = range(len(pieces))
+    grad_copy = pltpu.make_async_copy(grad_ref, grad_held, grad_sem.at[0])
+    piece_copies, matrix_copies = [], []
+    for at in every:
+        piece_copies += copy_in([pieces[at]], [piece_held.at[at]], piece_sems.at[at : at + 1])
+        if matrix_held.shape[0] > at:
+            block = matrix_ref
+            if matrix_held.shape[0] > 1:
+                block = matrix_ref.at[:, at * width : (at + 1) * width]
+            matrix_copies += copy_in([block], [matrix_held.at[at]], matrix_sems.at[at : at + 1])
+    grad_copy.start()
+    return grad_copy, piece_copies, matrix_copies
+
+
+def collect_held(copies, held):
+    grad_copy, piece_copies, matrix_copies = copies
+    total = None
+    width = held[0].shape[2]
+    for at, piece_copy in enumerate(piece_copies):
+        piece_copy.wait()
+        if at < len(matrix_copies):
+            matrix_copies[at].wait()
+        if len(matrix_copies) > 1:
+            block = held[1][at]
+        else:
+            block = held[1][0, :, at * width : (at + 1) * width]
+        product = back_dot(held[0][at], block)
+        total = product if total is None else total + product
+    grad_copy.wait()
+    return total + held[2][...]
+
+
+def collect_scratch(pieces, matrix, grad):
+    count = len(pieces)
+    rows, width = pieces[0].shape
+    blocks = 1 if width % 128 else count
+    return [
+        pltpu.VMEM((count, rows, width), jnp.bfloat16),
+        pltpu.VMEM((blocks, matrix.shape[0], matrix.shape[1] // blocks), jnp.bfloat16),
+        pltpu.VMEM(grad.shape, grad.dtype),
+        pltpu.SemaphoreType.DMA((count,)),
+        pltpu.SemaphoreType.DMA((count,)),
+        pltpu.SemaphoreType.DMA((1,)),
+    ]
+
+
+def collect_kernel(count, *refs):
+    pieces, (matrix_ref, grad_ref, result_ref), held = refs[:count], refs[count : count + 3], refs[count + 3 :]
+    copies = collect_copies(pieces, matrix_ref, grad_ref, held)
+    result_ref[...] = collect_held(copies, held).astype(result_ref.dtype)
+
+
+def collect(pieces, matrix, grad):
+    return scalar_call(
+        functools.partial(collect_kernel, len(pieces)),
+        "collect",
+        9,
+        (),
+        (*pieces, matrix, grad),
+        [(grad.shape, jnp.bfloat16)],
+        collect_scratch(pieces, matrix, grad),
+        specs={at: pl.BlockSpec(memory_space=pl.ANY) for at in range(len(pieces) + 2)},
+    )[0]
+
+
+def feed_back_kernel(parts, devices, count, me_ref, *refs):
     in_refs, back_refs, refs = refs[:parts], refs[parts : 2 * parts], refs[2 * parts :]
     (
         slope_ref,
         normal_one,
         matrix_ref,
-        gradient_ref,
-        normal_two,
-        inverse_two,
-        gain_two,
-        inverse_one,
-        gain_one,
-    ), refs = refs[:9], refs[9:]
+    ), refs = refs[:3], refs[3:]
+    behind, refs = refs[: max(count + 2, 1)], refs[max(count + 2, 1) :]
+    (normal_two, inverse_two, gain_two, inverse_one, gain_one), refs = refs[:5], refs[5:]
     grad_one_ref, refs = refs[0], refs[1:]
-    results, refs = refs[:-11], refs[-11:]
+    results, refs = refs[:devices], refs[devices:]
     held, total, in_held, back_held, slope_held, normal_held, matrix_held = refs[:7]
-    in_sems, back_sems, slope_sems, late_sems = refs[7:]
+    in_sems, back_sems, slope_sems, late_sems = refs[7:11]
     hidden = in_held.shape[2]
+    if count > 0:
+        collected = collect_copies(behind[:count], behind[count], behind[count + 1], refs[11:])
     back_copies = copy_in(back_refs, [back_held.at[t] for t in range(parts)], back_sems)
     slope_copies = copy_in(
         [slope_ref.at[:, t * hidden : (t + 1) * hidden] for t in range(parts)],
@@ -508,7 +579,10 @@
     )
     in_copies = copy_in(in_refs, [in_held.at[t] for t in range(parts)], in_sems)
     late_copies = copy_in([normal_one, matrix_ref], [normal_held, matrix_held], late_sems)
-    gradient = gradient_ref[...].astype(jnp.float32)
+    if count > 0:
+        gradient = collect_held(collected, refs[11:])
+    else:
+        gradient = behind[0][...].astype(jnp.float32)
     grad_two = normalize_back(gradient, normal_two[...], inverse_two[...], gain_two[...])
     held[...] = grad_two.astype(jnp.bfloat16)
     total[...] = grad_two
@@ -537,14 +611,15 @@
         result_ref[...] = product.astype(jnp.bfloat16)
 
 
-def feed_back(me, devices, ins, backs, gradient, slope, norms, gain_two, gain_one, matrix):
+def feed_back(me, devices, ins, backs, behind, slope, norms, gain_two, gain_one, matrix):
     normal_one, inverse_one, normal_two, inverse_two = norms
     parts = len(ins)
-    rows, width = gradient.shape
+    rows, width = normal_one.shape
+    count = len(behind) - 2
     hidden = ins[0].shape[1]
     anywhere = pl.BlockSpec(memory_space=pl.ANY)
     results = scalar_call(
-        functools.partial(feed_back_kernel, parts, devices),
+        functools.partial(feed_back_kernel, parts, devices, count),
         "feed_back",
         18,
         (me,),
@@ -554,7 +629,7 @@
             slope,
             normal_one,
             matrix,
-            gradient,
+            *behind,
             normal_two,
             inverse_two,
             gain_two,
@@ -575,31 +650,11 @@
             pltpu.SemaphoreType.DMA((parts,)),
             pltpu.SemaphoreType.DMA((parts,)),
             pltpu.SemaphoreType.DMA((2,)),
-        ],
-        specs={at: anywhere for at in range(2 * parts + 3)},
+        ]
+        + (collect_scratch(behind[:count], behind[count], behind[count + 1]) if count > 0 else []),
+        specs={at: anywhere for at in range(2 * parts + 3 + (count + 2 if count > 0 else 0))},
     )
     return results[0], results[1:]
-
-
-def collect_kernel(devices, *refs):
-    pieces, (grad_ref, matrix_ref, result_ref) = refs[:devices], refs[devices:]
-    total = grad_ref[...]
-    width = pieces[0].shape[1]
-    for step, piece_ref in enumerate(pieces):
-        total += back_dot(piece_ref[...], matrix_ref[:, step * width : (step + 1) * width])
-    result_ref[...] = total.astype(result_ref.dtype)
-
-
-def collect(pieces, grad_one, matrix, dtype):
-    return scalar_call(
-        functools.partial(collect_kernel, len(pieces)),
-        "collect",
-        9,
-        (),
-        (*pieces, grad_one, matrix),
-        [(grad_one.shape, dtype)],
-        [],
-    )[0]
 
 
 def local(
@@ -734,14 +789,14 @@
 
     saved = []
     tokens = first_tokens
+    shares = [hidden_share(w_in[0], w_back[0])]
     mat_own = [gather(own_qkv(w_qkv[0]))]
-    came = [mat_own[0]] + [found[bit] for found in first_tokens for bit in bits]
-    shares = [hidden_share(*after((w_in[0], w_back[0]), came))]
+    came = [found[bit] for found in first_tokens for bit in bits]
     mat_outs = [gather(after(w_out[0], came))]
     for layer in range(1, layer_count):
-        shares.append(hidden_share(*after((w_in[layer], w_back[layer]), came)))
-        mat_own.append(gather(own_qkv(after(w_qkv[layer], came))))
-        mat_outs.append(gather(after(w_out[layer], came)))
+        shares.append(hidden_share(*after((w_in[layer], w_back[layer]), tokens)))
+        mat_own.append(gather(own_qkv(after(w_qkv[layer], tokens))))
+        mat_outs.append(gather(after(w_out[layer], tokens)))
     parts = hidden_first(*shares[0], True)
     for layer in range(layer_count):
         last = layer + 1 == layer_count
@@ -804,7 +859,7 @@
             stride *= 2
         return own
 
-    gradient = cotangent[0]
+    behind = [cotangent[0]]
     prefix_grads = []
     for layer in reversed(range(layer_count)):
         (attended, prefix_k, prefix_v), norms, (ins, backs, slope, mat_out) = saved[layer]
@@ -813,7 +868,7 @@
             seq_count,
             ins,
             backs,
-            gradient,
+            behind,
             slope,
             norms,
             row_of(norm_gain[layer, 1]),
@@ -838,12 +893,15 @@
             layer_grads.append(prefix_grad)
             if grads:
                 found = after(found, grads[-1])
+            elif prefix_grads:
+                found = after(found, prefix_grads[-1])
             grads.append([found[0]] + [swap(found[k], k) for k in range(1, seq_count)])
         layer_grads = over_dp(jnp.concatenate(layer_grads, 2))
         layer_grads = after(layer_grads, grads[-1])
         prefix_grads.append([layer_grads] + [swap(layer_grads, k) for k in range(1, seq_count)])
         grads = [grads[group][k] for k in range(seq_count) for group in range(groups)]
-        gradient = collect(grads, grad_one, mat_qkv[layer], jnp.float32 if layer else jnp.bfloat16)
+        behind = [*grads, mat_qkv[layer], grad_one]
+    gradient = collect(behind[:-2], *behind[-2:])
 
     found = [jnp.stack(items) for items in zip(*prefix_grads[::-1], strict=True)]
     for bit in bits:

time: 634 us -> 616 us (0.972)
  waiting for transfers between devices: 180 us -> 155 us
  local copies, waits for them, and re-layouts: 40 us -> 48.7 us
    all_gather x2, waiting for transfers between devices: 39.2 us -> 0.02 us  [hidden_share(): both = lax.all_gather(jnp.stack([into, back]), 'dp')]
    all_gather x6, waiting for transfers between devices: 0.04 us -> 13.2 us  [gather(): return lax.all_gather(value, 'dp', axis=0, tiled=True)]
    pallas_call x14 -> x13, Pallas kernels: 315 us -> 312 us  [scalar_call(): pl.pallas_call(kernel, grid_spec=pltpu.PrefetchScalarGridSpec(num_scalar_...]
  transfers between devices with their start and end apart: 80 -> 80, of which waited for: 30 -> 24; matrix products, arithmetic and copies ran while one was open for 5% -> 7% of each run, Pallas kernels for 50% -> 51%
where the time goes in v4:
time: 616 us; the launch traced here: 611 us
  Pallas kernels  312 us (51%)
  waiting for transfers between devices  155 us (25%)
  starting transfers between devices  72.3 us (12%)
  local copies, waits for them, and re-layouts  48.7 us (8%)
  between operations  15.3 us (2%)
  other arithmetic  7.28 us (1%)
    pallas_call x13, Pallas kernels, scalar_call(): pl.pallas_call(kernel, grid_spec=pltpu.PrefetchScalarGridSpec(num_scalar_...  312 us
    ppermute x54, waiting for transfers between devices, swap(): return lax.ppermute(value, 'seq', [(i, i ^ step) for i in range(seq_count)])  124 us
    ppermute x54, starting transfers between devices, swap(): return lax.ppermute(value, 'seq', [(i, i ^ step) for i in range(seq_count)])  65.1 us
    ppermute x6, waiting for transfers between devices, over_dp_swap(): return lax.ppermute(value, 'dp', [(i, i ^ bit) for i in range(dp_count)])  17.7 us
    all_gather x6, waiting for transfers between devices, gather(): return lax.all_gather(value, 'dp', axis=0, tiled=True)  13.2 us
  transfers between devices with their start and end apart: 80, of which 24 were waited for; matrix products, arithmetic and copies ran while one was open for 7% of the time, Pallas kernels for 51%

profile of v4, /device:TPU:0, one launch (start us, length us, event | category | flops | bytes accessed | tf_op | source)
XLA Modules:
  0.0 610.7 jit_solution(2460189128918731397)
XLA Ops:
  16.3 2.9 collective-permute-start
  21.3 11.0 %collective-permute-done.refs_2_ = bf16[256,1024]{1,0:T(8,128)(2,1)} collective-permute-done((bf16[256,1024]{1,0:T(8,128)(2,1)}, bf16[256,1024]{1,0:T(8,128)(2,1)}, u32[]{:S(2)}, u32[]{:S(2)}) %collective-permute-start) | collective-permute-done | bytes 524320 | tf_op jit(solution)/shard_map/ppermute | solution.py:692
  38.2 7.5 %collective-permute-done.1.refs_4_ = bf16[256,1024]{1,0:T(8,128)(2,1)} collective-permute-done((bf16[256,1024]{1,0:T(8,128)(2,1)}, bf16[256,1024]{1,0:T(8,128)(2,1)}, u32[]{:S(2)}, u32[]{:S(2)}) %collective-permute-start.1) | collective-permute-done | bytes 524320 | tf_op jit(solution)/shard_map/ppermute | solution.py:692
  45.6 9.8 %collective-permute-done.2.refs_6_ = bf16[256,1024]{1,0:T(8,128)(2,1)} collective-permute-done((bf16[256,1024]{1,0:T(8,128)(2,1)}, bf16[256,1024]{1,0:T(8,128)(2,1)}, u32[]{:S(2)}, u32[]{:S(2)}) %collective-permute-start.2) | collective-permute-done | bytes 524320 | tf_op jit(solution)/shard_map/ppermute | solution.py:692
  77.4 13.2 %all-gather.11.cloned.1.call-done.refs_8_ = bf16[1024,768]{1,0:T(8,128)(2,1)} async-done(((bf16[128,768]{1,0:T(8,128)(2,1)}), bf16[1024,768]{1,0:T(8,128)(2,1)}) %all-gather.11.cloned.1.call-update) | async-done | bytes 1572880 | tf_op jit(solution)/shard_map/all_gather | solution.py:709
  92.0 39.8 %attend.2 = (bf16[512,256]{1,0:T(8,128)(2,1)}, bf16[512,256]{1,0:T(8,128)(2,1)}, bf16[512,256]{1,0:T(8,128)(2,1)}, bf16[512,256]{1,0:T(8,128)(2,1)}, f32[256,204...) custom-call(s32[8]{0:T(128)} %get-tuple-element.245.low_ref, ...), custom_call_target="tpu_custom_call" | custom-call | flops 44000002048 | tf_op jit(solution)/shard_map/attend/pallas_call | solution.py:63
  136.5 4.7 collective-permute-done.30.refs_1_
  145.7 24.9 %collective-permute-done.31.refs_2_ = bf16[512,256]{1,0:T(8,128)(2,1)S(1)} collective-permute-done((bf16[512,256]{1,0:T(8,128)(2,1)}, bf16[512,256]{1,0:T(8,128)(2,1)S(1)}, u32[]{:S(2)}, u32[]{:S(2)}) %collective-permute-start.31) | collective-permute-done | bytes 262176 | tf_op jit(solution)/shard_map/ppermute | solution.py:692
  177.3 5.5 mix.2
  185.9 22.8 %feed.2 = (bf16[256,1024]{1,0:T(8,128)(2,1)}, bf16[256,1024]{1,0:T(8,128)(2,1)}, bf16[512,4096]{1,0:T(8,128)(2,1)}, f32[512,1024]{1,0:T(8,128)}, f32[512,1]{1,0:T(8,128)}) custom-call(s32[1]{0:T(128)} %bitcast.me_ref, s32[1]{0:T(128)} %bitcast.1.core_ref, bf16[1024,512]{1,0:T(8,128)(2,1)} %copy-done.1, bf16[1024,512]{1,0:T(8,128)(2,1)} %get-tuple-element.196.refs_1_, ...), custom_call_target="tpu_custom_call" | custom-call | flops 24199999488 | tf_op jit(solution)/shard_map/feed/pallas_call | solution.py:63
  220.5 11.0 %collective-permute-done.33.refs_2_ = bf16[256,1024]{1,0:T(8,128)(2,1)S(1)} collective-permute-done((bf16[256,1024]{1,0:T(8,128)(2,1)}, bf16[256,1024]{1,0:T(8,128)(2,1)S(1)}, u32[]{:S(2)}, u32[]{:S(2)}) %collective-permute-start.33) | collective-permute-done | bytes 524320 | tf_op jit(solution)/shard_map/ppermute | solution.py:692
  237.0 5.7 collective-permute-done.34.refs_3_
  243.8 11.2 %collective-permute-done.37.refs_6_ = bf16[256,1024]{1,0:T(8,128)(2,1)S(1)} collective-permute-done((bf16[256,1024]{1,0:T(8,128)(2,1)S(1)}, bf16[256,1024]{1,0:T(8,128)(2,1)S(1)}, u32[]{:S(2)}, u32[]{:S(2)}) %collective-permute-start.37) | collective-permute-done | bytes 524320 | tf_op jit(solution)/shard_map/ppermute | solution.py:692
  258.3 39.7 %attend.3 = (bf16[512,256]{1,0:T(8,128)(2,1)}, bf16[512,256]{1,0:T(8,128)(2,1)}, bf16[512,256]{1,0:T(8,128)(2,1)}, bf16[512,256]{1,0:T(8,128)(2,1)}, f32[256,204...) custom-call(s32[8]{0:T(128)} %get-tuple-element.245.low_ref, ...), custom_call_target="tpu_custom_call" | custom-call | flops 44000002048 | tf_op jit(solution)/shard_map/attend/pallas_call | solution.py:63
  302.5 5.4 collective-permute-done.39.refs_1_
  313.5 5.3 mix.3
  319.8 22.7 %feed.3 = (bf16[512,1024]{1,0:T(8,128)(2,1)}, bf16[512,4096]{1,0:T(8,128)(2,1)}, f32[512,1024]{1,0:T(8,128)}, f32[512,1]{1,0:T(8,128)}) custom-call(s32[1]{0:T(128)} %bitcast.me_ref, s32[1]{0:T(128)} %bitcast.1.core_ref, bf16[1024,512]{1,0:T(8,128)(2,1)} %copy-done.2, bf16[1024,512]{1,0:T(8,128)(2,1)} %get-tuple-element.204.refs_1_, ...), custom_call_target="tpu_custom_call" | custom-call | flops 24199999488 | tf_op jit(solution)/shard_map/feed/pallas_call | solution.py:63
  342.5 17.3 %feed_back.2 = (f32[512,1024]{1,0:T(8,128)}, bf16[512,256]{1,0:T(8,128)(2,1)}, bf16[512,256]{1,0:T(8,128)(2,1)}, bf16[512,256]{1,0:T(8,128)(2,1)}, bf16[512,256]{1,0:T(8,128)(2,1)}) custom-call(s32[1]{0:T(128)} %bitcast.me_ref, bf16[1024,512]{1,0:T(8,128)(2,1)} %copy-done.2, bf16[1024,512]{1,0:T(8,128)(2,1)} %get-tuple-element.204.refs_1_, ...), custom_call_target="tpu_custom_call" | custom-call | flops 19800000512 | tf_op jit(solution)/shard_map/feed_back/pallas_call | solution.py:63
  364.4 4.8 collective-permute-done.42.refs_1_
  369.2 5.8 collective-permute-done.43.refs_2_
  375.8 31.0 %attend_back.4 = (bf16[512,384]{1,0:T(8,128)(2,1)}, bf16[512,384]{1,0:T(8,128)(2,1)}, bf16[512,384]{1,0:T(8,128)(2,1)}, bf16[512,384]{1,0:T(8,128)(2,1)}, f32[2,64,128]{2,1,0:T(8,128)}) custom-call(s32[8]{0:T(128)} %get-tuple-element.245.low_ref, s32[8]{0:T(128)} %get-tuple-element.244.high_ref, s32[1]{0:T(128)} %bitcast.me_ref, ...), custom_call_target="tpu_custom_call" | custom-call | flops 32999999488 | tf_op jit(solution)/shard_map/attend_back/pallas_call | solution.py:63
  410.3 31.1 %attend_back.5 = (bf16[512,384]{1,0:T(8,128)(2,1)}, bf16[512,384]{1,0:T(8,128)(2,1)}, bf16[512,384]{1,0:T(8,128)(2,1)}, bf16[512,384]{1,0:T(8,128)(2,1)}, f32[2,64,128]{2,1,0:T(8,128)}) custom-call(s32[8]{0:T(128)} %get-tuple-element.245.low_ref, s32[8]{0:T(128)} %get-tuple-element.244.high_ref, s32[1]{0:T(128)} %bitcast.me_ref, ...), custom_call_target="tpu_custom_call" | custom-call | flops 32999999488 | tf_op jit(solution)/shard_map/attend_back/pallas_call | solution.py:63
  448.1 5.7 collective-permute-done.48.refs_22_
  454.6 5.6 collective-permute-done.50.refs_26_
  461.0 27.0 %feed_back.3 = (f32[512,1024]{1,0:T(8,128)}, bf16[512,256]{1,0:T(8,128)(2,1)}, bf16[512,256]{1,0:T(8,128)(2,1)}, bf16[512,256]{1,0:T(8,128)(2,1)}, bf16[512,256]{1,0:T(8,128)(2,1)}) custom-call(s32[1]{0:T(128)} %bitcast.me_ref, bf16[1024,512]{1,0:T(8,128)(2,1)} %copy-done.1, bf16[1024,512]{1,0:T(8,128)(2,1)} %get-tuple-element.196.refs_1_, ...), custom_call_target="tpu_custom_call" | custom-call | flops 19800000512 | tf_op jit(solution)/shard_map/feed_back/pallas_call | solution.py:63
  493.5 5.5 collective-permute-done.56
  503.3 31.0 %attend_back.6 = (bf16[512,384]{1,0:T(8,128)(2,1)}, bf16[512,384]{1,0:T(8,128)(2,1)}, bf16[512,384]{1,0:T(8,128)(2,1)}, bf16[512,384]{1,0:T(8,128)(2,1)}, f32[2,64,128]{2,1,0:T(8,128)}) custom-call(s32[8]{0:T(128)} %get-tuple-element.245.low_ref, s32[8]{0:T(128)} %get-tuple-element.244.high_ref, s32[1]{0:T(128)} %bitcast.me_ref, ...), custom_call_target="tpu_custom_call" | custom-call | flops 32999999488 | tf_op jit(solution)/shard_map/attend_back/pallas_call | solution.py:63
  537.9 31.1 %attend_back.7 = (bf16[512,384]{1,0:T(8,128)(2,1)}, bf16[512,384]{1,0:T(8,128)(2,1)}, bf16[512,384]{1,0:T(8,128)(2,1)}, bf16[512,384]{1,0:T(8,128)(2,1)}, f32[2,64,128]{2,1,0:T(8,128)}) custom-call(s32[8]{0:T(128)} %get-tuple-element.245.low_ref, s32[8]{0:T(128)} %get-tuple-element.244.high_ref, s32[1]{0:T(128)} %bitcast.me_ref, ...), custom_call_target="tpu_custom_call" | custom-call | flops 32999999488 | tf_op jit(solution)/shard_map/attend_back/pallas_call | solution.py:63
  573.9 4.7 collective-permute-done.67
  580.4 6.2 %collective-permute-done.68 = f32[2,64,256]{2,1,0:T(8,128)S(1)} collective-permute-done((f32[2,64,256]{2,1,0:T(8,128)S(1)}, f32[2,64,256]{2,1,0:T(8,128)S(1)}, u32[]{:S(2)}, u32[]{:S(2)}) %collective-permute-start.68) | collective-permute-done | bytes 131104 | tf_op jit(solution)/shard_map/ppermute | solution.py:788
  586.6 4.0 collective-permute-done.64.refs_5_
  594.2 7.9 %collect.1 = bf16[512,1024]{1,0:T(8,128)(2,1)} custom-call(bf16[512,384]{1,0:T(8,128)(2,1)} %get-tuple-element.171.refs_0_, bf16[512,384]{1,0:T(8,128)(2,1)} %get-tuple-element.179.refs_1_, bf16[512,384]{1,0:T(8,128)(2,1)} %copy-done.26, bf16[512,384]{1,0:T(8,128)(2,1)} %copy-done.34, bf16[512,384]{1,0:T(8,128)(2,1)} %copy-done.27, ...), custom_call_target="tpu_custom_call" | custom-call | flops 9900000256 | tf_op jit(solution)/shard_map/collect/pallas_call | solution.py:63
  (335 shorter events, 133.6 us)
Async XLA Ops:
  7.2 60.8 %all-gather.25.cloned.1.call-start = ((), (), s32[]{:S(2)}) async-start(), calls=%async_computation.7 | async-start | bytes 4718592 | tf_op jit(solution)/shard_map/all_gather | solution.py:753
  15.2 75.4 %all-gather.11.cloned.1.call-start = ((), (), s32[]{:S(2)}) async-start(), calls=%async_computation | async-start | bytes 1769472 | tf_op jit(solution)/shard_map/all_gather | solution.py:709
  56.3 115.4 %all-gather.23.cloned.1.call-start = ((), (), s32[]{:S(2)}) async-start(), calls=%async_computation.6 | async-start | bytes 4718592 | tf_op jit(solution)/shard_map/all_gather | solution.py:753
  61.0 116.3 %all-gather.13.cloned.1.call-start = ((), (), s32[]{:S(2)}) async-start(), calls=%async_computation.1 | async-start | bytes 2359296 | tf_op jit(solution)/shard_map/all_gather | solution.py:709
  61.9 196.4 %all-gather.15.cloned.1.call-start = ((), (), s32[]{:S(2)}) async-start(), calls=%async_computation.2 | async-start | bytes 1769472 | tf_op jit(solution)/shard_map/all_gather | solution.py:709
  67.7 245.8 %all-gather.17.cloned.1.call-start = ((), (), s32[]{:S(2)}) async-start(), calls=%async_computation.3 | async-start | bytes 2359296 | tf_op jit(solution)/shard_map/all_gather | solution.py:709
  71.9 59.9 %collective-permute-start.18 = (bf16[1024,512]{1,0:T(8,128)(2,1)S(1)}, bf16[1024,512]{1,0:T(8,128)(2,1)}, u32[]{:S(2)}, u32[]{:S(2)}) collective-permute-start(bf16[1024,512]{1,0:T(8,128)(2,1)S(1)} %get-tuple-element.197.refs_0_), channel_id=1, source_target_pairs={{0,1},{1,0},{2,3},{3,2},{4,5},{5,4},{6,7},{7,6},{8,9},{9,8},{10,11... | collective-permute-start | bytes 3145736 | tf_op jit(solution)/shard_map/ppermute | solution.py:692
  72.2 59.6 %collective-permute-start.20 = (bf16[1024,512]{1,0:T(8,128)(2,1)S(1)}, bf16[1024,512]{1,0:T(8,128)(2,1)}, u32[]{:S(2)}, u32[]{:S(2)}) collective-permute-start(bf16[1024,512]{1,0:T(8,128)(2,1)S(1)} %get-tuple-element.197.refs_0_), channel_id=1, source_target_pairs={{0,2},{1,3},{2,0},{3,1},{4,6},{5,7},{6,4},{7,5},{8,10},{9,11},{10,... | collective-permute-start | bytes 3145736 | tf_op jit(solution)/shard_map/ppermute | solution.py:692
  75.4 56.3 %collective-permute-start.24 = (bf16[512,1024]{1,0:T(8,128)(2,1)}, bf16[512,1024]{1,0:T(8,128)(2,1)}, u32[]{:S(2)}, u32[]{:S(2)}) collective-permute-start(bf16[512,1024]{1,0:T(8,128)(2,1)} %get-tuple-element.195.refs_8_), channel_id=1, source_target_pairs={{0,1},{1,0},{2,3},{3,2},{4,5},{5,4},{6,7},{7,6},{8,9},{9,8},{10,11... | collective-permute-start | bytes 3145736 | tf_op jit(solution)/shard_map/ppermute | solution.py:692
  76.9 54.8 %collective-permute-start.26 = (bf16[512,1024]{1,0:T(8,128)(2,1)}, bf16[512,1024]{1,0:T(8,128)(2,1)}, u32[]{:S(2)}, u32[]{:S(2)}) collective-permute-start(bf16[512,1024]{1,0:T(8,128)(2,1)} %get-tuple-element.195.refs_8_), channel_id=1, source_target_pairs={{0,2},{1,3},{2,0},{3,1},{4,6},{5,7},{6,4},{7,5},{8,10},{9,11},{10,... | collective-permute-start | bytes 3145736 | tf_op jit(solution)/shard_map/ppermute | solution.py:692
  133.3 37.8 %collective-permute-start.19 = (bf16[1024,512]{1,0:T(8,128)(2,1)}, bf16[1024,512]{1,0:T(8,128)(2,1)S(1)}, u32[]{:S(2)}, u32[]{:S(2)}) collective-permute-start(bf16[1024,512]{1,0:T(8,128)(2,1)} %collective-permute-done.18.refs_2_), channel_id=1, source_target_pairs={{0,4},{4,0},{8,12},{12,8},{16,20},{20,16},{24,28},{28,24},{1,5},{5... | collective-permute-start | bytes 3145736 | tf_op jit(solution)/shard_map/ppermute | solution.py:706
  133.3 37.9 %collective-permute-start.22 = (bf16[1024,512]{1,0:T(8,128)(2,1)}, bf16[1024,512]{1,0:T(8,128)(2,1)}, u32[]{:S(2)}, u32[]{:S(2)}) collective-permute-start(bf16[1024,512]{1,0:T(8,128)(2,1)} %collective-permute-done.20.refs_4_), channel_id=1, source_target_pairs={{0,1},{1,0},{2,3},{3,2},{4,5},{5,4},{6,7},{7,6},{8,9},{9,8},{10,11... | collective-permute-start | bytes 3145736 | tf_op jit(solution)/shard_map/ppermute | solution.py:692
  133.9 37.8 %collective-permute-start.28 = (bf16[512,1024]{1,0:T(8,128)(2,1)}, bf16[512,1024]{1,0:T(8,128)(2,1)}, u32[]{:S(2)}, u32[]{:S(2)}) collective-permute-start(bf16[512,1024]{1,0:T(8,128)(2,1)} %collective-permute-done.24.refs_10_), channel_id=1, source_target_pairs={{0,2},{1,3},{2,0},{3,1},{4,6},{5,7},{6,4},{7,5},{8,10},{9,11},{10,... | collective-permute-start | bytes 3145736 | tf_op jit(solution)/shard_map/ppermute | solution.py:692
  136.0 34.6 %collective-permute-start.31 = (bf16[512,256]{1,0:T(8,128)(2,1)}, bf16[512,256]{1,0:T(8,128)(2,1)S(1)}, u32[]{:S(2)}, u32[]{:S(2)}) collective-permute-start(bf16[512,256]{1,0:T(8,128)(2,1)} %get-tuple-element.104), channel_id=1, source_target_pairs={{0,2},{1,3},{2,0},{3,1},{4,6},{5,7},{6,4},{7,5},{8,10},{9,11},{10,... | collective-permute-start | bytes 786440 | tf_op jit(solution)/shard_map/ppermute | solution.py:692
  141.2 29.4 %collective-permute-start.32 = (bf16[512,256]{1,0:T(8,128)(2,1)}, bf16[512,256]{1,0:T(8,128)(2,1)S(1)}, u32[]{:S(2)}, u32[]{:S(2)}) collective-permute-start(bf16[512,256]{1,0:T(8,128)(2,1)} %get-tuple-element.105), channel_id=1, source_target_pairs={{0,3},{1,2},{2,1},{3,0},{4,7},{5,6},{6,5},{7,4},{8,11},{9,10},{10,... | collective-permute-start | bytes 786440 | tf_op jit(solution)/shard_map/ppermute | solution.py:692
  145.5 314.8 %all-gather.19.cloned.1.call-start = ((), (), s32[]{:S(2)}) async-start(), calls=%async_computation.4 | async-start | bytes 7077888 | tf_op jit(solution)/shard_map/all_gather | solution.py:709
  216.3 377.9 %all-gather.21.cloned.1.call-start = ((), (), s32[]{:S(2)}) async-start(), calls=%async_computation.5 | async-start | bytes 7077888 | tf_op jit(solution)/shard_map/all_gather | solution.py:709
  236.0 62.0 %collective-permute-start.8 = (bf16[1024,512]{1,0:T(8,128)(2,1)S(1)}, bf16[1024,512]{1,0:T(8,128)(2,1)}, u32[]{:S(2)}, u32[]{:S(2)}) collective-permute-start(bf16[1024,512]{1,0:T(8,128)(2,1)S(1)} %get-tuple-element.205.refs_0_), channel_id=1, source_target_pairs={{0,2},{1,3},{2,0},{3,1},{4,6},{5,7},{6,4},{7,5},{8,10},{9,11},{10,... | collective-permute-start | bytes 3145736 | tf_op jit(solution)/shard_map/ppermute | solution.py:692
  242.7 55.3 %collective-permute-start.12 = (bf16[512,1024]{1,0:T(8,128)(2,1)S(1)}, bf16[512,1024]{1,0:T(8,128)(2,1)}, u32[]{:S(2)}, u32[]{:S(2)}) collective-permute-start(bf16[512,1024]{1,0:T(8,128)(2,1)S(1)} %copy-done.4), channel_id=1, source_target_pairs={{0,1},{1,0},{2,3},{3,2},{4,5},{5,4},{6,7},{7,6},{8,9},{9,8},{10,11... | collective-permute-start | bytes 3145736 | tf_op jit(solution)/shard_map/ppermute | solution.py:692
  243.8 58.2 %collective-permute-start.7 = (bf16[1024,512]{1,0:T(8,128)(2,1)}, bf16[1024,512]{1,0:T(8,128)(2,1)}, u32[]{:S(2)}, u32[]{:S(2)}) collective-permute-start(bf16[1024,512]{1,0:T(8,128)(2,1)} %copy-done.18), channel_id=1, source_target_pairs={{0,4},{4,0},{8,12},{12,8},{16,20},{20,16},{24,28},{28,24},{1,5},{5... | collective-permute-start | bytes 3145736 | tf_op jit(solution)/shard_map/ppermute | solution.py:706
  255.0 43.5 %collective-permute-start.10 = (bf16[1024,512]{1,0:T(8,128)(2,1)}, bf16[1024,512]{1,0:T(8,128)(2,1)}, u32[]{:S(2)}, u32[]{:S(2)}) collective-permute-start(bf16[1024,512]{1,0:T(8,128)(2,1)} %copy-done.18), channel_id=1, source_target_pairs={{0,2},{1,3},{2,0},{3,1},{4,6},{5,7},{6,4},{7,5},{8,10},{9,11},{10,... | collective-permute-start | bytes 3145736 | tf_op jit(solution)/shard_map/ppermute | solution.py:692
  257.3 41.2 %collective-permute-start.16 = (bf16[512,1024]{1,0:T(8,128)(2,1)}, bf16[512,1024]{1,0:T(8,128)(2,1)}, u32[]{:S(2)}, u32[]{:S(2)}) collective-permute-start(bf16[512,1024]{1,0:T(8,128)(2,1)} %collective-permute-done.14.refs_12_), channel_id=1, source_target_pairs={{0,1},{1,0},{2,3},{3,2},{4,5},{5,4},{6,7},{7,6},{8,9},{9,8},{10,11... | collective-permute-start | bytes 3145736 | tf_op jit(solution)/shard_map/ppermute | solution.py:692
  406.8 34.6 %collective-permute-start.45 = (bf16[512,384]{1,0:T(8,128)(2,1)}, bf16[512,384]{1,0:T(8,128)(2,1)S(1)}, u32[]{:S(2)}, u32[]{:S(2)}) collective-permute-start(bf16[512,384]{1,0:T(8,128)(2,1)} %get-tuple-element.143), channel_id=1, source_target_pairs={{0,1},{1,0},{2,3},{3,2},{4,5},{5,4},{6,7},{7,6},{8,9},{9,8},{10,11... | collective-permute-start | bytes 1179656 | tf_op jit(solution)/shard_map/ppermute | solution.py:692
  407.9 33.5 %collective-permute-start.46 = (bf16[512,384]{1,0:T(8,128)(2,1)}, bf16[512,384]{1,0:T(8,128)(2,1)S(1)}, u32[]{:S(2)}, u32[]{:S(2)}) collective-permute-start(bf16[512,384]{1,0:T(8,128)(2,1)} %get-tuple-element.144), channel_id=1, source_target_pairs={{0,2},{1,3},{2,0},{3,1},{4,6},{5,7},{6,4},{7,5},{8,10},{9,11},{10,... | collective-permute-start | bytes 1179656 | tf_op jit(solution)/shard_map/ppermute | solution.py:692
  408.9 32.6 %collective-permute-start.47 = (bf16[512,384]{1,0:T(8,128)(2,1)}, bf16[512,384]{1,0:T(8,128)(2,1)S(1)}, u32[]{:S(2)}, u32[]{:S(2)}) collective-permute-start(bf16[512,384]{1,0:T(8,128)(2,1)} %get-tuple-element.145), channel_id=1, source_target_pairs={{0,3},{1,2},{2,1},{3,0},{4,7},{5,6},{6,5},{7,4},{8,11},{9,10},{10,... | collective-permute-start | bytes 1179656 | tf_op jit(solution)/shard_map/ppermute | solution.py:692
  447.2 44.4 %collective-permute-start.55 = (f32[2,64,256]{2,1,0:T(8,128)S(1)}, f32[2,64,256]{2,1,0:T(8,128)S(1)}, u32[]{:S(2)}, u32[]{:S(2)}) collective-permute-start(f32[2,64,256]{2,1,0:T(8,128)S(1)} %add.89), channel_id=1, source_target_pairs={{0,8},{4,12},{8,0},{12,4},{16,24},{20,28},{24,16},{28,20},{1,9},{5... | collective-permute-start | bytes 393224 | tf_op jit(solution)/shard_map/ppermute | solution.py:788
  499.0 35.4 %collective-permute-start.57 = (f32[2,64,256]{2,1,0:T(8,128)S(1)}, f32[2,64,256]{2,1,0:T(8,128)S(1)}, u32[]{:S(2)}, u32[]{:S(2)}) collective-permute-start(f32[2,64,256]{2,1,0:T(8,128)S(1)} %add.91), channel_id=1, source_target_pairs={{0,1},{1,0},{2,3},{3,2},{4,5},{5,4},{6,7},{7,6},{8,9},{9,8},{10,11... | collective-permute-start | bytes 393224 | tf_op jit(solution)/shard_map/ppermute | solution.py:692
  499.8 34.5 %collective-permute-start.58 = (f32[2,64,256]{2,1,0:T(8,128)S(1)}, f32[2,64,256]{2,1,0:T(8,128)S(1)}, u32[]{:S(2)}, u32[]{:S(2)}) collective-permute-start(f32[2,64,256]{2,1,0:T(8,128)S(1)} %add.91), channel_id=1, source_target_pairs={{0,2},{1,3},{2,0},{3,1},{4,6},{5,7},{6,4},{7,5},{8,10},{9,11},{10,... | collective-permute-start | bytes 393224 | tf_op jit(solution)/shard_map/ppermute | solution.py:692
  501.5 32.9 %collective-permute-start.59 = (f32[2,64,256]{2,1,0:T(8,128)S(1)}, f32[2,64,256]{2,1,0:T(8,128)S(1)}, u32[]{:S(2)}, u32[]{:S(2)}) collective-permute-start(f32[2,64,256]{2,1,0:T(8,128)S(1)} %add.91), channel_id=1, source_target_pairs={{0,3},{1,2},{2,1},{3,0},{4,7},{5,6},{6,5},{7,4},{8,11},{9,10},{10,... | collective-permute-start | bytes 393224 | tf_op jit(solution)/shard_map/ppermute | solution.py:692
  534.4 35.5 %collective-permute-start.60 = (bf16[512,384]{1,0:T(8,128)(2,1)}, bf16[512,384]{1,0:T(8,128)(2,1)S(1)}, u32[]{:S(2)}, u32[]{:S(2)}) collective-permute-start(bf16[512,384]{1,0:T(8,128)(2,1)} %get-tuple-element.176), channel_id=1, source_target_pairs={{0,1},{1,0},{2,3},{3,2},{4,5},{5,4},{6,7},{7,6},{8,9},{9,8},{10,11... | collective-permute-start | bytes 1179656 | tf_op jit(solution)/shard_map/ppermute | solution.py:692
  535.2 34.7 %collective-permute-start.61 = (bf16[512,384]{1,0:T(8,128)(2,1)}, bf16[512,384]{1,0:T(8,128)(2,1)S(1)}, u32[]{:S(2)}, u32[]{:S(2)}) collective-permute-start(bf16[512,384]{1,0:T(8,128)(2,1)} %get-tuple-element.177), channel_id=1, source_target_pairs={{0,2},{1,3},{2,0},{3,1},{4,6},{5,7},{6,4},{7,5},{8,10},{9,11},{10,... | collective-permute-start | bytes 1179656 | tf_op jit(solution)/shard_map/ppermute | solution.py:692
  536.9 33.0 %collective-permute-start.62 = (bf16[512,384]{1,0:T(8,128)(2,1)}, bf16[512,384]{1,0:T(8,128)(2,1)S(1)}, u32[]{:S(2)}, u32[]{:S(2)}) collective-permute-start(bf16[512,384]{1,0:T(8,128)(2,1)} %get-tuple-element.178), channel_id=1, source_target_pairs={{0,3},{1,2},{2,1},{3,0},{4,7},{5,6},{6,5},{7,4},{8,11},{9,10},{10,... | collective-permute-start | bytes 1179656 | tf_op jit(solution)/shard_map/ppermute | solution.py:692
  (98 other events, 1458.4 us)
Sparse Core Ops, SparseCore 0:
  15.3 49.8 all-gather.24
  66.8 23.7 all-gather.10
  92.8 46.6 all-gather.22
  141.0 27.8 all-gather.12
  170.3 24.5 all-gather.14
  196.4 28.6 all-gather.16
  226.7 64.2 all-gather.18
  364.5 64.0 all-gather.20

commit v5 on v4

--- a/solution.py
+++ b/solution.py
@@ -306,7 +306,7 @@
     prefix_ref[1] = pv_sum[...]
 
     def key_step(j, carry):
-        place = pl.ds(pl.multiple_of(j * 2 * BLOCK, 2 * BLOCK), 2 * BLOCK)
+        place = pl.ds(pl.multiple_of(j * 4 * BLOCK, 4 * BLOCK), 4 * BLOCK)
         k_sum[...] = jnp.zeros_like(k_sum)
         v_sum[...] = jnp.zeros_like(v_sum)
         keys = k_ref[place, :]
@@ -318,12 +318,12 @@
             pair_of_blocks(i, keys, values, keys_turned, seen, k_sum, v_sum)
             return carry
 
-        lax.fori_loop(low_ref[2 * j], high_ref[2 * j + 1], query_step, 0)
+        lax.fori_loop(low_ref[4 * j], high_ref[4 * j + 3], query_step, 0)
         grads_ref[place, width : 2 * width] = (k_sum[...] * LN_2).astype(jnp.bfloat16)
         grads_ref[place, 2 * width :] = v_sum[...].astype(jnp.bfloat16)
         return carry
 
-    lax.fori_loop(0, blocks // 2, key_step, 0)
+    lax.fori_loop(0, blocks // 4, key_step, 0)
     grads_ref[:, :width] = (q_sum[...] * SCALE).T.astype(jnp.bfloat16)
     for step, result_ref in enumerate(results):
         result_ref[...] = grads_ref[rows_of(step), :]
@@ -360,8 +360,8 @@
             pltpu.VMEM((width, rows), jnp.bfloat16),
             pltpu.VMEM((width, rows), jnp.float32),
             pltpu.VMEM((1, count * rows), jnp.float32),
-            pltpu.VMEM((2 * BLOCK, width), jnp.float32),
-            pltpu.VMEM((2 * BLOCK, width), jnp.float32),
+            pltpu.VMEM((4 * BLOCK, width), jnp.float32),
+            pltpu.VMEM((4 * BLOCK, width), jnp.float32),
             pltpu.VMEM((prefix, width), jnp.float32),
             pltpu.VMEM((prefix, width), jnp.float32),
         ],

time: 616 us -> 613 us (level)
  no operation moved by 1% of the time
where the time goes in v5:
time: 613 us; the launch traced here: 608 us
  Pallas kernels  308 us (50%)
  waiting for transfers between devices  154 us (25%)
  starting transfers between devices  73.5 us (12%)
  local copies, waits for them, and re-layouts  48.7 us (8%)
  between operations  15.6 us (3%)
  other arithmetic  7.28 us (1%)
    pallas_call x13, Pallas kernels, scalar_call(): pl.pallas_call(kernel, grid_spec=pltpu.PrefetchScalarGridSpec(num_scalar_...  308 us
    ppermute x54, waiting for transfers between devices, swap(): return lax.ppermute(value, 'seq', [(i, i ^ step) for i in range(seq_count)])  123 us
    ppermute x54, starting transfers between devices, swap(): return lax.ppermute(value, 'seq', [(i, i ^ step) for i in range(seq_count)])  65.1 us
    ppermute x6, waiting for transfers between devices, over_dp_swap(): return lax.ppermute(value, 'dp', [(i, i ^ bit) for i in range(dp_count)])  17.2 us
    all_gather x6, waiting for transfers between devices, gather(): return lax.all_gather(value, 'dp', axis=0, tiled=True)  13.2 us
  transfers between devices with their start and end apart: 80, of which 24 were waited for; matrix products, arithmetic and copies ran while one was open for 7% of the time, Pallas kernels for 51%

profile of v5, /device:TPU:0, one launch (start us, length us, event | category | flops | bytes accessed | tf_op | source)
XLA Modules:
  0.0 607.5 jit_solution(17219276205856750140)
XLA Ops:
  16.3 2.9 collective-permute-start
  21.3 11.0 %collective-permute-done.refs_2_ = bf16[256,1024]{1,0:T(8,128)(2,1)} collective-permute-done((bf16[256,1024]{1,0:T(8,128)(2,1)}, bf16[256,1024]{1,0:T(8,128)(2,1)}, u32[]{:S(2)}, u32[]{:S(2)}) %collective-permute-start) | collective-permute-done | bytes 524320 | tf_op jit(solution)/shard_map/ppermute | solution.py:692
  38.2 7.5 %collective-permute-done.1.refs_4_ = bf16[256,1024]{1,0:T(8,128)(2,1)} collective-permute-done((bf16[256,1024]{1,0:T(8,128)(2,1)}, bf16[256,1024]{1,0:T(8,128)(2,1)}, u32[]{:S(2)}, u32[]{:S(2)}) %collective-permute-start.1) | collective-permute-done | bytes 524320 | tf_op jit(solution)/shard_map/ppermute | solution.py:692
  45.6 9.8 %collective-permute-done.2.refs_6_ = bf16[256,1024]{1,0:T(8,128)(2,1)} collective-permute-done((bf16[256,1024]{1,0:T(8,128)(2,1)}, bf16[256,1024]{1,0:T(8,128)(2,1)}, u32[]{:S(2)}, u32[]{:S(2)}) %collective-permute-start.2) | collective-permute-done | bytes 524320 | tf_op jit(solution)/shard_map/ppermute | solution.py:692
  77.5 13.2 %all-gather.11.cloned.1.call-done.refs_8_ = bf16[1024,768]{1,0:T(8,128)(2,1)} async-done(((bf16[128,768]{1,0:T(8,128)(2,1)}), bf16[1024,768]{1,0:T(8,128)(2,1)}) %all-gather.11.cloned.1.call-update) | async-done | bytes 1572880 | tf_op jit(solution)/shard_map/all_gather | solution.py:709
  92.0 39.8 %attend.2 = (bf16[512,256]{1,0:T(8,128)(2,1)}, bf16[512,256]{1,0:T(8,128)(2,1)}, bf16[512,256]{1,0:T(8,128)(2,1)}, bf16[512,256]{1,0:T(8,128)(2,1)}, f32[256,204...) custom-call(s32[8]{0:T(128)} %get-tuple-element.245.low_ref, ...), custom_call_target="tpu_custom_call" | custom-call | flops 44000002048 | tf_op jit(solution)/shard_map/attend/pallas_call | solution.py:63
  136.5 4.7 collective-permute-done.30.refs_1_
  145.9 24.7 %collective-permute-done.31.refs_2_ = bf16[512,256]{1,0:T(8,128)(2,1)S(1)} collective-permute-done((bf16[512,256]{1,0:T(8,128)(2,1)}, bf16[512,256]{1,0:T(8,128)(2,1)S(1)}, u32[]{:S(2)}, u32[]{:S(2)}) %collective-permute-start.31) | collective-permute-done | bytes 262176 | tf_op jit(solution)/shard_map/ppermute | solution.py:692
  177.3 5.5 mix.2
  185.9 22.5 %feed.2 = (bf16[256,1024]{1,0:T(8,128)(2,1)}, bf16[256,1024]{1,0:T(8,128)(2,1)}, bf16[512,4096]{1,0:T(8,128)(2,1)}, f32[512,1024]{1,0:T(8,128)}, f32[512,1]{1,0:T(8,128)}) custom-call(s32[1]{0:T(128)} %bitcast.me_ref, s32[1]{0:T(128)} %bitcast.1.core_ref, bf16[1024,512]{1,0:T(8,128)(2,1)} %copy-done.1, bf16[1024,512]{1,0:T(8,128)(2,1)} %get-tuple-element.196.refs_1_, ...), custom_call_target="tpu_custom_call" | custom-call | flops 24199999488 | tf_op jit(solution)/shard_map/feed/pallas_call | solution.py:63
  220.5 11.0 %collective-permute-done.33.refs_2_ = bf16[256,1024]{1,0:T(8,128)(2,1)S(1)} collective-permute-done((bf16[256,1024]{1,0:T(8,128)(2,1)}, bf16[256,1024]{1,0:T(8,128)(2,1)S(1)}, u32[]{:S(2)}, u32[]{:S(2)}) %collective-permute-start.33) | collective-permute-done | bytes 524320 | tf_op jit(solution)/shard_map/ppermute | solution.py:692
  237.0 5.7 collective-permute-done.34.refs_3_
  243.8 11.2 %collective-permute-done.37.refs_6_ = bf16[256,1024]{1,0:T(8,128)(2,1)S(1)} collective-permute-done((bf16[256,1024]{1,0:T(8,128)(2,1)S(1)}, bf16[256,1024]{1,0:T(8,128)(2,1)S(1)}, u32[]{:S(2)}, u32[]{:S(2)}) %collective-permute-start.37) | collective-permute-done | bytes 524320 | tf_op jit(solution)/shard_map/ppermute | solution.py:692
  258.3 39.7 %attend.3 = (bf16[512,256]{1,0:T(8,128)(2,1)}, bf16[512,256]{1,0:T(8,128)(2,1)}, bf16[512,256]{1,0:T(8,128)(2,1)}, bf16[512,256]{1,0:T(8,128)(2,1)}, f32[256,204...) custom-call(s32[8]{0:T(128)} %get-tuple-element.245.low_ref, ...), custom_call_target="tpu_custom_call" | custom-call | flops 44000002048 | tf_op jit(solution)/shard_map/attend/pallas_call | solution.py:63
  302.5 5.4 collective-permute-done.39.refs_1_
  313.5 5.3 mix.3
  319.9 22.7 %feed.3 = (bf16[512,1024]{1,0:T(8,128)(2,1)}, bf16[512,4096]{1,0:T(8,128)(2,1)}, f32[512,1024]{1,0:T(8,128)}, f32[512,1]{1,0:T(8,128)}) custom-call(s32[1]{0:T(128)} %bitcast.me_ref, s32[1]{0:T(128)} %bitcast.1.core_ref, bf16[1024,512]{1,0:T(8,128)(2,1)} %copy-done.2, bf16[1024,512]{1,0:T(8,128)(2,1)} %get-tuple-element.204.refs_1_, ...), custom_call_target="tpu_custom_call" | custom-call | flops 24199999488 | tf_op jit(solution)/shard_map/feed/pallas_call | solution.py:63
  342.5 17.3 %feed_back.2 = (f32[512,1024]{1,0:T(8,128)}, bf16[512,256]{1,0:T(8,128)(2,1)}, bf16[512,256]{1,0:T(8,128)(2,1)}, bf16[512,256]{1,0:T(8,128)(2,1)}, bf16[512,256]{1,0:T(8,128)(2,1)}) custom-call(s32[1]{0:T(128)} %bitcast.me_ref, bf16[1024,512]{1,0:T(8,128)(2,1)} %copy-done.2, bf16[1024,512]{1,0:T(8,128)(2,1)} %get-tuple-element.204.refs_1_, ...), custom_call_target="tpu_custom_call" | custom-call | flops 19800000512 | tf_op jit(solution)/shard_map/feed_back/pallas_call | solution.py:63
  364.4 4.8 collective-permute-done.42.refs_1_
  369.2 5.8 collective-permute-done.43.refs_2_
  375.8 30.0 %attend_back.4 = (bf16[512,384]{1,0:T(8,128)(2,1)}, bf16[512,384]{1,0:T(8,128)(2,1)}, bf16[512,384]{1,0:T(8,128)(2,1)}, bf16[512,384]{1,0:T(8,128)(2,1)}, f32[2,64,128]{2,1,0:T(8,128)}) custom-call(s32[8]{0:T(128)} %get-tuple-element.245.low_ref, s32[8]{0:T(128)} %get-tuple-element.244.high_ref, s32[1]{0:T(128)} %bitcast.me_ref, ...), custom_call_target="tpu_custom_call" | custom-call | flops 32999999488 | tf_op jit(solution)/shard_map/attend_back/pallas_call | solution.py:63
  409.3 30.3 %attend_back.5 = (bf16[512,384]{1,0:T(8,128)(2,1)}, bf16[512,384]{1,0:T(8,128)(2,1)}, bf16[512,384]{1,0:T(8,128)(2,1)}, bf16[512,384]{1,0:T(8,128)(2,1)}, f32[2,64,128]{2,1,0:T(8,128)}) custom-call(s32[8]{0:T(128)} %get-tuple-element.245.low_ref, s32[8]{0:T(128)} %get-tuple-element.244.high_ref, s32[1]{0:T(128)} %bitcast.me_ref, ...), custom_call_target="tpu_custom_call" | custom-call | flops 32999999488 | tf_op jit(solution)/shard_map/attend_back/pallas_call | solution.py:63
  446.8 5.2 collective-permute-done.48.refs_22_
  452.0 4.9 collective-permute-done.49.refs_24_
  459.3 27.0 %feed_back.3 = (f32[512,1024]{1,0:T(8,128)}, bf16[512,256]{1,0:T(8,128)(2,1)}, bf16[512,256]{1,0:T(8,128)(2,1)}, bf16[512,256]{1,0:T(8,128)(2,1)}, bf16[512,256]{1,0:T(8,128)(2,1)}) custom-call(s32[1]{0:T(128)} %bitcast.me_ref, bf16[1024,512]{1,0:T(8,128)(2,1)} %copy-done.1, bf16[1024,512]{1,0:T(8,128)(2,1)} %get-tuple-element.196.refs_1_, ...), custom_call_target="tpu_custom_call" | custom-call | flops 19800000512 | tf_op jit(solution)/shard_map/feed_back/pallas_call | solution.py:63
  491.7 5.5 collective-permute-done.56
  501.6 30.0 %attend_back.6 = (bf16[512,384]{1,0:T(8,128)(2,1)}, bf16[512,384]{1,0:T(8,128)(2,1)}, bf16[512,384]{1,0:T(8,128)(2,1)}, bf16[512,384]{1,0:T(8,128)(2,1)}, f32[2,64,128]{2,1,0:T(8,128)}) custom-call(s32[8]{0:T(128)} %get-tuple-element.245.low_ref, s32[8]{0:T(128)} %get-tuple-element.244.high_ref, s32[1]{0:T(128)} %bitcast.me_ref, ...), custom_call_target="tpu_custom_call" | custom-call | flops 32999999488 | tf_op jit(solution)/shard_map/attend_back/pallas_call | solution.py:63
  535.2 30.4 %attend_back.7 = (bf16[512,384]{1,0:T(8,128)(2,1)}, bf16[512,384]{1,0:T(8,128)(2,1)}, bf16[512,384]{1,0:T(8,128)(2,1)}, bf16[512,384]{1,0:T(8,128)(2,1)}, f32[2,64,128]{2,1,0:T(8,128)}) custom-call(s32[8]{0:T(128)} %get-tuple-element.245.low_ref, s32[8]{0:T(128)} %get-tuple-element.244.high_ref, s32[1]{0:T(128)} %bitcast.me_ref, ...), custom_call_target="tpu_custom_call" | custom-call | flops 32999999488 | tf_op jit(solution)/shard_map/attend_back/pallas_call | solution.py:63
  571.1 4.1 collective-permute-done.67
  576.9 6.3 %collective-permute-done.68 = f32[2,64,256]{2,1,0:T(8,128)S(1)} collective-permute-done((f32[2,64,256]{2,1,0:T(8,128)S(1)}, f32[2,64,256]{2,1,0:T(8,128)S(1)}, u32[]{:S(2)}, u32[]{:S(2)}) %collective-permute-start.68) | collective-permute-done | bytes 131104 | tf_op jit(solution)/shard_map/ppermute | solution.py:788
  583.2 4.0 collective-permute-done.64.refs_5_
  590.8 7.9 %collect.1 = bf16[512,1024]{1,0:T(8,128)(2,1)} custom-call(bf16[512,384]{1,0:T(8,128)(2,1)} %get-tuple-element.171.refs_0_, bf16[512,384]{1,0:T(8,128)(2,1)} %get-tuple-element.179.refs_1_, bf16[512,384]{1,0:T(8,128)(2,1)} %copy-done.26, bf16[512,384]{1,0:T(8,128)(2,1)} %copy-done.34, bf16[512,384]{1,0:T(8,128)(2,1)} %copy-done.27, ...), custom_call_target="tpu_custom_call" | custom-call | flops 9900000256 | tf_op jit(solution)/shard_map/collect/pallas_call | solution.py:63
  (335 shorter events, 135.8 us)
Async XLA Ops:
  7.2 60.8 %all-gather.25.cloned.1.call-start = ((), (), s32[]{:S(2)}) async-start(), calls=%async_computation.7 | async-start | bytes 4718592 | tf_op jit(solution)/shard_map/all_gather | solution.py:753
  15.2 75.4 %all-gather.11.cloned.1.call-start = ((), (), s32[]{:S(2)}) async-start(), calls=%async_computation | async-start | bytes 1769472 | tf_op jit(solution)/shard_map/all_gather | solution.py:709
  56.3 115.4 %all-gather.23.cloned.1.call-start = ((), (), s32[]{:S(2)}) async-start(), calls=%async_computation.6 | async-start | bytes 4718592 | tf_op jit(solution)/shard_map/all_gather | solution.py:753
  61.0 116.3 %all-gather.13.cloned.1.call-start = ((), (), s32[]{:S(2)}) async-start(), calls=%async_computation.1 | async-start | bytes 2359296 | tf_op jit(solution)/shard_map/all_gather | solution.py:709
  61.9 196.4 %all-gather.15.cloned.1.call-start = ((), (), s32[]{:S(2)}) async-start(), calls=%async_computation.2 | async-start | bytes 1769472 | tf_op jit(solution)/shard_map/all_gather | solution.py:709
  67.7 245.8 %all-gather.17.cloned.1.call-start = ((), (), s32[]{:S(2)}) async-start(), calls=%async_computation.3 | async-start | bytes 2359296 | tf_op jit(solution)/shard_map/all_gather | solution.py:709
  71.9 59.8 %collective-permute-start.18 = (bf16[1024,512]{1,0:T(8,128)(2,1)S(1)}, bf16[1024,512]{1,0:T(8,128)(2,1)}, u32[]{:S(2)}, u32[]{:S(2)}) collective-permute-start(bf16[1024,512]{1,0:T(8,128)(2,1)S(1)} %get-tuple-element.197.refs_0_), channel_id=1, source_target_pairs={{0,1},{1,0},{2,3},{3,2},{4,5},{5,4},{6,7},{7,6},{8,9},{9,8},{10,11... | collective-permute-start | bytes 3145736 | tf_op jit(solution)/shard_map/ppermute | solution.py:692
  72.2 59.5 %collective-permute-start.20 = (bf16[1024,512]{1,0:T(8,128)(2,1)S(1)}, bf16[1024,512]{1,0:T(8,128)(2,1)}, u32[]{:S(2)}, u32[]{:S(2)}) collective-permute-start(bf16[1024,512]{1,0:T(8,128)(2,1)S(1)} %get-tuple-element.197.refs_0_), channel_id=1, source_target_pairs={{0,2},{1,3},{2,0},{3,1},{4,6},{5,7},{6,4},{7,5},{8,10},{9,11},{10,... | collective-permute-start | bytes 3145736 | tf_op jit(solution)/shard_map/ppermute | solution.py:692
  75.5 56.3 %collective-permute-start.24 = (bf16[512,1024]{1,0:T(8,128)(2,1)}, bf16[512,1024]{1,0:T(8,128)(2,1)}, u32[]{:S(2)}, u32[]{:S(2)}) collective-permute-start(bf16[512,1024]{1,0:T(8,128)(2,1)} %get-tuple-element.195.refs_8_), channel_id=1, source_target_pairs={{0,1},{1,0},{2,3},{3,2},{4,5},{5,4},{6,7},{7,6},{8,9},{9,8},{10,11... | collective-permute-start | bytes 3145736 | tf_op jit(solution)/shard_map/ppermute | solution.py:692
  77.0 54.8 %collective-permute-start.26 = (bf16[512,1024]{1,0:T(8,128)(2,1)}, bf16[512,1024]{1,0:T(8,128)(2,1)}, u32[]{:S(2)}, u32[]{:S(2)}) collective-permute-start(bf16[512,1024]{1,0:T(8,128)(2,1)} %get-tuple-element.195.refs_8_), channel_id=1, source_target_pairs={{0,2},{1,3},{2,0},{3,1},{4,6},{5,7},{6,4},{7,5},{8,10},{9,11},{10,... | collective-permute-start | bytes 3145736 | tf_op jit(solution)/shard_map/ppermute | solution.py:692
  133.3 37.8 %collective-permute-start.19 = (bf16[1024,512]{1,0:T(8,128)(2,1)}, bf16[1024,512]{1,0:T(8,128)(2,1)S(1)}, u32[]{:S(2)}, u32[]{:S(2)}) collective-permute-start(bf16[1024,512]{1,0:T(8,128)(2,1)} %collective-permute-done.18.refs_2_), channel_id=1, source_target_pairs={{0,4},{4,0},{8,12},{12,8},{16,20},{20,16},{24,28},{28,24},{1,5},{5... | collective-permute-start | bytes 3145736 | tf_op jit(solution)/shard_map/ppermute | solution.py:706
  133.3 37.9 %collective-permute-start.22 = (bf16[1024,512]{1,0:T(8,128)(2,1)}, bf16[1024,512]{1,0:T(8,128)(2,1)}, u32[]{:S(2)}, u32[]{:S(2)}) collective-permute-start(bf16[1024,512]{1,0:T(8,128)(2,1)} %collective-permute-done.20.refs_4_), channel_id=1, source_target_pairs={{0,1},{1,0},{2,3},{3,2},{4,5},{5,4},{6,7},{7,6},{8,9},{9,8},{10,11... | collective-permute-start | bytes 3145736 | tf_op jit(solution)/shard_map/ppermute | solution.py:692
  133.9 37.8 %collective-permute-start.28 = (bf16[512,1024]{1,0:T(8,128)(2,1)}, bf16[512,1024]{1,0:T(8,128)(2,1)}, u32[]{:S(2)}, u32[]{:S(2)}) collective-permute-start(bf16[512,1024]{1,0:T(8,128)(2,1)} %collective-permute-done.24.refs_10_), channel_id=1, source_target_pairs={{0,2},{1,3},{2,0},{3,1},{4,6},{5,7},{6,4},{7,5},{8,10},{9,11},{10,... | collective-permute-start | bytes 3145736 | tf_op jit(solution)/shard_map/ppermute | solution.py:692
  136.0 34.6 %collective-permute-start.31 = (bf16[512,256]{1,0:T(8,128)(2,1)}, bf16[512,256]{1,0:T(8,128)(2,1)S(1)}, u32[]{:S(2)}, u32[]{:S(2)}) collective-permute-start(bf16[512,256]{1,0:T(8,128)(2,1)} %get-tuple-element.104), channel_id=1, source_target_pairs={{0,2},{1,3},{2,0},{3,1},{4,6},{5,7},{6,4},{7,5},{8,10},{9,11},{10,... | collective-permute-start | bytes 786440 | tf_op jit(solution)/shard_map/ppermute | solution.py:692
  141.2 29.4 %collective-permute-start.32 = (bf16[512,256]{1,0:T(8,128)(2,1)}, bf16[512,256]{1,0:T(8,128)(2,1)S(1)}, u32[]{:S(2)}, u32[]{:S(2)}) collective-permute-start(bf16[512,256]{1,0:T(8,128)(2,1)} %get-tuple-element.105), channel_id=1, source_target_pairs={{0,3},{1,2},{2,1},{3,0},{4,7},{5,6},{6,5},{7,4},{8,11},{9,10},{10,... | collective-permute-start | bytes 786440 | tf_op jit(solution)/shard_map/ppermute | solution.py:692
  145.5 313.1 %all-gather.19.cloned.1.call-start = ((), (), s32[]{:S(2)}) async-start(), calls=%async_computation.4 | async-start | bytes 7077888 | tf_op jit(solution)/shard_map/all_gather | solution.py:709
  216.3 374.5 %all-gather.21.cloned.1.call-start = ((), (), s32[]{:S(2)}) async-start(), calls=%async_computation.5 | async-start | bytes 7077888 | tf_op jit(solution)/shard_map/all_gather | solution.py:709
  236.0 62.1 %collective-permute-start.8 = (bf16[1024,512]{1,0:T(8,128)(2,1)S(1)}, bf16[1024,512]{1,0:T(8,128)(2,1)}, u32[]{:S(2)}, u32[]{:S(2)}) collective-permute-start(bf16[1024,512]{1,0:T(8,128)(2,1)S(1)} %get-tuple-element.205.refs_0_), channel_id=1, source_target_pairs={{0,2},{1,3},{2,0},{3,1},{4,6},{5,7},{6,4},{7,5},{8,10},{9,11},{10,... | collective-permute-start | bytes 3145736 | tf_op jit(solution)/shard_map/ppermute | solution.py:692
  242.7 55.3 %collective-permute-start.12 = (bf16[512,1024]{1,0:T(8,128)(2,1)S(1)}, bf16[512,1024]{1,0:T(8,128)(2,1)}, u32[]{:S(2)}, u32[]{:S(2)}) collective-permute-start(bf16[512,1024]{1,0:T(8,128)(2,1)S(1)} %copy-done.4), channel_id=1, source_target_pairs={{0,1},{1,0},{2,3},{3,2},{4,5},{5,4},{6,7},{7,6},{8,9},{9,8},{10,11... | collective-permute-start | bytes 3145736 | tf_op jit(solution)/shard_map/ppermute | solution.py:692
  243.8 58.2 %collective-permute-start.7 = (bf16[1024,512]{1,0:T(8,128)(2,1)}, bf16[1024,512]{1,0:T(8,128)(2,1)}, u32[]{:S(2)}, u32[]{:S(2)}) collective-permute-start(bf16[1024,512]{1,0:T(8,128)(2,1)} %copy-done.18), channel_id=1, source_target_pairs={{0,4},{4,0},{8,12},{12,8},{16,20},{20,16},{24,28},{28,24},{1,5},{5... | collective-permute-start | bytes 3145736 | tf_op jit(solution)/shard_map/ppermute | solution.py:706
  255.0 43.5 %collective-permute-start.10 = (bf16[1024,512]{1,0:T(8,128)(2,1)}, bf16[1024,512]{1,0:T(8,128)(2,1)}, u32[]{:S(2)}, u32[]{:S(2)}) collective-permute-start(bf16[1024,512]{1,0:T(8,128)(2,1)} %copy-done.18), channel_id=1, source_target_pairs={{0,2},{1,3},{2,0},{3,1},{4,6},{5,7},{6,4},{7,5},{8,10},{9,11},{10,... | collective-permute-start | bytes 3145736 | tf_op jit(solution)/shard_map/ppermute | solution.py:692
  257.3 41.2 %collective-permute-start.16 = (bf16[512,1024]{1,0:T(8,128)(2,1)}, bf16[512,1024]{1,0:T(8,128)(2,1)}, u32[]{:S(2)}, u32[]{:S(2)}) collective-permute-start(bf16[512,1024]{1,0:T(8,128)(2,1)} %collective-permute-done.14.refs_12_), channel_id=1, source_target_pairs={{0,1},{1,0},{2,3},{3,2},{4,5},{5,4},{6,7},{7,6},{8,9},{9,8},{10,11... | collective-permute-start | bytes 3145736 | tf_op jit(solution)/shard_map/ppermute | solution.py:692
  405.8 33.8 %collective-permute-start.45 = (bf16[512,384]{1,0:T(8,128)(2,1)}, bf16[512,384]{1,0:T(8,128)(2,1)S(1)}, u32[]{:S(2)}, u32[]{:S(2)}) collective-permute-start(bf16[512,384]{1,0:T(8,128)(2,1)} %get-tuple-element.143), channel_id=1, source_target_pairs={{0,1},{1,0},{2,3},{3,2},{4,5},{5,4},{6,7},{7,6},{8,9},{9,8},{10,11... | collective-permute-start | bytes 1179656 | tf_op jit(solution)/shard_map/ppermute | solution.py:692
  406.9 32.7 %collective-permute-start.46 = (bf16[512,384]{1,0:T(8,128)(2,1)}, bf16[512,384]{1,0:T(8,128)(2,1)S(1)}, u32[]{:S(2)}, u32[]{:S(2)}) collective-permute-start(bf16[512,384]{1,0:T(8,128)(2,1)} %get-tuple-element.144), channel_id=1, source_target_pairs={{0,2},{1,3},{2,0},{3,1},{4,6},{5,7},{6,4},{7,5},{8,10},{9,11},{10,... | collective-permute-start | bytes 1179656 | tf_op jit(solution)/shard_map/ppermute | solution.py:692
  407.9 31.8 %collective-permute-start.47 = (bf16[512,384]{1,0:T(8,128)(2,1)}, bf16[512,384]{1,0:T(8,128)(2,1)S(1)}, u32[]{:S(2)}, u32[]{:S(2)}) collective-permute-start(bf16[512,384]{1,0:T(8,128)(2,1)} %get-tuple-element.145), channel_id=1, source_target_pairs={{0,3},{1,2},{2,1},{3,0},{4,7},{5,6},{6,5},{7,4},{8,11},{9,10},{10,... | collective-permute-start | bytes 1179656 | tf_op jit(solution)/shard_map/ppermute | solution.py:692
  445.4 44.5 %collective-permute-start.55 = (f32[2,64,256]{2,1,0:T(8,128)S(1)}, f32[2,64,256]{2,1,0:T(8,128)S(1)}, u32[]{:S(2)}, u32[]{:S(2)}) collective-permute-start(f32[2,64,256]{2,1,0:T(8,128)S(1)} %add.89), channel_id=1, source_target_pairs={{0,8},{4,12},{8,0},{12,4},{16,24},{20,28},{24,16},{28,20},{1,9},{5... | collective-permute-start | bytes 393224 | tf_op jit(solution)/shard_map/ppermute | solution.py:788
  497.2 34.4 %collective-permute-start.57 = (f32[2,64,256]{2,1,0:T(8,128)S(1)}, f32[2,64,256]{2,1,0:T(8,128)S(1)}, u32[]{:S(2)}, u32[]{:S(2)}) collective-permute-start(f32[2,64,256]{2,1,0:T(8,128)S(1)} %add.91), channel_id=1, source_target_pairs={{0,1},{1,0},{2,3},{3,2},{4,5},{5,4},{6,7},{7,6},{8,9},{9,8},{10,11... | collective-permute-start | bytes 393224 | tf_op jit(solution)/shard_map/ppermute | solution.py:692
  498.1 33.5 %collective-permute-start.58 = (f32[2,64,256]{2,1,0:T(8,128)S(1)}, f32[2,64,256]{2,1,0:T(8,128)S(1)}, u32[]{:S(2)}, u32[]{:S(2)}) collective-permute-start(f32[2,64,256]{2,1,0:T(8,128)S(1)} %add.91), channel_id=1, source_target_pairs={{0,2},{1,3},{2,0},{3,1},{4,6},{5,7},{6,4},{7,5},{8,10},{9,11},{10,... | collective-permute-start | bytes 393224 | tf_op jit(solution)/shard_map/ppermute | solution.py:692
  499.8 31.9 %collective-permute-start.59 = (f32[2,64,256]{2,1,0:T(8,128)S(1)}, f32[2,64,256]{2,1,0:T(8,128)S(1)}, u32[]{:S(2)}, u32[]{:S(2)}) collective-permute-start(f32[2,64,256]{2,1,0:T(8,128)S(1)} %add.91), channel_id=1, source_target_pairs={{0,3},{1,2},{2,1},{3,0},{4,7},{5,6},{6,5},{7,4},{8,11},{9,10},{10,... | collective-permute-start | bytes 393224 | tf_op jit(solution)/shard_map/ppermute | solution.py:692
  531.6 34.8 %collective-permute-start.60 = (bf16[512,384]{1,0:T(8,128)(2,1)}, bf16[512,384]{1,0:T(8,128)(2,1)S(1)}, u32[]{:S(2)}, u32[]{:S(2)}) collective-permute-start(bf16[512,384]{1,0:T(8,128)(2,1)} %get-tuple-element.176), channel_id=1, source_target_pairs={{0,1},{1,0},{2,3},{3,2},{4,5},{5,4},{6,7},{7,6},{8,9},{9,8},{10,11... | collective-permute-start | bytes 1179656 | tf_op jit(solution)/shard_map/ppermute | solution.py:692
  532.5 34.0 %collective-permute-start.61 = (bf16[512,384]{1,0:T(8,128)(2,1)}, bf16[512,384]{1,0:T(8,128)(2,1)S(1)}, u32[]{:S(2)}, u32[]{:S(2)}) collective-permute-start(bf16[512,384]{1,0:T(8,128)(2,1)} %get-tuple-element.177), channel_id=1, source_target_pairs={{0,2},{1,3},{2,0},{3,1},{4,6},{5,7},{6,4},{7,5},{8,10},{9,11},{10,... | collective-permute-start | bytes 1179656 | tf_op jit(solution)/shard_map/ppermute | solution.py:692
  534.2 32.3 %collective-permute-start.62 = (bf16[512,384]{1,0:T(8,128)(2,1)}, bf16[512,384]{1,0:T(8,128)(2,1)S(1)}, u32[]{:S(2)}, u32[]{:S(2)}) collective-permute-start(bf16[512,384]{1,0:T(8,128)(2,1)} %get-tuple-element.178), channel_id=1, source_target_pairs={{0,3},{1,2},{2,1},{3,0},{4,7},{5,6},{6,5},{7,4},{8,11},{9,10},{10,... | collective-permute-start | bytes 1179656 | tf_op jit(solution)/shard_map/ppermute | solution.py:692
  (98 other events, 1457.6 us)
Sparse Core Ops, SparseCore 0:
  15.3 49.8 all-gather.24
  66.8 23.7 all-gather.10
  92.8 46.6 all-gather.22
  141.0 27.8 all-gather.12
  170.3 24.5 all-gather.14
  196.4 28.6 all-gather.16
  226.7 64.2 all-gather.18
  364.5 64.0 all-gather.20

commit v6 on v5

--- a/solution.py
+++ b/solution.py
@@ -419,8 +419,11 @@
     slope_ref, normal_two, inverse_two, held, total, in_held, back_held, slope_held = refs[:8]
     in_sems, back_sems, slope_sems = refs[8:]
     hidden = in_held.shape[2]
-    in_copies = copy_in(in_refs, [in_held.at[t] for t in range(parts)], in_sems)
-    back_copies = copy_in(back_refs, [back_held.at[t] for t in range(parts)], back_sems)
+    in_copies, back_copies = [], []
+    for t in range(parts):
+        one = slice(t, t + 1)
+        in_copies += copy_in(in_refs[one], [in_held.at[t]], in_sems.at[one])
+        back_copies += copy_in(back_refs[one], [back_held.at[t]], back_sems.at[one])
     normed = normal_ref[...] * gain_one[...] + shift_one[...]
     held[...] = normed.astype(jnp.bfloat16)
     total[...] = normed + bias_back[...]
@@ -571,13 +574,13 @@
     hidden = in_held.shape[2]
     if count > 0:
         collected = collect_copies(behind[:count], behind[count], behind[count + 1], refs[11:])
-    back_copies = copy_in(back_refs, [back_held.at[t] for t in range(parts)], back_sems)
-    slope_copies = copy_in(
-        [slope_ref.at[:, t * hidden : (t + 1) * hidden] for t in range(parts)],
-        [slope_held.at[t] for t in range(parts)],
-        slope_sems,
-    )
-    in_copies = copy_in(in_refs, [in_held.at[t] for t in range(parts)], in_sems)
+    back_copies, slope_copies, in_copies = [], [], []
+    for t in range(parts):
+        one = slice(t, t + 1)
+        slope_part = slope_ref.at[:, t * hidden : (t + 1) * hidden]
+        back_copies += copy_in(back_refs[one], [back_held.at[t]], back_sems.at[one])
+        slope_copies += copy_in([slope_part], [slope_held.at[t]], slope_sems.at[one])
+        in_copies += copy_in(in_refs[one], [in_held.at[t]], in_sems.at[one])
     late_copies = copy_in([normal_one, matrix_ref], [normal_held, matrix_held], late_sems)
     if count > 0:
         gradient = collect_held(collected, refs[11:])

time: 613 us -> 613 us (level)
  no operation moved by 1% of the time
where the time goes in v6:
time: 613 us; the launch traced here: 607 us
  Pallas kernels  308 us (50%)
  waiting for transfers between devices  154 us (25%)
  starting transfers between devices  74 us (12%)
  local copies, waits for them, and re-layouts  48.7 us (8%)
  between operations  15.6 us (3%)
  other arithmetic  7.28 us (1%)
    pallas_call x13, Pallas kernels, scalar_call(): pl.pallas_call(kernel, grid_spec=pltpu.PrefetchScalarGridSpec(num_scalar_...  308 us
    ppermute x54, waiting for transfers between devices, swap(): return lax.ppermute(value, 'seq', [(i, i ^ step) for i in range(seq_count)])  123 us
    ppermute x54, starting transfers between devices, swap(): return lax.ppermute(value, 'seq', [(i, i ^ step) for i in range(seq_count)])  65.1 us
    ppermute x6, waiting for transfers between devices, over_dp_swap(): return lax.ppermute(value, 'dp', [(i, i ^ bit) for i in range(dp_count)])  16.9 us
    all_gather x6, waiting for transfers between devices, gather(): return lax.all_gather(value, 'dp', axis=0, tiled=True)  13.2 us
  transfers between devices with their start and end apart: 80, of which 24 were waited for; matrix products, arithmetic and copies ran while one was open for 7% of the time, Pallas kernels for 51%

profile of v6, /device:TPU:0, one launch (start us, length us, event | category | flops | bytes accessed | tf_op | source)
XLA Modules:
  0.0 607.4 jit_solution(17219276205856750140)
XLA Ops:
  16.3 2.9 collective-permute-start
  21.3 11.0 %collective-permute-done.refs_2_ = bf16[256,1024]{1,0:T(8,128)(2,1)} collective-permute-done((bf16[256,1024]{1,0:T(8,128)(2,1)}, bf16[256,1024]{1,0:T(8,128)(2,1)}, u32[]{:S(2)}, u32[]{:S(2)}) %collective-permute-start) | collective-permute-done | bytes 524320 | tf_op jit(solution)/shard_map/ppermute | solution.py:695
  38.2 7.5 %collective-permute-done.1.refs_4_ = bf16[256,1024]{1,0:T(8,128)(2,1)} collective-permute-done((bf16[256,1024]{1,0:T(8,128)(2,1)}, bf16[256,1024]{1,0:T(8,128)(2,1)}, u32[]{:S(2)}, u32[]{:S(2)}) %collective-permute-start.1) | collective-permute-done | bytes 524320 | tf_op jit(solution)/shard_map/ppermute | solution.py:695
  45.6 9.8 %collective-permute-done.2.refs_6_ = bf16[256,1024]{1,0:T(8,128)(2,1)} collective-permute-done((bf16[256,1024]{1,0:T(8,128)(2,1)}, bf16[256,1024]{1,0:T(8,128)(2,1)}, u32[]{:S(2)}, u32[]{:S(2)}) %collective-permute-start.2) | collective-permute-done | bytes 524320 | tf_op jit(solution)/shard_map/ppermute | solution.py:695
  77.5 13.2 %all-gather.11.cloned.1.call-done.refs_8_ = bf16[1024,768]{1,0:T(8,128)(2,1)} async-done(((bf16[128,768]{1,0:T(8,128)(2,1)}), bf16[1024,768]{1,0:T(8,128)(2,1)}) %all-gather.11.cloned.1.call-update) | async-done | bytes 1572880 | tf_op jit(solution)/shard_map/all_gather | solution.py:712
  92.0 39.7 %attend.2 = (bf16[512,256]{1,0:T(8,128)(2,1)}, bf16[512,256]{1,0:T(8,128)(2,1)}, bf16[512,256]{1,0:T(8,128)(2,1)}, bf16[512,256]{1,0:T(8,128)(2,1)}, f32[256,204...) custom-call(s32[8]{0:T(128)} %get-tuple-element.245.low_ref, ...), custom_call_target="tpu_custom_call" | custom-call | flops 44000002048 | tf_op jit(solution)/shard_map/attend/pallas_call | solution.py:63
  136.5 4.7 collective-permute-done.30.refs_1_
  145.9 24.7 %collective-permute-done.31.refs_2_ = bf16[512,256]{1,0:T(8,128)(2,1)S(1)} collective-permute-done((bf16[512,256]{1,0:T(8,128)(2,1)}, bf16[512,256]{1,0:T(8,128)(2,1)S(1)}, u32[]{:S(2)}, u32[]{:S(2)}) %collective-permute-start.31) | collective-permute-done | bytes 262176 | tf_op jit(solution)/shard_map/ppermute | solution.py:695
  177.3 5.5 mix.2
  185.8 22.5 %feed.2 = (bf16[256,1024]{1,0:T(8,128)(2,1)}, bf16[256,1024]{1,0:T(8,128)(2,1)}, bf16[512,4096]{1,0:T(8,128)(2,1)}, f32[512,1024]{1,0:T(8,128)}, f32[512,1]{1,0:T(8,128)}) custom-call(s32[1]{0:T(128)} %bitcast.me_ref, s32[1]{0:T(128)} %bitcast.1.core_ref, bf16[1024,512]{1,0:T(8,128)(2,1)} %copy-done.1, bf16[1024,512]{1,0:T(8,128)(2,1)} %get-tuple-element.196.refs_1_, ...), custom_call_target="tpu_custom_call" | custom-call | flops 24199999488 | tf_op jit(solution)/shard_map/feed/pallas_call | solution.py:63
  220.4 11.0 %collective-permute-done.33.refs_2_ = bf16[256,1024]{1,0:T(8,128)(2,1)S(1)} collective-permute-done((bf16[256,1024]{1,0:T(8,128)(2,1)}, bf16[256,1024]{1,0:T(8,128)(2,1)S(1)}, u32[]{:S(2)}, u32[]{:S(2)}) %collective-permute-start.33) | collective-permute-done | bytes 524320 | tf_op jit(solution)/shard_map/ppermute | solution.py:695
  236.9 5.7 collective-permute-done.34.refs_3_
  243.7 11.2 %collective-permute-done.37.refs_6_ = bf16[256,1024]{1,0:T(8,128)(2,1)S(1)} collective-permute-done((bf16[256,1024]{1,0:T(8,128)(2,1)S(1)}, bf16[256,1024]{1,0:T(8,128)(2,1)S(1)}, u32[]{:S(2)}, u32[]{:S(2)}) %collective-permute-start.37) | collective-permute-done | bytes 524320 | tf_op jit(solution)/shard_map/ppermute | solution.py:695
  258.3 39.7 %attend.3 = (bf16[512,256]{1,0:T(8,128)(2,1)}, bf16[512,256]{1,0:T(8,128)(2,1)}, bf16[512,256]{1,0:T(8,128)(2,1)}, bf16[512,256]{1,0:T(8,128)(2,1)}, f32[256,204...) custom-call(s32[8]{0:T(128)} %get-tuple-element.245.low_ref, ...), custom_call_target="tpu_custom_call" | custom-call | flops 44000002048 | tf_op jit(solution)/shard_map/attend/pallas_call | solution.py:63
  302.4 5.4 collective-permute-done.39.refs_1_
  313.5 5.3 mix.3
  319.8 22.7 %feed.3 = (bf16[512,1024]{1,0:T(8,128)(2,1)}, bf16[512,4096]{1,0:T(8,128)(2,1)}, f32[512,1024]{1,0:T(8,128)}, f32[512,1]{1,0:T(8,128)}) custom-call(s32[1]{0:T(128)} %bitcast.me_ref, s32[1]{0:T(128)} %bitcast.1.core_ref, bf16[1024,512]{1,0:T(8,128)(2,1)} %copy-done.2, bf16[1024,512]{1,0:T(8,128)(2,1)} %get-tuple-element.204.refs_1_, ...), custom_call_target="tpu_custom_call" | custom-call | flops 24199999488 | tf_op jit(solution)/shard_map/feed/pallas_call | solution.py:63
  342.5 17.3 %feed_back.2 = (f32[512,1024]{1,0:T(8,128)}, bf16[512,256]{1,0:T(8,128)(2,1)}, bf16[512,256]{1,0:T(8,128)(2,1)}, bf16[512,256]{1,0:T(8,128)(2,1)}, bf16[512,256]{1,0:T(8,128)(2,1)}) custom-call(s32[1]{0:T(128)} %bitcast.me_ref, bf16[1024,512]{1,0:T(8,128)(2,1)} %copy-done.2, bf16[1024,512]{1,0:T(8,128)(2,1)} %get-tuple-element.204.refs_1_, ...), custom_call_target="tpu_custom_call" | custom-call | flops 19800000512 | tf_op jit(solution)/shard_map/feed_back/pallas_call | solution.py:63
  364.3 4.8 collective-permute-done.42.refs_1_
  369.2 5.8 collective-permute-done.43.refs_2_
  375.8 30.0 %attend_back.4 = (bf16[512,384]{1,0:T(8,128)(2,1)}, bf16[512,384]{1,0:T(8,128)(2,1)}, bf16[512,384]{1,0:T(8,128)(2,1)}, bf16[512,384]{1,0:T(8,128)(2,1)}, f32[2,64,128]{2,1,0:T(8,128)}) custom-call(s32[8]{0:T(128)} %get-tuple-element.245.low_ref, s32[8]{0:T(128)} %get-tuple-element.244.high_ref, s32[1]{0:T(128)} %bitcast.me_ref, ...), custom_call_target="tpu_custom_call" | custom-call | flops 32999999488 | tf_op jit(solution)/shard_map/attend_back/pallas_call | solution.py:63
  409.2 30.3 %attend_back.5 = (bf16[512,384]{1,0:T(8,128)(2,1)}, bf16[512,384]{1,0:T(8,128)(2,1)}, bf16[512,384]{1,0:T(8,128)(2,1)}, bf16[512,384]{1,0:T(8,128)(2,1)}, f32[2,64,128]{2,1,0:T(8,128)}) custom-call(s32[8]{0:T(128)} %get-tuple-element.245.low_ref, s32[8]{0:T(128)} %get-tuple-element.244.high_ref, s32[1]{0:T(128)} %bitcast.me_ref, ...), custom_call_target="tpu_custom_call" | custom-call | flops 32999999488 | tf_op jit(solution)/shard_map/attend_back/pallas_call | solution.py:63
  446.9 5.0 collective-permute-done.48.refs_22_
  451.9 4.9 collective-permute-done.49.refs_24_
  459.2 27.0 %feed_back.3 = (f32[512,1024]{1,0:T(8,128)}, bf16[512,256]{1,0:T(8,128)(2,1)}, bf16[512,256]{1,0:T(8,128)(2,1)}, bf16[512,256]{1,0:T(8,128)(2,1)}, bf16[512,256]{1,0:T(8,128)(2,1)}) custom-call(s32[1]{0:T(128)} %bitcast.me_ref, bf16[1024,512]{1,0:T(8,128)(2,1)} %copy-done.1, bf16[1024,512]{1,0:T(8,128)(2,1)} %get-tuple-element.196.refs_1_, ...), custom_call_target="tpu_custom_call" | custom-call | flops 19800000512 | tf_op jit(solution)/shard_map/feed_back/pallas_call | solution.py:63
  491.7 5.5 collective-permute-done.56
  501.6 30.0 %attend_back.6 = (bf16[512,384]{1,0:T(8,128)(2,1)}, bf16[512,384]{1,0:T(8,128)(2,1)}, bf16[512,384]{1,0:T(8,128)(2,1)}, bf16[512,384]{1,0:T(8,128)(2,1)}, f32[2,64,128]{2,1,0:T(8,128)}) custom-call(s32[8]{0:T(128)} %get-tuple-element.245.low_ref, s32[8]{0:T(128)} %get-tuple-element.244.high_ref, s32[1]{0:T(128)} %bitcast.me_ref, ...), custom_call_target="tpu_custom_call" | custom-call | flops 32999999488 | tf_op jit(solution)/shard_map/attend_back/pallas_call | solution.py:63
  535.1 30.4 %attend_back.7 = (bf16[512,384]{1,0:T(8,128)(2,1)}, bf16[512,384]{1,0:T(8,128)(2,1)}, bf16[512,384]{1,0:T(8,128)(2,1)}, bf16[512,384]{1,0:T(8,128)(2,1)}, f32[2,64,128]{2,1,0:T(8,128)}) custom-call(s32[8]{0:T(128)} %get-tuple-element.245.low_ref, s32[8]{0:T(128)} %get-tuple-element.244.high_ref, s32[1]{0:T(128)} %bitcast.me_ref, ...), custom_call_target="tpu_custom_call" | custom-call | flops 32999999488 | tf_op jit(solution)/shard_map/attend_back/pallas_call | solution.py:63
  571.2 4.0 collective-permute-done.67
  576.9 6.2 %collective-permute-done.68 = f32[2,64,256]{2,1,0:T(8,128)S(1)} collective-permute-done((f32[2,64,256]{2,1,0:T(8,128)S(1)}, f32[2,64,256]{2,1,0:T(8,128)S(1)}, u32[]{:S(2)}, u32[]{:S(2)}) %collective-permute-start.68) | collective-permute-done | bytes 131104 | tf_op jit(solution)/shard_map/ppermute | solution.py:791
  583.1 4.0 collective-permute-done.64.refs_5_
  590.7 7.9 %collect.1 = bf16[512,1024]{1,0:T(8,128)(2,1)} custom-call(bf16[512,384]{1,0:T(8,128)(2,1)} %get-tuple-element.171.refs_0_, bf16[512,384]{1,0:T(8,128)(2,1)} %get-tuple-element.179.refs_1_, bf16[512,384]{1,0:T(8,128)(2,1)} %copy-done.26, bf16[512,384]{1,0:T(8,128)(2,1)} %copy-done.34, bf16[512,384]{1,0:T(8,128)(2,1)} %copy-done.27, ...), custom_call_target="tpu_custom_call" | custom-call | flops 9900000256 | tf_op jit(solution)/shard_map/collect/pallas_call | solution.py:63
  (335 shorter events, 136.3 us)
Async XLA Ops:
  7.2 60.8 %all-gather.25.cloned.1.call-start = ((), (), s32[]{:S(2)}) async-start(), calls=%async_computation.7 | async-start | bytes 4718592 | tf_op jit(solution)/shard_map/all_gather | solution.py:756
  15.2 75.4 %all-gather.11.cloned.1.call-start = ((), (), s32[]{:S(2)}) async-start(), calls=%async_computation | async-start | bytes 1769472 | tf_op jit(solution)/shard_map/all_gather | solution.py:712
  56.3 115.4 %all-gather.23.cloned.1.call-start = ((), (), s32[]{:S(2)}) async-start(), calls=%async_computation.6 | async-start | bytes 4718592 | tf_op jit(solution)/shard_map/all_gather | solution.py:756
  61.0 116.3 %all-gather.13.cloned.1.call-start = ((), (), s32[]{:S(2)}) async-start(), calls=%async_computation.1 | async-start | bytes 2359296 | tf_op jit(solution)/shard_map/all_gather | solution.py:712
  61.9 196.4 %all-gather.15.cloned.1.call-start = ((), (), s32[]{:S(2)}) async-start(), calls=%async_computation.2 | async-start | bytes 1769472 | tf_op jit(solution)/shard_map/all_gather | solution.py:712
  67.7 245.8 %all-gather.17.cloned.1.call-start = ((), (), s32[]{:S(2)}) async-start(), calls=%async_computation.3 | async-start | bytes 2359296 | tf_op jit(solution)/shard_map/all_gather | solution.py:712
  71.9 59.8 %collective-permute-start.18 = (bf16[1024,512]{1,0:T(8,128)(2,1)S(1)}, bf16[1024,512]{1,0:T(8,128)(2,1)}, u32[]{:S(2)}, u32[]{:S(2)}) collective-permute-start(bf16[1024,512]{1,0:T(8,128)(2,1)S(1)} %get-tuple-element.197.refs_0_), channel_id=1, source_target_pairs={{0,1},{1,0},{2,3},{3,2},{4,5},{5,4},{6,7},{7,6},{8,9},{9,8},{10,11... | collective-permute-start | bytes 3145736 | tf_op jit(solution)/shard_map/ppermute | solution.py:695
  72.2 59.5 %collective-permute-start.20 = (bf16[1024,512]{1,0:T(8,128)(2,1)S(1)}, bf16[1024,512]{1,0:T(8,128)(2,1)}, u32[]{:S(2)}, u32[]{:S(2)}) collective-permute-start(bf16[1024,512]{1,0:T(8,128)(2,1)S(1)} %get-tuple-element.197.refs_0_), channel_id=1, source_target_pairs={{0,2},{1,3},{2,0},{3,1},{4,6},{5,7},{6,4},{7,5},{8,10},{9,11},{10,... | collective-permute-start | bytes 3145736 | tf_op jit(solution)/shard_map/ppermute | solution.py:695
  75.5 56.2 %collective-permute-start.24 = (bf16[512,1024]{1,0:T(8,128)(2,1)}, bf16[512,1024]{1,0:T(8,128)(2,1)}, u32[]{:S(2)}, u32[]{:S(2)}) collective-permute-start(bf16[512,1024]{1,0:T(8,128)(2,1)} %get-tuple-element.195.refs_8_), channel_id=1, source_target_pairs={{0,1},{1,0},{2,3},{3,2},{4,5},{5,4},{6,7},{7,6},{8,9},{9,8},{10,11... | collective-permute-start | bytes 3145736 | tf_op jit(solution)/shard_map/ppermute | solution.py:695
  77.0 54.7 %collective-permute-start.26 = (bf16[512,1024]{1,0:T(8,128)(2,1)}, bf16[512,1024]{1,0:T(8,128)(2,1)}, u32[]{:S(2)}, u32[]{:S(2)}) collective-permute-start(bf16[512,1024]{1,0:T(8,128)(2,1)} %get-tuple-element.195.refs_8_), channel_id=1, source_target_pairs={{0,2},{1,3},{2,0},{3,1},{4,6},{5,7},{6,4},{7,5},{8,10},{9,11},{10,... | collective-permute-start | bytes 3145736 | tf_op jit(solution)/shard_map/ppermute | solution.py:695
  133.3 37.8 %collective-permute-start.19 = (bf16[1024,512]{1,0:T(8,128)(2,1)}, bf16[1024,512]{1,0:T(8,128)(2,1)S(1)}, u32[]{:S(2)}, u32[]{:S(2)}) collective-permute-start(bf16[1024,512]{1,0:T(8,128)(2,1)} %collective-permute-done.18.refs_2_), channel_id=1, source_target_pairs={{0,4},{4,0},{8,12},{12,8},{16,20},{20,16},{24,28},{28,24},{1,5},{5... | collective-permute-start | bytes 3145736 | tf_op jit(solution)/shard_map/ppermute | solution.py:709
  133.3 37.9 %collective-permute-start.22 = (bf16[1024,512]{1,0:T(8,128)(2,1)}, bf16[1024,512]{1,0:T(8,128)(2,1)}, u32[]{:S(2)}, u32[]{:S(2)}) collective-permute-start(bf16[1024,512]{1,0:T(8,128)(2,1)} %collective-permute-done.20.refs_4_), channel_id=1, source_target_pairs={{0,1},{1,0},{2,3},{3,2},{4,5},{5,4},{6,7},{7,6},{8,9},{9,8},{10,11... | collective-permute-start | bytes 3145736 | tf_op jit(solution)/shard_map/ppermute | solution.py:695
  133.8 37.8 %collective-permute-start.28 = (bf16[512,1024]{1,0:T(8,128)(2,1)}, bf16[512,1024]{1,0:T(8,128)(2,1)}, u32[]{:S(2)}, u32[]{:S(2)}) collective-permute-start(bf16[512,1024]{1,0:T(8,128)(2,1)} %collective-permute-done.24.refs_10_), channel_id=1, source_target_pairs={{0,2},{1,3},{2,0},{3,1},{4,6},{5,7},{6,4},{7,5},{8,10},{9,11},{10,... | collective-permute-start | bytes 3145736 | tf_op jit(solution)/shard_map/ppermute | solution.py:695
  135.9 34.6 %collective-permute-start.31 = (bf16[512,256]{1,0:T(8,128)(2,1)}, bf16[512,256]{1,0:T(8,128)(2,1)S(1)}, u32[]{:S(2)}, u32[]{:S(2)}) collective-permute-start(bf16[512,256]{1,0:T(8,128)(2,1)} %get-tuple-element.104), channel_id=1, source_target_pairs={{0,2},{1,3},{2,0},{3,1},{4,6},{5,7},{6,4},{7,5},{8,10},{9,11},{10,... | collective-permute-start | bytes 786440 | tf_op jit(solution)/shard_map/ppermute | solution.py:695
  141.1 29.4 %collective-permute-start.32 = (bf16[512,256]{1,0:T(8,128)(2,1)}, bf16[512,256]{1,0:T(8,128)(2,1)S(1)}, u32[]{:S(2)}, u32[]{:S(2)}) collective-permute-start(bf16[512,256]{1,0:T(8,128)(2,1)} %get-tuple-element.105), channel_id=1, source_target_pairs={{0,3},{1,2},{2,1},{3,0},{4,7},{5,6},{6,5},{7,4},{8,11},{9,10},{10,... | collective-permute-start | bytes 786440 | tf_op jit(solution)/shard_map/ppermute | solution.py:695
  145.4 313.1 %all-gather.19.cloned.1.call-start = ((), (), s32[]{:S(2)}) async-start(), calls=%async_computation.4 | async-start | bytes 7077888 | tf_op jit(solution)/shard_map/all_gather | solution.py:712
  216.3 374.4 %all-gather.21.cloned.1.call-start = ((), (), s32[]{:S(2)}) async-start(), calls=%async_computation.5 | async-start | bytes 7077888 | tf_op jit(solution)/shard_map/all_gather | solution.py:712
  235.9 62.0 %collective-permute-start.8 = (bf16[1024,512]{1,0:T(8,128)(2,1)S(1)}, bf16[1024,512]{1,0:T(8,128)(2,1)}, u32[]{:S(2)}, u32[]{:S(2)}) collective-permute-start(bf16[1024,512]{1,0:T(8,128)(2,1)S(1)} %get-tuple-element.205.refs_0_), channel_id=1, source_target_pairs={{0,2},{1,3},{2,0},{3,1},{4,6},{5,7},{6,4},{7,5},{8,10},{9,11},{10,... | collective-permute-start | bytes 3145736 | tf_op jit(solution)/shard_map/ppermute | solution.py:695
  242.7 55.3 %collective-permute-start.12 = (bf16[512,1024]{1,0:T(8,128)(2,1)S(1)}, bf16[512,1024]{1,0:T(8,128)(2,1)}, u32[]{:S(2)}, u32[]{:S(2)}) collective-permute-start(bf16[512,1024]{1,0:T(8,128)(2,1)S(1)} %copy-done.4), channel_id=1, source_target_pairs={{0,1},{1,0},{2,3},{3,2},{4,5},{5,4},{6,7},{7,6},{8,9},{9,8},{10,11... | collective-permute-start | bytes 3145736 | tf_op jit(solution)/shard_map/ppermute | solution.py:695
  243.7 58.2 %collective-permute-start.7 = (bf16[1024,512]{1,0:T(8,128)(2,1)}, bf16[1024,512]{1,0:T(8,128)(2,1)}, u32[]{:S(2)}, u32[]{:S(2)}) collective-permute-start(bf16[1024,512]{1,0:T(8,128)(2,1)} %copy-done.18), channel_id=1, source_target_pairs={{0,4},{4,0},{8,12},{12,8},{16,20},{20,16},{24,28},{28,24},{1,5},{5... | collective-permute-start | bytes 3145736 | tf_op jit(solution)/shard_map/ppermute | solution.py:709
  255.0 43.5 %collective-permute-start.10 = (bf16[1024,512]{1,0:T(8,128)(2,1)}, bf16[1024,512]{1,0:T(8,128)(2,1)}, u32[]{:S(2)}, u32[]{:S(2)}) collective-permute-start(bf16[1024,512]{1,0:T(8,128)(2,1)} %copy-done.18), channel_id=1, source_target_pairs={{0,2},{1,3},{2,0},{3,1},{4,6},{5,7},{6,4},{7,5},{8,10},{9,11},{10,... | collective-permute-start | bytes 3145736 | tf_op jit(solution)/shard_map/ppermute | solution.py:695
  257.3 41.2 %collective-permute-start.16 = (bf16[512,1024]{1,0:T(8,128)(2,1)}, bf16[512,1024]{1,0:T(8,128)(2,1)}, u32[]{:S(2)}, u32[]{:S(2)}) collective-permute-start(bf16[512,1024]{1,0:T(8,128)(2,1)} %collective-permute-done.14.refs_12_), channel_id=1, source_target_pairs={{0,1},{1,0},{2,3},{3,2},{4,5},{5,4},{6,7},{7,6},{8,9},{9,8},{10,11... | collective-permute-start | bytes 3145736 | tf_op jit(solution)/shard_map/ppermute | solution.py:695
  405.7 33.8 %collective-permute-start.45 = (bf16[512,384]{1,0:T(8,128)(2,1)}, bf16[512,384]{1,0:T(8,128)(2,1)S(1)}, u32[]{:S(2)}, u32[]{:S(2)}) collective-permute-start(bf16[512,384]{1,0:T(8,128)(2,1)} %get-tuple-element.143), channel_id=1, source_target_pairs={{0,1},{1,0},{2,3},{3,2},{4,5},{5,4},{6,7},{7,6},{8,9},{9,8},{10,11... | collective-permute-start | bytes 1179656 | tf_op jit(solution)/shard_map/ppermute | solution.py:695
  406.9 32.7 %collective-permute-start.46 = (bf16[512,384]{1,0:T(8,128)(2,1)}, bf16[512,384]{1,0:T(8,128)(2,1)S(1)}, u32[]{:S(2)}, u32[]{:S(2)}) collective-permute-start(bf16[512,384]{1,0:T(8,128)(2,1)} %get-tuple-element.144), channel_id=1, source_target_pairs={{0,2},{1,3},{2,0},{3,1},{4,6},{5,7},{6,4},{7,5},{8,10},{9,11},{10,... | collective-permute-start | bytes 1179656 | tf_op jit(solution)/shard_map/ppermute | solution.py:695
  407.8 31.7 %collective-permute-start.47 = (bf16[512,384]{1,0:T(8,128)(2,1)}, bf16[512,384]{1,0:T(8,128)(2,1)S(1)}, u32[]{:S(2)}, u32[]{:S(2)}) collective-permute-start(bf16[512,384]{1,0:T(8,128)(2,1)} %get-tuple-element.145), channel_id=1, source_target_pairs={{0,3},{1,2},{2,1},{3,0},{4,7},{5,6},{6,5},{7,4},{8,11},{9,10},{10,... | collective-permute-start | bytes 1179656 | tf_op jit(solution)/shard_map/ppermute | solution.py:695
  445.3 44.5 %collective-permute-start.55 = (f32[2,64,256]{2,1,0:T(8,128)S(1)}, f32[2,64,256]{2,1,0:T(8,128)S(1)}, u32[]{:S(2)}, u32[]{:S(2)}) collective-permute-start(f32[2,64,256]{2,1,0:T(8,128)S(1)} %add.89), channel_id=1, source_target_pairs={{0,8},{4,12},{8,0},{12,4},{16,24},{20,28},{24,16},{28,20},{1,9},{5... | collective-permute-start | bytes 393224 | tf_op jit(solution)/shard_map/ppermute | solution.py:791
  497.2 34.3 %collective-permute-start.57 = (f32[2,64,256]{2,1,0:T(8,128)S(1)}, f32[2,64,256]{2,1,0:T(8,128)S(1)}, u32[]{:S(2)}, u32[]{:S(2)}) collective-permute-start(f32[2,64,256]{2,1,0:T(8,128)S(1)} %add.91), channel_id=1, source_target_pairs={{0,1},{1,0},{2,3},{3,2},{4,5},{5,4},{6,7},{7,6},{8,9},{9,8},{10,11... | collective-permute-start | bytes 393224 | tf_op jit(solution)/shard_map/ppermute | solution.py:695
  498.0 33.6 %collective-permute-start.58 = (f32[2,64,256]{2,1,0:T(8,128)S(1)}, f32[2,64,256]{2,1,0:T(8,128)S(1)}, u32[]{:S(2)}, u32[]{:S(2)}) collective-permute-start(f32[2,64,256]{2,1,0:T(8,128)S(1)} %add.91), channel_id=1, source_target_pairs={{0,2},{1,3},{2,0},{3,1},{4,6},{5,7},{6,4},{7,5},{8,10},{9,11},{10,... | collective-permute-start | bytes 393224 | tf_op jit(solution)/shard_map/ppermute | solution.py:695
  499.7 31.8 %collective-permute-start.59 = (f32[2,64,256]{2,1,0:T(8,128)S(1)}, f32[2,64,256]{2,1,0:T(8,128)S(1)}, u32[]{:S(2)}, u32[]{:S(2)}) collective-permute-start(f32[2,64,256]{2,1,0:T(8,128)S(1)} %add.91), channel_id=1, source_target_pairs={{0,3},{1,2},{2,1},{3,0},{4,7},{5,6},{6,5},{7,4},{8,11},{9,10},{10,... | collective-permute-start | bytes 393224 | tf_op jit(solution)/shard_map/ppermute | solution.py:695
  531.6 34.8 %collective-permute-start.60 = (bf16[512,384]{1,0:T(8,128)(2,1)}, bf16[512,384]{1,0:T(8,128)(2,1)S(1)}, u32[]{:S(2)}, u32[]{:S(2)}) collective-permute-start(bf16[512,384]{1,0:T(8,128)(2,1)} %get-tuple-element.176), channel_id=1, source_target_pairs={{0,1},{1,0},{2,3},{3,2},{4,5},{5,4},{6,7},{7,6},{8,9},{9,8},{10,11... | collective-permute-start | bytes 1179656 | tf_op jit(solution)/shard_map/ppermute | solution.py:695
  532.4 34.0 %collective-permute-start.61 = (bf16[512,384]{1,0:T(8,128)(2,1)}, bf16[512,384]{1,0:T(8,128)(2,1)S(1)}, u32[]{:S(2)}, u32[]{:S(2)}) collective-permute-start(bf16[512,384]{1,0:T(8,128)(2,1)} %get-tuple-element.177), channel_id=1, source_target_pairs={{0,2},{1,3},{2,0},{3,1},{4,6},{5,7},{6,4},{7,5},{8,10},{9,11},{10,... | collective-permute-start | bytes 1179656 | tf_op jit(solution)/shard_map/ppermute | solution.py:695
  534.1 32.3 %collective-permute-start.62 = (bf16[512,384]{1,0:T(8,128)(2,1)}, bf16[512,384]{1,0:T(8,128)(2,1)S(1)}, u32[]{:S(2)}, u32[]{:S(2)}) collective-permute-start(bf16[512,384]{1,0:T(8,128)(2,1)} %get-tuple-element.178), channel_id=1, source_target_pairs={{0,3},{1,2},{2,1},{3,0},{4,7},{5,6},{6,5},{7,4},{8,11},{9,10},{10,... | collective-permute-start | bytes 1179656 | tf_op jit(solution)/shard_map/ppermute | solution.py:695
  (98 other events, 1457.2 us)
Sparse Core Ops, SparseCore 0:
  15.3 49.8 all-gather.24
  66.8 23.7 all-gather.10
  92.8 46.6 all-gather.22
  141.0 27.8 all-gather.12
  170.3 24.5 all-gather.14
  196.4 28.6 all-gather.16
  226.7 64.2 all-gather.18
  364.5 64.0 all-gather.20
